TPU v7x, 32 devices: a whole 2x2x4 slice. The times are simulated.
32 devices in a mesh: dp: 4 (over y, x), tensor: 8 (over z, core).
Axes of the slice: x: 2, y: 2, z: 4, core: 2. Of those that a mesh axis runs over, the one named last changes fastest.
Arguments:
- tokens: bfloat16 [8192, 2048], P(('dp', 'tensor')), may hold values from -6 to 6
- cotangent: bfloat16 [8192, 2048], P(('dp', 'tensor')), may hold values from -6 to 6
- resets: int32 [8], P('dp'), may hold values 0 or 1
- init_state: float32 [8, 2752], P('dp', 'tensor'), may hold values from -4 to 4
- init_conv: float32 [8, 3, 2752], P('dp', None, 'tensor'), may hold values from -6 to 6
- norm_gain: bfloat16 [2048], replicated, may hold values from 0.5 to 1.5
- w_input: bfloat16 [2048, 2752], P(None, 'tensor'), may hold values from -0.125 to 0.125
- w_branch: bfloat16 [2048, 2752], P(None, 'tensor'), may hold values from -0.125 to 0.125
- conv_params: float32 [5, 2752], P(None, 'tensor'), may hold values from -3 to 3
- gate_weights: bfloat16 [2, 16, 172, 172], P(None, 'tensor'), may hold values from -0.4375 to 0.4375
- gate_bias: float32 [2, 2752], P(None, 'tensor'), may hold values from -4 to 4
- decay_rate: float32 [2752], P('tensor'), may hold values from 0.0002 to 0.3
- w_output: bfloat16 [2752, 2048], P('tensor'), may hold values from -0.4375 to 0.4375
- mlp_gain: bfloat16 [2048], replicated, may hold values from 0.5 to 1.5
- w_gelu: bfloat16 [2048, 6144], P(None, 'tensor'), may hold values from -0.125 to 0.125
- w_linear: bfloat16 [2048, 6144], P(None, 'tensor'), may hold values from -0.125 to 0.125
- w_down: bfloat16 [6144, 2048], P('tensor'), may hold values from -0.15625 to 0.15625
Outputs:
- output: bfloat16 [8192, 2048], P(('dp', 'tensor'))
- input_grad: float32 [8192, 2048], P(('dp', 'tensor'))
- final_state: float32 [8, 2752], P('dp', 'tensor')
- final_conv: float32 [8, 3, 2752], P('dp', None, 'tensor')
- grad_norm_gain: float32 [2048], P('tensor')
- grad_w_input: float32 [2048, 2752], P(None, 'tensor')
- grad_w_branch: float32 [2048, 2752], P(None, 'tensor')
- grad_conv_params: float32 [5, 2752], P(None, 'tensor')
- grad_gate_weights: float32 [2, 16, 172, 172], P(None, 'tensor')
- grad_gate_bias: float32 [2, 2752], P(None, 'tensor')
- grad_decay_rate: float32 [2752], P('tensor')
- grad_w_output: float32 [2752, 2048], P('tensor')
- grad_mlp_gain: float32 [2048], P('tensor')
- grad_w_gelu: float32 [2048, 6144], P(None, 'tensor')
- grad_w_linear: float32 [2048, 6144], P(None, 'tensor')
- grad_w_down: float32 [6144, 2048], P('tensor')
All inputs are finite; a program needn't handle non-finite values. No bound on the sum of `resets` on one device may be relied on, other than what follows from the above.
Results may differ from a plain program's by a relative error of at most 0.029.
Values may be sent and summed in bfloat16 or wider, within the bound.
A program may use at most 256 MiB of HBM per device.

v0:
```python
import jax
import jax.numpy as jnp
from jax import lax
from jax.sharding import PartitionSpec as P

EPSILON = 1e-06


def normalize(values, gain_row):
    inv_rms = lax.rsqrt(jnp.mean(values * values, axis=-1, keepdims=True) + EPSILON)
    return (values * inv_rms * gain_row, inv_rms)


def norm_backward(values, gain_row, inv_rms, gradient):
    unit_rows = values * inv_rms
    scaled_grad = gradient * gain_row
    centred = jnp.mean(scaled_grad * unit_rows, axis=-1, keepdims=True)
    return (inv_rms * (scaled_grad - unit_rows * centred), jnp.sum(gradient * unit_rows, axis=0))


def convolve(recur_in, conv_params, start_conv):
    length = recur_in.shape[1]
    history = jnp.concatenate([start_conv, recur_in], axis=1)
    result = (
        conv_params[4]
        + conv_params[0] * history[:, 3:]
        + conv_params[1] * history[:, 2 : length + 2]
    )
    return (
        result + conv_params[2] * history[:, 1 : length + 1] + conv_params[3] * history[:, :length]
    )


def gate_inputs(pre_gates, convolved, decay_rate):
    recall = jax.nn.sigmoid(pre_gates[0])
    ingate = jax.nn.sigmoid(pre_gates[1])
    log_decay = -8.0 * recall * decay_rate
    return (jnp.exp(log_decay), jnp.sqrt(-jnp.expm1(2.0 * log_decay)) * ingate * convolved)


def combine(earlier, latter):
    return (earlier[0] * latter[0], latter[0] * earlier[1] + latter[1])


def gelu_tanh(values):
    return jax.nn.gelu(values, approximate=True)


def body(
    tokens,
    cotangent,
    resets,
    init_state,
    init_conv,
    norm_gain,
    w_input,
    w_branch,
    conv_params,
    gate_weights,
    gate_bias,
    decay_rate,
    w_output,
    mlp_gain,
    w_gelu,
    w_linear,
    w_down,
):
    shards = lax.axis_size("tensor")
    local_rows = tokens.shape[0]
    sequences = resets.shape[0]
    group_rows = local_rows * shards
    length = group_rows // sequences
    channels = w_input.shape[1]
    hidden_cols = w_gelu.shape[1]
    local_blocks = gate_weights.shape[1]
    block_width = gate_weights.shape[2]
    survive = (1 - resets).astype(jnp.float32)
    start_state = init_state * survive[:, None]
    start_conv = init_conv * survive[:, None, None]
    inputs_f = tokens.astype(jnp.float32)
    gain_first = norm_gain.astype(jnp.float32)
    normed, inv_first = normalize(inputs_f, gain_first)
    normed_low = normed.astype(jnp.bfloat16)
    w_pair = jnp.concatenate([w_input, w_branch], axis=1)
    projected = jnp.dot(
        lax.all_gather(normed_low, "tensor", axis=0, tiled=True),
        w_pair,
        preferred_element_type=jnp.float32,
    )
    recur_in = projected[:, :channels].reshape(sequences, length, channels)
    branch = projected[:, channels:]
    gating, gelu_branch = jax.vjp(gelu_tanh, branch)
    convolved, conv_pull = jax.vjp(
        lambda values, params: convolve(values, params, start_conv), recur_in, conv_params
    )
    conv_low = convolved.astype(jnp.bfloat16)
    conv_grouped = conv_low.reshape(group_rows, local_blocks, block_width)
    pre_gates = jnp.einsum(
        "nkb,gkbc->gnkc", conv_grouped, gate_weights, preferred_element_type=jnp.float32
    )
    pre_gates = pre_gates.reshape(2, sequences, length, channels) + gate_bias[:, None, None, :]
    (decay_step, driving), gate_pull = jax.vjp(
        gate_inputs, pre_gates, conv_low.astype(jnp.float32), decay_rate
    )
    seeded = jnp.concatenate(
        [driving[:, :1] + decay_step[:, :1] * start_state[:, None], driving[:, 1:]], axis=1
    )
    scanned = lax.associative_scan(combine, (decay_step, seeded), axis=1)
    states = scanned[1]
    final_state = states[:, -1]
    final_conv = recur_in[:, -3:]
    states_flat = states.reshape(group_rows, channels)
    mixture = (states_flat * gating).astype(jnp.bfloat16)
    branch_out = lax.psum_scatter(
        jnp.dot(mixture, w_output, preferred_element_type=jnp.float32).astype(jnp.bfloat16),
        "tensor",
        scatter_dimension=0,
        tiled=True,
    ).astype(jnp.float32)
    residual = inputs_f + branch_out
    gain_second = mlp_gain.astype(jnp.float32)
    normed_mlp, inv_second = normalize(residual, gain_second)
    normed_mlp_low = normed_mlp.astype(jnp.bfloat16)
    w_ups = jnp.concatenate([w_gelu, w_linear], axis=1)
    ups = jnp.dot(
        lax.all_gather(normed_mlp_low, "tensor", axis=0, tiled=True),
        w_ups,
        preferred_element_type=jnp.float32,
    )
    first_up = ups[:, :hidden_cols]
    second_up = ups[:, hidden_cols:]
    activated, gelu_first = jax.vjp(gelu_tanh, first_up)
    hidden = (activated * second_up).astype(jnp.bfloat16)
    down_out = lax.psum_scatter(
        jnp.dot(hidden, w_down, preferred_element_type=jnp.float32).astype(jnp.bfloat16),
        "tensor",
        scatter_dimension=0,
        tiled=True,
    ).astype(jnp.float32)
    output = (residual + down_out).astype(jnp.bfloat16)
    grad_full = lax.all_gather(cotangent, "tensor", axis=0, tiled=True)
    g_hidden = jnp.einsum("nd,fd->nf", grad_full, w_down, preferred_element_type=jnp.float32)
    grad_down = jnp.einsum("nf,nd->fd", hidden, grad_full, preferred_element_type=jnp.float32)
    g_second = g_hidden * activated
    g_first = gelu_first(g_hidden * second_up)[0]
    g_ups = jnp.concatenate([g_first.astype(jnp.bfloat16), g_second.astype(jnp.bfloat16)], axis=1)
    g_normed_mlp = lax.psum_scatter(
        jnp.einsum("nf,df->nd", g_ups, w_ups, preferred_element_type=jnp.float32).astype(
            jnp.bfloat16
        ),
        "tensor",
        scatter_dimension=0,
        tiled=True,
    ).astype(jnp.float32)
    matching = g_ups
    grad_ups = jnp.einsum(
        "nd,nf->df",
        lax.all_gather(normed_mlp_low, "tensor", axis=0, tiled=True),
        matching,
        preferred_element_type=jnp.float32,
    )
    residual_norm_grad, gain_second_grad = norm_backward(
        residual, gain_second, inv_second, g_normed_mlp
    )
    g_residual = cotangent.astype(jnp.float32) + residual_norm_grad
    g_branch_out = lax.all_gather(g_residual.astype(jnp.bfloat16), "tensor", axis=0, tiled=True)
    g_mixture = jnp.einsum("nd,rd->nr", g_branch_out, w_output, preferred_element_type=jnp.float32)
    grad_output = jnp.einsum("nr,nd->rd", mixture, g_branch_out, preferred_element_type=jnp.float32)
    g_states = (g_mixture * gating).reshape(sequences, length, channels)
    g_branch = gelu_branch(g_mixture * states_flat)[0].astype(jnp.bfloat16)
    decay_next = jnp.concatenate([decay_step[:, 1:], jnp.zeros_like(decay_step[:, :1])], axis=1)
    flipped = lax.associative_scan(
        combine, (jnp.flip(decay_next, 1), jnp.flip(g_states, 1)), axis=1
    )
    carried = jnp.flip(flipped[1], 1)
    previous = jnp.concatenate([start_state[:, None], states[:, :-1]], axis=1)
    g_pre, g_conv_direct, grad_decay = gate_pull((carried * previous, carried))
    g_pre_low = g_pre.astype(jnp.bfloat16)
    g_pre_grouped = g_pre_low.reshape(2, group_rows, local_blocks, block_width)
    grad_gates = jnp.einsum(
        "nkb,gnkc->gkbc", conv_grouped, g_pre_grouped, preferred_element_type=jnp.float32
    )
    grad_gate_bias = jnp.sum(g_pre_low.astype(jnp.float32), axis=(1, 2))
    g_conv_back = jnp.einsum(
        "gnkc,gkbc->nkb", g_pre_grouped, gate_weights, preferred_element_type=jnp.float32
    )
    g_convolved = g_conv_direct + g_conv_back.reshape(sequences, length, channels)
    g_recur, grad_conv = conv_pull(g_convolved)
    g_inputs = jnp.concatenate(
        [g_recur.reshape(group_rows, channels).astype(jnp.bfloat16), g_branch], axis=1
    )
    g_normed = lax.psum_scatter(
        jnp.einsum("nr,dr->nd", g_inputs, w_pair, preferred_element_type=jnp.float32).astype(
            jnp.bfloat16
        ),
        "tensor",
        scatter_dimension=0,
        tiled=True,
    ).astype(jnp.float32)
    matching = g_inputs
    grad_pair = jnp.einsum(
        "nd,nr->dr",
        lax.all_gather(normed_low, "tensor", axis=0, tiled=True),
        matching,
        preferred_element_type=jnp.float32,
    )
    input_norm_grad, gain_first_grad = norm_backward(inputs_f, gain_first, inv_first, g_normed)
    input_grad = g_residual + input_norm_grad
    gain_parts = (
        lax.psum_scatter(gain_first_grad, "tensor", scatter_dimension=0, tiled=True),
        lax.psum_scatter(gain_second_grad, "tensor", scatter_dimension=0, tiled=True),
    )
    summed = (
        lax.psum(grad_pair.astype(jnp.bfloat16), "dp").astype(jnp.float32),
        lax.psum(grad_conv.astype(jnp.bfloat16), "dp").astype(jnp.float32),
        lax.psum(grad_gates.astype(jnp.bfloat16), "dp").astype(jnp.float32),
        lax.psum(grad_gate_bias.astype(jnp.bfloat16), "dp").astype(jnp.float32),
        lax.psum(grad_decay.astype(jnp.bfloat16), "dp").astype(jnp.float32),
        lax.psum(grad_output.astype(jnp.bfloat16), "dp").astype(jnp.float32),
        lax.psum(gain_parts[0].astype(jnp.bfloat16), "dp").astype(jnp.float32),
        lax.psum(gain_parts[1].astype(jnp.bfloat16), "dp").astype(jnp.float32),
        lax.psum(grad_ups.astype(jnp.bfloat16), "dp").astype(jnp.float32),
        lax.psum(grad_down.astype(jnp.bfloat16), "dp").astype(jnp.float32),
    )
    (
        grad_pair,
        grad_conv,
        grad_gates,
        grad_gate_bias,
        grad_decay,
        grad_output,
        grad_gain_first,
        grad_gain_second,
        grad_ups,
        grad_down,
    ) = summed
    return (
        output,
        input_grad,
        final_state,
        final_conv,
        grad_gain_first,
        grad_pair[:, :channels],
        grad_pair[:, channels:],
        grad_conv,
        grad_gates,
        grad_gate_bias,
        grad_decay,
        grad_output,
        grad_gain_second,
        grad_ups[:, :hidden_cols],
        grad_ups[:, hidden_cols:],
        grad_down,
    )


def solution(mesh):
    in_specs = (
        P(("dp", "tensor"), None),
        P(("dp", "tensor"), None),
        P("dp"),
        P("dp", "tensor"),
        P("dp", None, "tensor"),
        P(),
        P(None, "tensor"),
        P(None, "tensor"),
        P(None, "tensor"),
        P(None, "tensor", None, None),
        P(None, "tensor"),
        P("tensor"),
        P("tensor", None),
        P(),
        P(None, "tensor"),
        P(None, "tensor"),
        P("tensor", None),
    )
    out_specs = (
        P(("dp", "tensor"), None),
        P(("dp", "tensor"), None),
        P("dp", "tensor"),
        P("dp", None, "tensor"),
        P("tensor"),
        P(None, "tensor"),
        P(None, "tensor"),
        P(None, "tensor"),
        P(None, "tensor", None, None),
        P(None, "tensor"),
        P("tensor"),
        P("tensor", None),
        P("tensor"),
        P(None, "tensor"),
        P(None, "tensor"),
        P("tensor", None),
    )
    return jax.shard_map(body, mesh=mesh, in_specs=in_specs, out_specs=out_specs, check_vma=False)
```

profile of v0, /device:TPU:8, one launch (start us, length us, event | category | flops | bytes accessed | tf_op | source)
XLA Modules:
  0.0 1657.6 jit_solution(1804354802632792584)
XLA Ops:
  17.1 76.4 %all-gather.5.cloned.1.call-done = bf16[2048,2048]{1,0:T(8,128)(2,1)} async-done(((bf16[256,2048]{1,0:T(8,128)(2,1)}), bf16[2048,2048]{1,0:T(8,128)(2,1)}) %all-gather.5.cloned.1.call-update) | async-done | bytes 8388624 | tf_op jit(solution)/shard_map/all_gather | solution.py:86
  131.1 12.6 copy.155
  380.3 87.4 %reduce-scatter.5.cloned.1.call-done = bf16[256,2048]{1,0:T(8,128)(2,1)} async-done(((bf16[2048,2048]{1,0:T(8,128)(2,1)}), bf16[256,2048]{1,0:T(8,128)(2,1)}) %reduce-scatter.5.cloned.1.call-update) | async-done | bytes 1048592 | tf_op jit(solution)/shard_map/reduce_scatter | solution.py:114
  479.1 74.4 %all-gather.7.cloned.1.call-done = bf16[2048,2048]{1,0:T(8,128)(2,1)} async-done(((bf16[256,2048]{1,0:T(8,128)(2,1)}), bf16[2048,2048]{1,0:T(8,128)(2,1)}) %all-gather.7.cloned.1.call-update) | async-done | bytes 8388624 | tf_op jit(solution)/shard_map/all_gather | solution.py:126
  553.4 19.4 %fusion.121 = f32[2048,1536]{0,1:T(8,128)} fusion(bf16[2048,2048]{1,0:T(8,128)(2,1)} %all-gather.7.cloned.1.call-done, bf16[2048,1536]{1,0:T(8,128)(2,1)} %constant_dynamic-update-slice_fusion.2), kind=kOutput, calls=%fused_computation.260 | convolution fusion | flops 12884901888 | bytes 27262976 | tf_op jit(solution)/shard_map/dot_general | solution.py:125
  572.8 62.7 %all-gather.9.cloned.1.call-done = bf16[2048,2048]{1,0:T(8,128)(2,1)} async-done(((bf16[256,2048]{1,0:T(8,128)(2,1)}), bf16[2048,2048]{1,0:T(8,128)(2,1)}) %all-gather.9.cloned.1.call-update) | async-done | bytes 8388624 | tf_op jit(solution)/shard_map/all_gather | solution.py:141
  635.5 17.5 %fusion.6 = (bf16[2048,768]{0,1:T(8,128)(2,1)S(1)}, bf16[2048,768]{0,1:T(8,128)(2,1)}, bf16[2048,768]{0,1:T(8,128)(2,1)}) fusion(f32[2048,1536]{0,1:T(8,128)} %fusion.121, bf16[2048,2048]{1,0:T(8,128)(2,1)} %all-gather.9.cloned.1.call-done, bf16[768,2048]{1,0:T(8,128)(2,1)S(1)} %copy-done), kind=kOutput, calls=%fused_computation.13 | convolution fusion | flops 6483345408 | bytes 33554432 | tf_op jit(solution)/shard_map/nd,fd->nf/dot_general | solution.py:142
  654.7 18.7 %convolution_convert_fusion.1 = bf16[2048,2048]{1,0:T(8,128)(2,1)} fusion(bf16[2048,1536]{1,0:T(8,128)(2,1)} %constant_dynamic-update-slice_fusion.2, bf16[2048,768]{0,1:T(8,128)(2,1)} %get-tuple-element.128, bf16[2048,768]{0,1:T(8,128)(2,1)S(1)} %get-tuple-element.127), kind=kOutput, calls=%fused_computation.3 | convolution fusion | flops 12901679104 | bytes 20971520 | tf_op jit(solution)/shard_map/nf,df->nd/dot_general | solution.py:148
  673.5 88.0 %reduce-scatter.9.cloned.1.call-done = bf16[256,2048]{1,0:T(8,128)(2,1)} async-done(((bf16[2048,2048]{1,0:T(8,128)(2,1)}), bf16[256,2048]{1,0:T(8,128)(2,1)}) %reduce-scatter.9.cloned.1.call-update) | async-done | bytes 1048592 | tf_op jit(solution)/shard_map/reduce_scatter | solution.py:147
  799.1 12.8 slice.656
  811.9 13.2 slice.647
  825.1 12.7 slice.649
  853.3 17.5 %convolution_convert_fusion.4 = bf16[2048,1536]{1,0:T(8,128)(2,1)} fusion(bf16[2048,2048]{1,0:T(8,128)(2,1)S(1)} %bitcast.134, bf16[2048,768]{0,1:T(8,128)(2,1)} %get-tuple-element.128, bf16[2048,768]{0,1:T(8,128)(2,1)} %copy-done.77), kind=kOutput, calls=%fused_computation.6 | convolution fusion | flops 12900630528 | bytes 20971520 | tf_op jit(solution)/shard_map/nd,nf->df/dot_general | solution.py:156
  870.8 12.3 fusion.66
  913.7 12.8 slice.651
  926.5 12.7 slice.653
  1020.6 13.1 slice.725
  1091.5 24.7 %rev.6 = f32[2,1024,344]{2,1,0:T(8,128)} reverse(f32[2,1024,344]{2,1,0:T(8,128)} %add.470), dimensions={1} | reverse | bytes 5636096 | tf_op jit(solution)/shard_map/jit(_flip)/rev | solution.py:175
  1160.1 11.6 multiply_reduce_fusion.4
  1185.5 11.7 convolution_convert_fusion.6
  1224.3 240.3 %all-reduce.59.cloned.1.call-done = (bf16[2048,688]{0,1:T(8,128)(2,1)}, bf16[2,2,172,172]{2,3,0,1:T(8,128)(2,1)}, bf16[2048,1536]{1,0:T(8,128)(2,1)}, bf16[344,2048]{1,0:T(8,128)(2,1)}, bf16[768,2048]{1,0:T(8,128)(2,1)}) async-done(((bf16[2048,688]{0,1:T(8,128)(2,1)}, bf16[2,2,172,172]{2,3,0,1:T(8,128)(2,1)}, bf16[2048,1536]{1,0:T(8,128)(2,1)}, bf16[344,2048]{1,0:T(8,128)(2,1)}, ...) | async-done | bytes 13900944 | tf_op jit(solution)/shard_map/psum | solution.py:214
  1483.1 70.6 %reduce-scatter.11.cloned.1.call-done = bf16[256,2048]{1,0:T(8,128)(2,1)} async-done(((bf16[2048,2048]{1,0:T(8,128)(2,1)}), bf16[256,2048]{1,0:T(8,128)(2,1)}) %reduce-scatter.11.cloned.1.call-update) | async-done | bytes 1048592 | tf_op jit(solution)/shard_map/reduce_scatter | solution.py:192
  1556.1 26.1 %all-reduce.54 = (bf16[2048]{0:T(1024)(128)(2,1)S(1)}, bf16[2048]{0:T(1024)(128)(2,1)S(1)}) all-reduce(f32[2048]{0:T(1024)S(1)} %get-tuple-element.103, f32[2048]{0:T(1024)S(1)} %copy-done.40), channel_id=6, replica_groups=mesh['dp'=4,'tensor'=8] {'tensor'}, use_global_device_ids=true, to_apply=%region_9.10.clone | all-reduce | flops 4096 | bytes 24576
  1595.4 49.1 %reduce-scatter.7.cloned.1.call-done = bf16[256,2048]{1,0:T(8,128)(2,1)} async-done(((bf16[2048,2048]{1,0:T(8,128)(2,1)}), bf16[256,2048]{1,0:T(8,128)(2,1)}) %reduce-scatter.7.cloned.1.call-update) | async-done | bytes 1048592 | tf_op jit(solution)/shard_map/reduce_scatter | solution.py:134
  (500 shorter events, 643.3 us)
Async XLA Ops:
  7.2 628.3 %copy-start = (bf16[768,2048]{1,0:T(8,128)(2,1)S(1)}, bf16[768,2048]{1,0:T(8,128)(2,1)}, u32[]{:S(2)}) copy-start(bf16[768,2048]{1,0:T(8,128)(2,1)} %param.33) | copy-start | bytes 9437188
  7.2 86.3 %all-gather.5.cloned.1.call-start = ((), (), s32[]{:S(2)}) async-start(), calls=%async_computation.4 | async-start | bytes 9437184 | tf_op jit(solution)/shard_map/all_gather | solution.py:86
  12.8 454.9 %reduce-scatter.5.cloned.1.call-start = ((), (), s32[]{:S(2)}) async-start(), calls=%async_computation.5 | async-start | bytes 9437184 | tf_op jit(solution)/shard_map/reduce_scatter | solution.py:114
  13.0 97.6 %copy-start.32 = (f32[2,3,344]{2,1,0:T(4,128)}, f32[2,3,344]{2,1,0:T(4,128)S(1)}, u32[]{:S(2)}) copy-start(f32[2,3,344]{2,1,0:T(4,128)S(1)} %copy.137) | copy-start | bytes 24772
  13.0 97.5 %copy-start.45 = (f32[344]{0:T(512)}, f32[344]{0:T(512)S(1)}, u32[]{:S(2)}) copy-start(f32[344]{0:T(512)S(1)} %get-tuple-element.106) | copy-start | bytes 4132
  13.0 97.5 %copy-start.47 = (f32[344]{0:T(512)}, f32[344]{0:T(512)S(1)}, u32[]{:S(2)}) copy-start(f32[344]{0:T(512)S(1)} %get-tuple-element.107) | copy-start | bytes 4132
  13.1 97.5 %copy-start.49 = (f32[344]{0:T(512)}, f32[344]{0:T(512)S(1)}, u32[]{:S(2)}) copy-start(f32[344]{0:T(512)S(1)} %get-tuple-element.108) | copy-start | bytes 4132
  13.1 97.5 %copy-start.51 = (f32[344]{0:T(512)}, f32[344]{0:T(512)S(1)}, u32[]{:S(2)}) copy-start(f32[344]{0:T(512)S(1)} %get-tuple-element.109) | copy-start | bytes 4132
  13.1 145.1 %copy-start.41 = (f32[344]{0:T(512)}, f32[344]{0:T(512)S(1)}, u32[]{:S(2)}) copy-start(f32[344]{0:T(512)S(1)} %broadcast_multiply_fusion.5) | copy-start | bytes 4132
  379.7 173.8 %all-gather.7.cloned.1.call-start = ((), (), s32[]{:S(2)}) async-start(), calls=%async_computation.6 | async-start | bytes 9437184 | tf_op jit(solution)/shard_map/all_gather | solution.py:126
  380.3 384.7 %copy-start.24 = (f32[2048]{0:T(1024)}, f32[2048]{0:T(1024)S(1)}, u32[]{:S(2)}) copy-start(f32[2048]{0:T(1024)S(1)} %convert_element_type.150) | copy-start | bytes 24580
  469.7 295.4 %copy-start.43 = (f32[256]{0:T(256)}, f32[256]{0:T(256)S(1)}, u32[]{:S(2)}) copy-start(f32[256]{0:T(256)S(1)} %add_rsqrt_fusion) | copy-start | bytes 3076
  472.6 162.8 %all-gather.9.cloned.1.call-start = ((), (), s32[]{:S(2)}) async-start(), calls=%async_computation.8 | async-start | bytes 9437184 | tf_op jit(solution)/shard_map/all_gather | solution.py:141
  473.2 288.3 %reduce-scatter.9.cloned.1.call-start = ((), (), s32[]{:S(2)}) async-start(), calls=%async_computation.9 | async-start | bytes 9437184 | tf_op jit(solution)/shard_map/reduce_scatter | solution.py:147
  673.4 197.4 %all-gather.11.cloned.1.call-start = ((), (), s32[]{:S(2)}) async-start(), calls=%async_computation.10 | async-start | bytes 9437184 | tf_op jit(solution)/shard_map/all_gather | solution.py:166
  769.0 695.6 %all-reduce.59.cloned.1.call-start = ((), (), s32[]{:S(2)}) async-start(), calls=%async_computation.12 | async-start | bytes 28049408 | tf_op jit(solution)/shard_map/psum | solution.py:214
  1197.1 356.6 %reduce-scatter.11.cloned.1.call-start = ((), (), s32[]{:S(2)}) async-start(), calls=%async_computation.11 | async-start | bytes 9437184 | tf_op jit(solution)/shard_map/reduce_scatter | solution.py:192
  1208.5 436.0 %reduce-scatter.7.cloned.1.call-start = ((), (), s32[]{:S(2)}) async-start(), calls=%async_computation.7 | async-start | bytes 9437184 | tf_op jit(solution)/shard_map/reduce_scatter | solution.py:134
  1477.4 76.3 %copy-start.31 = (f32[2048]{0:T(1024)S(1)}, f32[2048]{0:T(1024)}, u32[]{:S(2)}) copy-start(f32[2048]{0:T(1024)} %copy-done.30) | copy-start | bytes 24580
  1477.4 76.3 %copy-start.54 = (f32[256]{0:T(256)S(1)}, f32[256]{0:T(256)}, u32[]{:S(2)}) copy-start(f32[256]{0:T(256)} %copy-done.53) | copy-start | bytes 3076
  1477.4 78.7 %copy-start.40 = (f32[2048]{0:T(1024)S(1)}, f32[2048]{0:T(1024)}, u32[]{:S(2)}) copy-start(f32[2048]{0:T(1024)} %get-tuple-element.99) | copy-start | bytes 24580
  1477.4 167.1 %copy-start.25 = (f32[2048]{0:T(1024)S(1)}, f32[2048]{0:T(1024)}, u32[]{:S(2)}) copy-start(f32[2048]{0:T(1024)} %copy-done.24) | copy-start | bytes 24580
  1477.4 167.1 %copy-start.44 = (f32[256]{0:T(256)S(1)}, f32[256]{0:T(256)}, u32[]{:S(2)}) copy-start(f32[256]{0:T(256)} %copy-done.43) | copy-start | bytes 3076
  1477.4 167.1 %copy-start.64 = (f32[256]{0:T(256)S(1)}, f32[256]{0:T(256)}, u32[]{:S(2)}) copy-start(f32[256]{0:T(256)} %copy-done.63) | copy-start | bytes 3076
  (67 other events, 653.3 us)
Sparse Core Ops, SparseCore 0:
  12.9 80.5 all-gather.4
  379.8 87.9 reduce-scatter.4
  472.8 80.5 all-gather.6
  554.9 80.5 all-gather.8
  673.6 87.9 reduce-scatter.8
  769.1 80.6 all-gather.10
  1197.3 267.3 all-reduce.58
  1466.9 86.7 reduce-scatter.10
  1556.0 88.4 reduce-scatter.6
where the time goes:
time: 1690 us; the launch traced here: 1660 us
  waiting for transfers between devices  750 us (44%)
  local copies, waits for them, and re-layouts  508 us (30%)
  other arithmetic  182 us (11%)
  matrix products  166 us (10%)
  blocking collectives  36.2 us (2%)
    psum x1, waiting for transfers between devices, body(): lax.psum(grad_pair.astype(jnp.bfloat16), 'dp').astype(jnp.float32)  240 us
    slice x66, local copies, waits for them, and re-layouts, body(): lax.associative_scan(combine, (jnp.flip(decay_next, 1), jnp.flip(g_states...  196 us
    slice x59, local copies, waits for them, and re-layouts, body(): scanned = lax.associative_scan(combine, (decay_step, seeded), axis=1)  118 us
    reduce_scatter x1, waiting for transfers between devices, body(): lax.psum_scatter(jnp.einsum('nf,df->nd', g_ups, w_ups, preferred_element_...  88 us
    reduce_scatter x1, waiting for transfers between devices, body(): lax.psum_scatter(jnp.dot(mixture, w_output, preferred_element_type=jnp.fl...  87.4 us
    all_gather x1, waiting for transfers between devices, body(): lax.all_gather(normed_low, 'tensor', axis=0, tiled=True)  76.4 us
    all_gather x1, waiting for transfers between devices, body(): lax.all_gather(normed_mlp_low, 'tensor', axis=0, tiled=True)  74.4 us
    reduce_scatter x1, waiting for transfers between devices, body(): lax.psum_scatter(jnp.einsum('nr,dr->nd', g_inputs, w_pair, preferred_elem...  70.6 us
  transfers between devices with their start and end apart: 9, of which 8 were waited for; matrix products, arithmetic and copies ran while one was open for 11% of the time, Pallas kernels for 0%

commit v1 on v0

v1 whole, which is shorter than its diff:
```python
import functools

import jax
import jax.numpy as jnp
from jax import lax
from jax.experimental import pallas as pl
from jax.experimental.pallas import tpu as pltpu
from jax.sharding import PartitionSpec as P

EPSILON = 1e-06
KAPPA = 0.7978845608028654
CUBIC = 0.044715
PIECES = 2
F32 = jnp.float32
BF16 = jnp.bfloat16
ANY = pl.BlockSpec(memory_space=pl.ANY)
VM = pl.BlockSpec(memory_space=pltpu.VMEM)
VMEM_LIMIT = 61 * 1024 * 1024
MESH = pl.DeviceIdType.MESH


def dot(a, b):
    return jnp.dot(a, b, preferred_element_type=F32)


def dot_nt(a, b):
    return lax.dot_general(a, b, (((1,), (1,)), ((), ())), preferred_element_type=F32)


def dot_tn(a, b):
    return lax.dot_general(a, b, (((0,), (0,)), ((), ())), preferred_element_type=F32)


def tile_of(extent, wanted):
    while extent % wanted:
        wanted //= 2
    return wanted


def span(i, size):
    return pl.ds(pl.multiple_of(i * size, size), size)


def loop(count, body):
    def step(i, carry):
        body(i)
        return carry

    lax.fori_loop(0, count, step, 0)


class Place:
    def __init__(self, n):
        self.n = n
        self.nz = n // 2
        self.t = lax.axis_index("tensor")
        self.c = lax.rem(self.t, 2)
        self.j = lax.div(self.t, 2)
        self.sib = self.t + 1 - 2 * self.c
        self.has_up = self.j < self.nz - 1
        self.has_down = self.j > 0

    def greet(self):
        barrier = pltpu.get_barrier_semaphore()

        def signal(t):
            pl.semaphore_signal(barrier, inc=1, device_id={"tensor": t}, device_id_type=MESH)

        signal(self.sib)
        pl.when(self.has_up)(lambda: signal(self.t + 2))
        pl.when(self.has_down)(lambda: signal(self.t - 2))
        pl.semaphore_wait(
            barrier, 1 + self.has_up.astype(jnp.int32) + self.has_down.astype(jnp.int32)
        )

    def copy(self, src, dst, send, recv, t):
        return pltpu.make_async_remote_copy(
            src_ref=src,
            dst_ref=dst,
            send_sem=send,
            recv_sem=recv,
            device_id={"tensor": t},
            device_id_type=MESH,
        )


class Gather:
    def __init__(self, place, full, sent, came):
        self.place, self.full, self.sent, self.came = place, full, sent, came
        self.pieces = full.shape[1]

    @staticmethod
    def scratch(n, rows, width):
        return [
            pltpu.VMEM((n, PIECES, rows // PIECES, width), BF16),
            pltpu.SemaphoreType.DMA((n, PIECES, 3)),
            pltpu.SemaphoreType.DMA((n, PIECES)),
        ]

    def copy(self, t, p, way, to):
        return self.place.copy(
            self.full.at[t, p],
            self.full.at[t, p],
            self.sent.at[t, p, way],
            self.came.at[t, p],
            to,
        )

    def start(self):
        g = self.place
        for p in range(self.pieces):
            pl.when(g.has_up)(lambda: self.copy(g.t, p, 0, g.t + 2).start())
            pl.when(g.has_down)(lambda: self.copy(g.t, p, 1, g.t - 2).start())
        for p in range(self.pieces):
            self.copy(g.t, p, 2, g.sib).start()

    def forward(self, d):
        g = self.place
        for p in range(self.pieces):

            @pl.when(g.j - d >= 0)
            def _():
                t = g.t - 2 * d
                self.copy(t, p, 0, g.sib).wait_recv()
                pl.when(g.has_up)(lambda: self.copy(t, p, 0, g.t + 2).start())
                self.copy(t, p, 2, g.sib).start()

            @pl.when(g.j + d < g.nz)
            def _():
                t = g.t + 2 * d
                self.copy(t, p, 1, g.sib).wait_recv()
                pl.when(g.has_down)(lambda: self.copy(t, p, 1, g.t - 2).start())
                self.copy(t, p, 2, g.sib).start()

    def each(self, d, use):
        g = self.place

        def visit(q):
            core, way = lax.div(q, 2), 2 * lax.rem(q, 2) - 1
            j = g.j + way * d
            there = jnp.logical_and(j >= 0, j < g.nz)

            @pl.when(jnp.logical_and(there, jnp.logical_or(d > 0, way > 0)))
            def _():
                t = 2 * j + lax.rem(g.c + core, 2)

                @pl.when(core > 0)
                def _():
                    for p in range(self.pieces):
                        self.copy(t, p, 2, g.sib).wait_recv()

                use(t)

        loop(4, visit)

    def finish(self):
        g = self.place

        def done(t):
            for p in range(self.pieces):
                self.copy(t, p, 2, g.sib).wait_send()

                @pl.when(jnp.logical_and(t <= g.t, g.has_up))
                def _():
                    self.copy(t, p, 0, g.sib).wait_send()

                @pl.when(jnp.logical_and(t >= g.t, g.has_down))
                def _():
                    self.copy(t, p, 1, g.sib).wait_send()

        loop(g.nz, lambda k: done(2 * k + g.c))


class Scatter:
    def __init__(self, place, partial, tile, bufs):
        self.place, self.partial, self.tile = place, partial, tile
        self.to_sib, self.from_sib, self.line, self.out, self.acc = bufs[:5]
        self.sib_send, self.sib_recv, self.line_send, self.line_recv = bufs[5:]
        self.tiles = self.acc.shape[1] // tile

    @staticmethod
    def scratch(n, rows, width):
        nz = n // 2
        return [
            pltpu.VMEM((nz, rows, width), BF16),
            pltpu.VMEM((nz, rows, width), BF16),
            pltpu.VMEM((nz + 1, rows, width), BF16),
            pltpu.VMEM((nz, rows, width), BF16),
            pltpu.VMEM((rows, width), F32),
            pltpu.SemaphoreType.DMA((nz,)),
            pltpu.SemaphoreType.DMA((nz,)),
            pltpu.SemaphoreType.DMA((nz,)),
            pltpu.SemaphoreType.DMA((nz + 1,)),
        ]

    def sib_copy(self, k):
        return self.place.copy(
            self.to_sib.at[k],
            self.from_sib.at[k],
            self.sib_send.at[k],
            self.sib_recv.at[k],
            self.place.sib,
        )

    def line_copy(self, k, slot, to):
        return self.place.copy(
            self.out.at[k], self.line.at[slot], self.line_send.at[k], self.line_recv.at[slot], to
        )

    def offer(self, k):
        t = 2 * k + 1 - self.place.c

        def part(i):
            cols = span(i, self.tile)
            self.to_sib[k, :, cols] = self.partial(t, cols).astype(BF16)

        loop(self.tiles, part)
        self.sib_copy(k).start()

    def pair(self, k):
        self.sib_copy(k).wait_recv()
        t = 2 * k + self.place.c

        def part(i):
            cols = span(i, self.tile)
            self.acc[:, cols] = self.partial(t, cols) + self.from_sib[k, :, cols].astype(F32)

        loop(self.tiles, part)

    def offers(self, d):
        g = self.place

        def way_of(w):
            k = g.j + (1 - 2 * w) * d

            @pl.when(jnp.logical_and(jnp.logical_and(k >= 0, k < g.nz), jnp.logical_or(d > 0, w == 0)))
            def _():
                self.offer(k)

        loop(2, way_of)

    def step(self, d):
        g = self.place

        def way_of(w):
            sign = 1 - 2 * w
            k = g.j + sign * d

            @pl.when(jnp.logical_and(k >= 0, k < g.nz))
            def _():
                self.pair(k)
                upstream = g.j - sign
                more = jnp.logical_and(upstream >= 0, upstream < g.nz)

                @pl.when(more)
                def _():
                    self.line_copy(k, k, g.sib).wait_recv()
                    self.out[k] = (self.acc[...] + self.line[k].astype(F32)).astype(BF16)

                @pl.when(jnp.logical_not(more))
                def _():
                    self.out[k] = self.acc[...].astype(BF16)

                slot = jnp.where(jnp.logical_and(d == 1, w == 1), g.nz, k)
                self.line_copy(k, slot, g.t + 2 * sign).start()

        loop(2, way_of)

    def last(self):
        g = self.place
        self.pair(g.j)

        @pl.when(g.has_down)
        def _():
            self.line_copy(g.j, g.j, g.sib).wait_recv()
            self.acc[...] += self.line[g.j].astype(F32)

        @pl.when(g.has_up)
        def _():
            self.line_copy(g.j, g.nz, g.sib).wait_recv()
            self.acc[...] += self.line[g.nz].astype(F32)

    def finish(self):
        g = self.place

        def done(k):
            self.sib_copy(k).wait_send()
            pl.when(g.j != k)(lambda: self.line_copy(k, k, g.sib).wait_send())

        loop(g.nz, done)


def comm_params(collective_id):
    return pltpu.CompilerParams(
        collective_id=collective_id, has_side_effects=True, vmem_limit_bytes=VMEM_LIMIT
    )


def cost(flops):
    return pl.CostEstimate(flops=int(flops), bytes_accessed=200_000_000, transcendentals=0)


def shape(*dims, dtype=F32):
    return jax.ShapeDtypeStruct(dims, dtype)


def inv_rms(values):
    return lax.rsqrt(jnp.mean(values * values, axis=-1, keepdims=True) + EPSILON)


def norm_grad(values, gain, gradient):
    inv = inv_rms(values)
    unit = values * inv
    scaled = gradient * gain
    centred = jnp.mean(scaled * unit, axis=-1, keepdims=True)
    return inv * (scaled - unit * centred), gradient * unit


def sigmoid(v):
    return 1.0 / (1.0 + jnp.exp(-v))


def gelu_parts(v):
    square = v * v
    bend = jnp.tanh(KAPPA * v * (1.0 + CUBIC * square))
    half = 0.5 * (1.0 + bend)
    slope = half + 0.5 * v * (1.0 - bend * bend) * (KAPPA * (1.0 + 3.0 * CUBIC * square))
    return v * half, slope


def one_minus_square(log_decay, decay):
    m = -2.0 * log_decay
    series = m * (
        1.0 - m * (1 / 2) * (1.0 - m * (1 / 3) * (1.0 - m * (1 / 4) * (1.0 - m * (1 / 5) * (1.0 - m * (1 / 6)))))
    )
    return jnp.where(m < 0.35, series, 1.0 - decay * decay)


def project_kernel(n, tokens, gain, w_in, w_br, normed, recur, branch, full, sent, came, held_a, held_b, saved):
    g = Place(n)
    gather = Gather(g, full, sent, came)
    size = full.shape[2]
    for p in range(PIECES):
        values = tokens[p * size : (p + 1) * size].astype(F32)
        full[g.t, p] = (values * inv_rms(values) * gain[...].astype(F32)).astype(BF16)
    g.greet()
    gather.start()

    def use(t):
        pltpu.make_async_copy(full.at[t], normed.at[t], saved.at[t, 0]).start()
        for p in range(PIECES):
            rows = slice(p * size, (p + 1) * size)
            held_a[t, rows] = dot(full[t, p], w_in[...])
            held_b[t, rows] = dot(full[t, p], w_br[...])
        pltpu.make_async_copy(held_a.at[t], recur.at[t], saved.at[t, 1]).start()
        pltpu.make_async_copy(held_b.at[t], branch.at[t], saved.at[t, 2]).start()

    gather.each(0, use)

    def away(i):
        gather.forward(i + 1)
        gather.each(i + 1, use)

    loop(g.nz - 1, away)

    def done(t):
        pltpu.make_async_copy(full.at[t], normed.at[t], saved.at[t, 0]).wait()
        pltpu.make_async_copy(held_a.at[t], recur.at[t], saved.at[t, 1]).wait()
        pltpu.make_async_copy(held_b.at[t], branch.at[t], saved.at[t, 2]).wait()

    loop(n, done)
    gather.finish()


def project(n, tokens, gain, w_in, w_br):
    rows, width = tokens.shape
    channels = w_in.shape[1]
    return pl.pallas_call(
        functools.partial(project_kernel, n),
        out_shape=(
            shape(n, PIECES, rows // PIECES, width, dtype=BF16),
            shape(n, rows, channels),
            shape(n, rows, channels),
        ),
        in_specs=[VM] * 4,
        out_specs=(ANY,) * 3,
        scratch_shapes=Gather.scratch(n, rows, width)
        + [pltpu.VMEM((n, rows, channels), F32)] * 2
        + [pltpu.SemaphoreType.DMA((n, 3))],
        compiler_params=comm_params(1),
        cost_estimate=cost(4 * n * rows * width * channels),
        name="project",
    )(tokens, gain, w_in, w_br)


def recur_kernel(
    u, branch, start_state, start_conv, conv, gate_w, bias, decay,
    states, mixture, conv_low, recall, ingate, final_state, final_conv,
    hist, decay_buf, drive_buf, carry,
):
    chunk = pl.program_id(1)
    rows, channels = u.shape
    tile = 32

    @pl.when(chunk == 0)
    def _():
        carry[...] = jnp.broadcast_to(start_state[0], (8, channels))
        hist[0:8] = jnp.concatenate([jnp.zeros((5, channels), F32), start_conv[0]], axis=0)

    @pl.when(chunk > 0)
    def _():
        hist[0:8] = hist[rows : rows + 8]

    hist[8:] = u[...]

    def convolve(i):
        window = hist[pl.ds(pl.multiple_of(i * tile, tile), tile + 8)]
        value = conv[4:5] + conv[0:1] * window[8:] + conv[1:2] * window[7 : tile + 7]
        value = value + conv[2:3] * window[6 : tile + 6] + conv[3:4] * window[5 : tile + 5]
        conv_low[span(i, tile)] = value.astype(BF16)

    loop(rows // tile, convolve)
    low = conv_low[...]
    recall[...] = dot(low, gate_w[0])
    ingate[...] = dot(low, gate_w[1])

    def gates(i):
        at = span(i, tile)
        r = sigmoid(recall[at] + bias[0:1])
        k = sigmoid(ingate[at] + bias[1:2])
        recall[at] = r
        ingate[at] = k
        log_decay = -8.0 * r * decay[...]
        step = jnp.exp(log_decay)
        decay_buf[at] = step
        drive_buf[at] = jnp.sqrt(one_minus_square(log_decay, step)) * k * conv_low[at].astype(F32)

    loop(rows // tile, gates)
    row = lax.broadcasted_iota(jnp.int32, (8, channels), 0)

    def scan(i, before):
        for part in range(4):
            at = pl.ds(pl.multiple_of(i * 32 + part * 8, 8), 8)
            a, b = decay_buf[at], drive_buf[at]
            for shift in (1, 2, 4):
                inside = row >= shift
                b = b + a * jnp.where(inside, pltpu.roll(b, shift, 0), 0.0)
                a = a * jnp.where(inside, pltpu.roll(a, shift, 0), 1.0)
            h = a * before + b
            states[at] = h
            before = jnp.broadcast_to(h[7:8], (8, channels))
        return before

    carry[...] = lax.fori_loop(0, rows // 32, scan, carry[...])

    def mix(i):
        at = span(i, tile)
        value, _ = gelu_parts(branch[at])
        mixture[at] = (states[at] * value).astype(BF16)

    loop(rows // tile, mix)

    @pl.when(chunk == pl.num_programs(1) - 1)
    def _():
        final_state[0] = carry[0:1]
        final_conv[0] = hist[rows + 5 : rows + 8]


def recur_forward(u, branch, start_state, start_conv, conv, gate_w, bias, decay):
    total, channels = u.shape
    sequences = start_state.shape[0]
    length = total // sequences
    rows = tile_of(length, 256)
    chunks = length // rows
    block = pl.BlockSpec((rows, channels), lambda s, c: (s * chunks + c, 0))

    def whole(x):
        return pl.BlockSpec(x.shape, lambda s, c: (0,) * x.ndim)

    return pl.pallas_call(
        recur_kernel,
        grid=(sequences, chunks),
        out_shape=(
            shape(total, channels),
            shape(total, channels, dtype=BF16),
            shape(total, channels, dtype=BF16),
            shape(total, channels),
            shape(total, channels),
            shape(sequences, 1, channels),
            shape(sequences, 3, channels),
        ),
        in_specs=[
            block,
            block,
            pl.BlockSpec((1, 1, channels), lambda s, c: (s, 0, 0)),
            pl.BlockSpec((1, 3, channels), lambda s, c: (s, 0, 0)),
            whole(conv),
            whole(gate_w),
            whole(bias),
            whole(decay),
        ],
        out_specs=(block,) * 5
        + (
            pl.BlockSpec((1, 1, channels), lambda s, c: (s, 0, 0)),
            pl.BlockSpec((1, 3, channels), lambda s, c: (s, 0, 0)),
        ),
        scratch_shapes=[
            pltpu.VMEM((rows + 8, channels), F32),
            pltpu.VMEM((rows, channels), F32),
            pltpu.VMEM((rows, channels), F32),
            pltpu.VMEM((8, channels), F32),
        ],
        compiler_params=pltpu.CompilerParams(vmem_limit_bytes=VMEM_LIMIT),
        name="recur_forward",
    )(u, branch, start_state, start_conv, conv, gate_w, bias, decay)


def mixer_out_kernel(
    n, mixture, w_output, cotangent, tokens, gain, cot_full, residual, normed,
    full, sent, came, saved, *bufs
):
    g = Place(n)
    gather = Gather(g, full, sent, came)
    scatter = Scatter(g, lambda t, cols: dot(mixture[t], w_output[:, cols]), tile_of(residual.shape[1], 512), bufs)
    size = full.shape[2]
    for p in range(PIECES):
        full[g.t, p] = cotangent[p * size : (p + 1) * size]
    g.greet()

    def use(t):
        pltpu.make_async_copy(full.at[t], cot_full.at[t], saved.at[t]).start()

    scatter.offers(g.nz - 1)
    gather.start()

    def around(i):
        d = g.nz - 1 - i
        scatter.offers(d - 1)
        scatter.step(d)
        gather.each(i, use)
        gather.forward(i + 1)

    loop(g.nz - 1, around)
    scatter.last()
    part = 64

    def rows_of(i):
        at = span(i, part)
        values = scatter.acc[at] + tokens[at].astype(F32)
        residual[at] = values
        normed[at] = (values * inv_rms(values) * gain[...].astype(F32)).astype(BF16)

    loop(residual.shape[0] // part, rows_of)
    gather.each(g.nz - 1, use)
    loop(n, lambda t: pltpu.make_async_copy(full.at[t], cot_full.at[t], saved.at[t]).wait())
    scatter.finish()
    gather.finish()


def mixer_out(n, mixture, w_output, cotangent, tokens, gain):
    rows, width = tokens.shape
    return pl.pallas_call(
        functools.partial(mixer_out_kernel, n),
        out_shape=(
            shape(n, PIECES, rows // PIECES, width, dtype=BF16),
            shape(rows, width),
            shape(rows, width, dtype=BF16),
        ),
        in_specs=[VM] * 5,
        out_specs=(ANY, VM, VM),
        scratch_shapes=Gather.scratch(n, rows, width)
        + [pltpu.SemaphoreType.DMA((n,))]
        + Scatter.scratch(n, rows, width),
        compiler_params=comm_params(2),
        cost_estimate=cost(2 * n * rows * width * mixture.shape[-1]),
        name="mixer_out",
    )(mixture, w_output, cotangent, tokens, gain)


def mlp_kernel(
    n, normed, cot_full, w_gelu, w_linear, w_down, hidden, g_first, g_second, grad_gelu, grad_linear, grad_down,
    full, sent, came, cot, keep_h, keep_f, keep_s, acc_g, acc_l, acc_d, stage_c, stage_w, saved, fetched, drained,
):
    g = Place(n)
    gather = Gather(g, full, sent, came)
    size = full.shape[2]
    rows = PIECES * size
    columns = w_gelu.shape[1]
    width = full.shape[3]
    tile = tile_of(columns, 256)
    wide = tile_of(width, 512)
    for p in range(PIECES):
        full[g.t, p] = normed[p * size : (p + 1) * size]
    g.greet()
    gather.start()
    acc_g[...] = jnp.zeros_like(acc_g)
    acc_l[...] = jnp.zeros_like(acc_l)
    acc_d[...] = jnp.zeros_like(acc_d)

    def save(t, i, start):
        for q, (held, out) in enumerate(((keep_h, hidden), (keep_f, g_first), (keep_s, g_second))):
            copy = pltpu.make_async_copy(held.at[t], out.at[t], saved.at[t, q])
            copy.start() if start else copy.wait()

    def use(t):
        fetch = pltpu.make_async_copy(cot_full.at[t], cot, fetched)
        fetch.start()
        fetch.wait()

        def piece(p):
            at = span(p, size)

            def part(i):
                cols = span(i, tile)
                first = dot(full[t, p], w_gelu[:, cols])
                second = dot(full[t, p], w_linear[:, cols])
                back = dot_nt(cot[p], w_down[cols])
                value, slope = gelu_parts(first)
                keep_h[t, at, cols] = (value * second).astype(BF16)
                keep_f[t, at, cols] = (back * second * slope).astype(BF16)
                keep_s[t, at, cols] = (back * value).astype(BF16)

            loop(columns // tile, part)

        loop(PIECES, piece)
        save(t, 0, True)

        def part(i):
            at = span(i, wide)
            for p in range(PIECES):
                rows_p = slice(p * size, (p + 1) * size)
                acc_g[at] += dot_tn(full[t, p, :, at], keep_f[t, rows_p])
                acc_l[at] += dot_tn(full[t, p, :, at], keep_s[t, rows_p])
                acc_d[:, at] += dot_tn(keep_h[t, rows_p], cot[p, :, at])

        loop(width // wide, part)

    gather.each(0, use)

    def away(i):
        gather.forward(i + 1)
        gather.each(i + 1, use)

    loop(g.nz - 1, away)
    loop(n, lambda t: save(t, 0, False))
    gather.finish()

    def drain(acc, stage, out, sem):
        part = stage.shape[1]

        def move(i):
            slot = lax.rem(i, 2)
            at = span(i, part)
            copy = pltpu.make_async_copy(stage.at[slot], out.at[at], sem.at[slot])
            pl.when(i >= 2)(copy.wait)
            stage[slot] = acc[at].astype(BF16)
            copy.start()

        count = acc.shape[0] // part
        loop(count, move)
        for slot in range(min(count, 2)):
            pltpu.make_async_copy(stage.at[slot], out.at[0:part], sem.at[slot]).wait()

    drain(acc_g, stage_c, grad_gelu, drained)
    drain(acc_l, stage_c, grad_linear, drained)
    drain(acc_d, stage_w, grad_down, drained)


def mlp(n, normed, cot_full, w_gelu, w_linear, w_down):
    rows, width = normed.shape
    columns = w_gelu.shape[1]
    kept = pltpu.VMEM((n, rows, columns), BF16)
    return pl.pallas_call(
        functools.partial(mlp_kernel, n),
        out_shape=(shape(n, rows, columns, dtype=BF16),) * 3
        + (shape(width, columns, dtype=BF16),) * 2
        + (shape(columns, width, dtype=BF16),),
        in_specs=[VM, ANY, VM, VM, VM],
        out_specs=(ANY,) * 6,
        scratch_shapes=Gather.scratch(n, rows, width)
        + [pltpu.VMEM((PIECES, rows // PIECES, width), BF16)]
        + [kept] * 3
        + [pltpu.VMEM((width, columns), F32)] * 2
        + [pltpu.VMEM((columns, width), F32)]
        + [pltpu.VMEM((2, tile_of(width, 256), columns), BF16)]
        + [pltpu.VMEM((2, tile_of(columns, 128), width), BF16)]
        + [pltpu.SemaphoreType.DMA((n, 3)), pltpu.SemaphoreType.DMA, pltpu.SemaphoreType.DMA((2,))],
        compiler_params=comm_params(3),
        cost_estimate=cost(12 * n * rows * width * columns),
        name="mlp",
    )(normed, cot_full, w_gelu, w_linear, w_down)


def mlp_back_kernel(n, g_first, g_second, w_gelu, w_linear, residual, cotangent, gain, g_residual, g_low, g_gain, *bufs):
    g = Place(n)

    def partial(t, cols):
        return dot_nt(g_first[t], w_gelu[cols]) + dot_nt(g_second[t], w_linear[cols])

    scatter = Scatter(g, partial, tile_of(residual.shape[1], 512), bufs)
    g.greet()
    scatter.offers(g.nz - 1)

    def around(i):
        d = g.nz - 1 - i
        scatter.offers(d - 1)
        scatter.step(d)

    loop(g.nz - 1, around)
    scatter.last()
    part = 32
    g_gain[...] = jnp.zeros_like(g_gain)

    def rows_of(i):
        at = span(i, part)
        back, terms = norm_grad(residual[at], gain[...].astype(F32), scatter.acc[at])
        value = cotangent[at].astype(F32) + back
        g_residual[at] = value
        g_low[at] = value.astype(BF16)
        g_gain[...] += jnp.sum(terms, axis=0, keepdims=True)

    loop(residual.shape[0] // part, rows_of)
    scatter.finish()


def mlp_back(n, g_first, g_second, w_gelu, w_linear, residual, cotangent, gain):
    rows, width = residual.shape
    return pl.pallas_call(
        functools.partial(mlp_back_kernel, n),
        out_shape=(shape(rows, width), shape(rows, width, dtype=BF16), shape(1, width)),
        in_specs=[VM] * 7,
        out_specs=(VM,) * 3,
        scratch_shapes=Scatter.scratch(n, rows, width),
        compiler_params=comm_params(4),
        cost_estimate=cost(4 * n * rows * width * w_gelu.shape[1]),
        name="mlp_back",
    )(g_first, g_second, w_gelu, w_linear, residual, cotangent, gain)


def down_kernel(
    n, hidden, w_down, residual, g_low, w_output, mixture, output, g_mixture, grad_output,
    full, sent, came, acc_o, *bufs
):
    g = Place(n)
    gather = Gather(g, full, sent, came)
    width = residual.shape[1]
    wide = tile_of(width, 512)
    scatter = Scatter(g, lambda t, cols: dot(hidden[t], w_down[:, cols]), wide, bufs)
    size = full.shape[2]
    for p in range(PIECES):
        full[g.t, p] = g_low[p * size : (p + 1) * size]
    g.greet()

    def use(t):
        for p in range(PIECES):
            rows = slice(p * size, (p + 1) * size)
            g_mixture[t, rows] = dot_nt(full[t, p], w_output[...])

        def part(i):
            at = span(i, wide)
            for p in range(PIECES):
                rows = slice(p * size, (p + 1) * size)
                acc_o[:, at] += dot_tn(mixture[t, rows], full[t, p, :, at])

        loop(width // wide, part)

    gather.start()
    acc_o[...] = jnp.zeros_like(acc_o)
    scatter.offers(g.nz - 1)

    def around(i):
        d = g.nz - 1 - i
        scatter.offers(d - 1)
        scatter.step(d)
        gather.each(i, use)
        gather.forward(i + 1)

    loop(g.nz - 1, around)
    gather.each(g.nz - 1, use)
    grad_output[...] = acc_o[...].astype(BF16)
    scatter.last()
    output[...] = (scatter.acc[...] + residual[...]).astype(BF16)
    scatter.finish()
    gather.finish()


def down(n, hidden, w_down, residual, g_low, w_output, mixture):
    rows, width = residual.shape
    channels = w_output.shape[0]
    return pl.pallas_call(
        functools.partial(down_kernel, n),
        out_shape=(
            shape(rows, width, dtype=BF16),
            shape(n, rows, channels),
            shape(channels, width, dtype=BF16),
        ),
        in_specs=[VM] * 6,
        out_specs=(VM,) * 3,
        scratch_shapes=Gather.scratch(n, rows, width)
        + [pltpu.VMEM((channels, width), F32)]
        + Scatter.scratch(n, rows, width),
        compiler_params=comm_params(5),
        cost_estimate=cost(2 * n * rows * width * (hidden.shape[-1] + 2 * channels)),
        name="down",
    )(hidden, w_down, residual, g_low, w_output, mixture)


def recur_back_kernel(
    g_mix, branch, states, states_before, u, u_before, conv_low, recall, ingate, start_state, start_conv,
    conv, gate_w, decay,
    g_recur, g_branch, small, g_gates,
    g_state, step_buf, root_buf, g_conv, pre_r, pre_i, carry, hist_s, hist_u, sums,
):
    sequence, back = pl.program_id(0), pl.program_id(1)
    last = pl.num_programs(1) - 1
    rows, channels = u.shape
    tile = 32

    @pl.when(jnp.logical_and(sequence == 0, back == 0))
    def _():
        sums[...] = jnp.zeros_like(sums)
        g_gates[...] = jnp.zeros_like(g_gates)

    @pl.when(back == 0)
    def _():
        carry[...] = jnp.zeros_like(carry)
        g_conv[rows : rows + 8] = jnp.zeros((8, channels), F32)

    @pl.when(back > 0)
    def _():
        g_conv[rows : rows + 8] = g_conv[0:8]

    @pl.when(back == last)
    def _():
        hist_s[0:8] = jnp.broadcast_to(start_state[0], (8, channels))
        hist_u[0:8] = jnp.concatenate([jnp.zeros((5, channels), F32), start_conv[0]], axis=0)

    @pl.when(back < last)
    def _():
        hist_s[0:8] = states_before[...]
        hist_u[0:8] = u_before[...]

    hist_s[8:] = states[...]
    hist_u[8:] = u[...]

    def first(i):
        at = span(i, tile)
        value, slope = gelu_parts(branch[at])
        gm = g_mix[at]
        g_state[at] = gm * value
        g_branch[at] = (gm * states[at] * slope).astype(BF16)
        log_decay = -8.0 * recall[at] * decay[...]
        step = jnp.exp(log_decay)
        step_buf[at] = step
        root_buf[at] = jnp.sqrt(one_minus_square(log_decay, step))

    loop(rows // tile, first)
    row = lax.broadcasted_iota(jnp.int32, (8, channels), 0)
    groups = rows // 32

    def scan(i, after):
        for part in range(4):
            at = pl.ds(pl.multiple_of((groups - 1 - i) * 32 + (3 - part) * 8, 8), 8)
            a, gs = step_buf[at], g_state[at]
            b = a * gs
            for shift in (1, 2, 4):
                inside = row < 8 - shift
                b = b + a * jnp.where(inside, pltpu.roll(b, 8 - shift, 0), 0.0)
                a = a * jnp.where(inside, pltpu.roll(a, 8 - shift, 0), 1.0)
            e = a * after + b
            g_state[at] = gs + jnp.where(row < 7, pltpu.roll(e, 7, 0), after)
            after = jnp.broadcast_to(e[0:1], (8, channels))
        return after

    carry[...] = lax.fori_loop(0, groups, scan, carry[...])

    def fold(x):
        return jnp.sum(x.reshape(tile // 8, 8, channels), axis=0)

    def second(i):
        at = span(i, tile)
        window = hist_s[pl.ds(pl.multiple_of(i * tile, tile), tile + 8)]
        before = window[7 : tile + 7]
        g, r, k = g_state[at], recall[at], ingate[at]
        c = conv_low[at].astype(F32)
        step, root = step_buf[at], root_buf[at]
        kc = k * c
        g_log = g * (before * step - kc * (step * step) / root)
        slow = -8.0 * r
        sums[7] += fold(g_log * slow)
        low_r = (g_log * (slow * decay[...]) * (1.0 - r)).astype(BF16)
        low_i = (g * root * kc * (1.0 - k)).astype(BF16)
        pre_r[at] = low_r
        pre_i[at] = low_i
        sums[5] += fold(low_r.astype(F32))
        sums[6] += fold(low_i.astype(F32))
        g_conv[at] = g * root * k

    loop(rows // tile, second)
    low_r, low_i, low_c = pre_r[...], pre_i[...], conv_low[...]
    g_gates[0] += dot_tn(low_c, low_r)
    g_gates[1] += dot_tn(low_c, low_i)
    g_conv[0:rows] += dot_nt(low_r, gate_w[0]) + dot_nt(low_i, gate_w[1])

    def third(i):
        at = span(i, tile)
        start = pl.multiple_of(i * tile, tile)
        window = g_conv[pl.ds(start, tile + 8)]
        value = conv[0:1] * window[0:tile]
        for k in (1, 2, 3):
            value = value + conv[k : k + 1] * window[k : tile + k]
        g_recur[at] = value.astype(BF16)
        past = hist_u[pl.ds(start, tile + 8)]
        gc = window[0:tile]
        for k in range(4):
            sums[k] += fold(gc * past[8 - k : tile + 8 - k])
        sums[4] += fold(gc)

    loop(rows // tile, third)

    @pl.when(jnp.logical_and(sequence == pl.num_programs(0) - 1, back == last))
    def _():
        small[...] = jnp.sum(sums[...], axis=1)


def recur_back(g_mix, branch, states, u, conv_low, recall, ingate, start_state, start_conv, conv, gate_w, decay):
    total, channels = u.shape
    sequences = start_state.shape[0]
    length = total // sequences
    rows = tile_of(length, 256)
    chunks = length // rows
    eights = rows // 8

    def at(s, c):
        return (s * chunks + chunks - 1 - c, 0)

    def earlier(s, c):
        return (jnp.maximum((s * chunks + chunks - 1 - c) * eights - 1, 0), 0)

    block = pl.BlockSpec((rows, channels), at)
    before = pl.BlockSpec((8, channels), earlier)

    def whole(x):
        return pl.BlockSpec(x.shape, lambda s, c: (0,) * x.ndim)

    wide = pltpu.VMEM((rows, channels), F32)
    narrow = pltpu.VMEM((rows, channels), BF16)
    long = pltpu.VMEM((rows + 8, channels), F32)
    return pl.pallas_call(
        recur_back_kernel,
        grid=(sequences, chunks),
        out_shape=(
            shape(total, channels, dtype=BF16),
            shape(total, channels, dtype=BF16),
            shape(8, channels),
            shape(2, channels, channels),
        ),
        in_specs=[
            block, block, block, before, block, before, block, block, block,
            pl.BlockSpec((1, 1, channels), lambda s, c: (s, 0, 0)),
            pl.BlockSpec((1, 3, channels), lambda s, c: (s, 0, 0)),
            whole(conv), whole(gate_w), whole(decay),
        ],
        out_specs=(
            block,
            block,
            pl.BlockSpec((8, channels), lambda s, c: (0, 0)),
            pl.BlockSpec((2, channels, channels), lambda s, c: (0, 0, 0)),
        ),
        scratch_shapes=[
            wide, wide, wide, long, narrow, narrow,
            pltpu.VMEM((8, channels), F32), long, long,
            pltpu.VMEM((8, 8, channels), F32),
        ],
        compiler_params=pltpu.CompilerParams(vmem_limit_bytes=VMEM_LIMIT),
        name="recur_back",
    )(g_mix, branch, states, states, u, u, conv_low, recall, ingate, start_state, start_conv, conv, gate_w, decay)


def input_back_kernel(n, g_recur, g_branch, w_in, w_br, tokens, g_residual, gain, input_grad, g_gain, *bufs):
    g = Place(n)

    def partial(t, cols):
        return dot_nt(g_recur[t], w_in[cols]) + dot_nt(g_branch[t], w_br[cols])

    scatter = Scatter(g, partial, tile_of(tokens.shape[1], 512), bufs)
    g.greet()
    scatter.offers(g.nz - 1)

    def around(i):
        d = g.nz - 1 - i
        scatter.offers(d - 1)
        scatter.step(d)

    loop(g.nz - 1, around)
    scatter.last()
    part = 32
    g_gain[...] = jnp.zeros_like(g_gain)

    def rows_of(i):
        at = span(i, part)
        back, terms = norm_grad(tokens[at].astype(F32), gain[...].astype(F32), scatter.acc[at])
        input_grad[at] = g_residual[at] + back
        g_gain[...] += jnp.sum(terms, axis=0, keepdims=True)

    loop(tokens.shape[0] // part, rows_of)
    scatter.finish()


def input_back(n, g_recur, g_branch, w_in, w_br, tokens, g_residual, gain):
    rows, width = tokens.shape
    return pl.pallas_call(
        functools.partial(input_back_kernel, n),
        out_shape=(shape(rows, width), shape(1, width)),
        in_specs=[VM] * 7,
        out_specs=(VM,) * 2,
        scratch_shapes=Scatter.scratch(n, rows, width),
        compiler_params=comm_params(6),
        cost_estimate=cost(4 * n * rows * width * w_in.shape[1]),
        name="input_back",
    )(g_recur, g_branch, w_in, w_br, tokens, g_residual, gain)


def after(first, *rest):
    return lax.optimization_barrier((first, *rest))[1:]


def body(
    n,
    tokens,
    cotangent,
    resets,
    init_state,
    init_conv,
    norm_gain,
    w_input,
    w_branch,
    conv_params,
    gate_weights,
    gate_bias,
    decay_rate,
    w_output,
    mlp_gain,
    w_gelu,
    w_linear,
    w_down,
):
    rows, width = tokens.shape
    total = rows * n
    channels = w_input.shape[1]
    blocks, block = gate_weights.shape[1], gate_weights.shape[2]
    survive = (1 - resets).astype(F32)
    start_state = (init_state * survive[:, None])[:, None]
    start_conv = init_conv * survive[:, None, None]
    gain_first, gain_second = norm_gain[None], mlp_gain[None]
    gate_w = (gate_weights[:, :, :, None] * jnp.eye(blocks, dtype=BF16)[None, :, None, :, None]).reshape(
        2, channels, channels
    )
    decay = decay_rate[None]

    def flat(x):
        return x.reshape(total, x.shape[-1])

    def blocked(x):
        return x.reshape(n, rows, x.shape[-1])

    normed, recur, branch = project(n, tokens, gain_first, w_input, w_branch)
    recur, branch = flat(recur), flat(branch)
    states, mixture, conv_low, recall, ingate, final_state, final_conv = recur_forward(
        recur, branch, start_state, start_conv, conv_params, gate_w, gate_bias, decay
    )
    mixture = blocked(mixture)
    cot_full, residual, normed_mlp = mixer_out(n, mixture, w_output, cotangent, tokens, gain_second)
    hidden, g_first, g_second, grad_gelu, grad_linear, grad_down = mlp(
        n, normed_mlp, cot_full, w_gelu, w_linear, w_down
    )
    mlp_sums = lax.psum((grad_gelu, grad_linear, grad_down), "dp")
    g_residual, g_low, gain_second_grad = mlp_back(
        n, g_first, g_second, w_gelu, w_linear, residual, cotangent, gain_second
    )
    output, g_mixture, grad_output = down(n, hidden, w_down, residual, g_low, w_output, mixture)
    g_recur, g_branch, small, g_gates = recur_back(
        flat(g_mixture), branch, states, recur, conv_low, recall, ingate, start_state, start_conv,
        conv_params, gate_w, decay,
    )
    whole = normed.reshape(total, width)
    grad_input = dot_tn(whole, g_recur).astype(BF16)
    grad_branch = dot_tn(whole, g_branch).astype(BF16)
    gates = g_gates.reshape(2, blocks, block, blocks, block)
    gates = jnp.stack([gates[:, i, :, i] for i in range(blocks)], axis=1)
    late = (grad_output, grad_input, grad_branch, gates.astype(BF16), small.astype(BF16))
    mlp_sums, late = lax.optimization_barrier((mlp_sums, late))
    late_sums = lax.psum(late, "dp")
    input_grad, gain_first_grad = input_back(
        n, blocked(g_recur), blocked(g_branch), w_input, w_branch, tokens, g_residual, gain_first
    )
    gains = jnp.concatenate([gain_first_grad, gain_second_grad], axis=0)
    gains = lax.psum_scatter(gains, "tensor", scatter_dimension=1, tiled=True)
    gains = lax.psum(gains, "dp")
    grad_gelu, grad_linear, grad_down = (x.astype(F32) for x in mlp_sums)
    grad_output, grad_input, grad_branch, gates, small = (x.astype(F32) for x in late_sums)
    return (
        output,
        input_grad,
        final_state[:, 0],
        final_conv,
        gains[0],
        grad_input,
        grad_branch,
        small[:5],
        gates,
        small[5:7],
        small[7],
        grad_output,
        gains[1],
        grad_gelu,
        grad_linear,
        grad_down,
    )


def solution(mesh):
    in_specs = (
        P(("dp", "tensor"), None),
        P(("dp", "tensor"), None),
        P("dp"),
        P("dp", "tensor"),
        P("dp", None, "tensor"),
        P(),
        P(None, "tensor"),
        P(None, "tensor"),
        P(None, "tensor"),
        P(None, "tensor", None, None),
        P(None, "tensor"),
        P("tensor"),
        P("tensor", None),
        P(),
        P(None, "tensor"),
        P(None, "tensor"),
        P("tensor", None),
    )
    out_specs = (
        P(("dp", "tensor"), None),
        P(("dp", "tensor"), None),
        P("dp", "tensor"),
        P("dp", None, "tensor"),
        P("tensor"),
        P(None, "tensor"),
        P(None, "tensor"),
        P(None, "tensor"),
        P(None, "tensor", None, None),
        P(None, "tensor"),
        P("tensor"),
        P("tensor", None),
        P("tensor"),
        P(None, "tensor"),
        P(None, "tensor"),
        P("tensor", None),
    )
    return jax.shard_map(
        functools.partial(body, mesh.shape["tensor"]),
        mesh=mesh,
        in_specs=in_specs,
        out_specs=out_specs,
        check_vma=False,
    )
```

time: 1690 us -> 830 us (0.49); the launches traced: 1660 us -> 828 us
  waiting for transfers between devices: 750 us -> 78 us
  Pallas kernels: 0 us -> 655 us
  local copies, waits for them, and re-layouts: 508 us -> 22.1 us
  other arithmetic: 182 us -> 22.4 us
  matrix products: 166 us -> 15.5 us
  blocking collectives: 36.2 us -> 18.6 us
    pallas_call x0 -> x8, Pallas kernels: none -> 655 us  [the longest x1 116 us: mlp_back(): pl.pallas_call(functools.partial(mlp_back_kernel, n), out_shape=(shape(ro...]
    slice x133 -> x5, local copies, waits for them, and re-layouts: 334 us -> 2.97 us  [the longest x1 0.62 us: body(): gates = jnp.stack([gates[:, i, :, i] for i in range(blocks)], axis=1)]
    reduce_scatter x4 -> x0, waiting for transfers between devices: 295 us -> none  [the longest x1 88 us: body(): lax.psum_scatter(jnp.einsum('nf,df->nd', g_ups, w_ups, preferred_element_...]
    all_gather x4 -> x0, waiting for transfers between devices: 213 us -> none  [the longest x1 76.4 us: body(): lax.all_gather(normed_low, 'tensor', axis=0, tiled=True)]
    psum x1 -> x2, waiting for transfers between devices: 240 us -> 69.1 us  [the longest x1 69.1 us: body(): late_sums = lax.psum(late, 'dp')]
    dot_general x15 -> x2, matrix products: 166 us -> 15.5 us  [dot_tn(): lax.dot_general(a, b, (((0,), (0,)), ((), ())), preferred_element_type=F32)]
    add x42 -> x0, other arithmetic: 60.8 us -> none  [the longest x12 20.5 us: body(): scanned = lax.associative_scan(combine, (decay_step, seeded), axis=1)]
    pad x36 -> x0, local copies, waits for them, and re-layouts: 59.4 us -> none  [the longest x18 29.7 us: body(): scanned = lax.associative_scan(combine, (decay_step, seeded), axis=1)]
  transfers between devices with their start and end apart: 9 -> 3, of which waited for: 8 -> 2; matrix products, arithmetic and copies ran while one was open for 11% -> 4% of each run, Pallas kernels for 0% -> 41%
where the time goes in v1:
time: 830 us; the launch traced here: 828 us
  Pallas kernels  655 us (79%)
  waiting for transfers between devices  78 us (9%)
  other arithmetic  22.4 us (3%)
  local copies, waits for them, and re-layouts  22.1 us (3%)
  blocking collectives  18.6 us (2%)
  between operations  15.7 us (2%)
  matrix products  15.5 us (2%)
    pallas_call x1, Pallas kernels, mlp_back(): pl.pallas_call(functools.partial(mlp_back_kernel, n), out_shape=(shape(ro...  116 us
    pallas_call x1, Pallas kernels, mlp(): pl.pallas_call(functools.partial(mlp_kernel, n), out_shape=(shape(n, rows...  114 us
    pallas_call x1, Pallas kernels, mixer_out(): pl.pallas_call(functools.partial(mixer_out_kernel, n), out_shape=(shape(n...  108 us
    pallas_call x1, Pallas kernels, down(): pl.pallas_call(functools.partial(down_kernel, n), out_shape=(shape(rows,...  108 us
    pallas_call x1, Pallas kernels, input_back(): pl.pallas_call(functools.partial(input_back_kernel, n), out_shape=(shape(...  89.3 us
    pallas_call x1, Pallas kernels, project(): pl.pallas_call(functools.partial(project_kernel, n), out_shape=(shape(n,...  72.4 us
    psum x1, waiting for transfers between devices, body(): late_sums = lax.psum(late, 'dp')  69.1 us
    pallas_call x1, Pallas kernels, recur_back(): pl.pallas_call(recur_back_kernel, grid=(sequences, chunks), out_shape=(sh...  28.7 us
  transfers between devices with their start and end apart: 3, of which 2 were waited for; matrix products, arithmetic and copies ran while one was open for 4% of the time, Pallas kernels for 41%

profile of v1, /device:TPU:8, one launch (start us, length us, event | category | flops | bytes accessed | tf_op | source)
XLA Modules:
  0.0 827.6 jit_solution(10935297771364755621)
XLA Ops:
  14.0 1.4 copy_multiply_fusion.start_conv
  18.3 1.6 copy.52.w_in
  19.9 1.6 copy.53.w_br
  22.4 72.4 %project.1 = (bf16[8,2,128,2048]{3,2,1,0:T(8,128)(2,1)}, f32[8,256,344]{2,1,0:T(8,128)}, f32[8,256,344]{2,1,0:T(8,128)}) custom-call(bf16[256,2048]{1,0:T(8,128)(2,1)} %tokens.5, bf16[1,2048]{1,0:T(2,128)(2,1)} %broadcast_in_dim.16.gain, bf16[2048,344]{1,0:T(8,128)(2,1)} %copy.52.w_in, bf16[2048,344]{1,0:T(8,128)(2,1)} %copy.53.w_br), custom_call_target="tpu_custom_call" | custom-call | flops 5771362304 | bytes 200000000 | tf_op jit(solution)/shard_map/project/pallas_call | solution.py:378
  94.7 19.4 %recur_forward.1 = (f32[2048,344]{1,0:T(8,128)}, bf16[2048,344]{1,0:T(8,128)(2,1)}, bf16[2048,344]{1,0:T(8,128)(2,1)}, f32[2048,344]{1,0:T(8,128)}, f32[2048,344...) custom-call(f32[2048,344]{1,0:T(8,128)} %bitcast.22, f32[2048,344]{1,0:T(8,128)} %bitcast.25, ...), custom_call_target="tpu_custom_call" | custom-call | tf_op jit(solution)/shard_map/recur_forward/pallas_call | solution.py:480
  114.1 107.7 %mixer_out.1 = (bf16[8,2,128,2048]{3,2,1,0:T(8,128)(2,1)}, f32[256,2048]{1,0:T(8,128)}, bf16[256,2048]{1,0:T(8,128)(2,1)}) custom-call(bf16[8,256,344]{2,1,0:T(8,128)(2,1)} %bitcast.33, bf16[344,2048]{1,0:T(8,128)(2,1)} %w_output.3, bf16[256,2048]{1,0:T(8,128)(2,1)} %cotangent.3, bf16[256,2048]{1,0:T(8,128)(2,1)} %tokens.5, ...), custom_call_target="tpu_custom_call" | custom-call | flops 2885681152 | bytes 200000000 | tf_op jit(solution)/shard_map/mixer_out/pallas_call | solution.py:562
  221.9 113.6 %mlp.1 = (bf16[8,256,768]{2,1,0:T(8,128)(2,1)}, bf16[8,256,768]{2,1,0:T(8,128)(2,1)}, bf16[8,256,768]{2,1,0:T(8,128)(2,1)}, bf16[2048,768]{1,0:T(8,128)(2,1)}, b...) custom-call(bf16[256,2048]{1,0:T(8,128)(2,1)} %get-tuple-element.58.normed, ...), custom_call_target="tpu_custom_call" | custom-call | flops 38654705664 | bytes 200000000 | tf_op jit(solution)/shard_map/mlp/pallas_call | solution.py:673
  335.6 116.4 %mlp_back.1 = (f32[256,2048]{1,0:T(8,128)}, bf16[256,2048]{1,0:T(8,128)(2,1)}, f32[1,2048]{1,0:T(1,128)}) custom-call(bf16[8,256,768]{2,1,0:T(8,128)(2,1)} %get-tuple-element.62.g_first, bf16[8,256,768]{2,1,0:T(8,128)(2,1)} %get-tuple-element.63.g_second, bf16[2048,768]{1,0:T(8,128)(2,1)} %w_gelu.3, bf16[2048,768]{1,0:T(8,128)(2,1)} %w_linear.3, ...), custom_call_target="tpu_custom_call" | custom-call | flops 12884901888 | bytes 200000000 | tf_op jit(solution)/shard_map/mlp_back/pallas_call | solution.py:728
  452.0 107.6 %down.1 = (bf16[256,2048]{1,0:T(8,128)(2,1)}, f32[8,256,344]{2,1,0:T(8,128)}, bf16[344,2048]{1,0:T(8,128)(2,1)}) custom-call(bf16[8,256,768]{2,1,0:T(8,128)(2,1)} %get-tuple-element.60.hidden, bf16[768,2048]{1,0:T(8,128)(2,1)} %w_down.3, f32[256,2048]{1,0:T(8,128)} %get-tuple-element.61.residual, bf16[256,2048]{1,0:T(8,128)(2,1)} %get-tuple-element.64.g_low, ...), custom_call_target="tpu_custom_call" | custom-call | flops 12213813248 | bytes 200000000 | tf_op jit(solution)/shard_map/down/pallas_call | solution.py:790
  559.6 28.7 %recur_back.1 = (bf16[2048,344]{1,0:T(8,128)(2,1)}, bf16[2048,344]{1,0:T(8,128)(2,1)}, f32[8,344]{1,0:T(8,128)}, f32[2,344,344]{2,1,0:T(8,128)}) custom-call(f32[2048,344]{1,0:T(8,128)} %bitcast.28, f32[2048,344]{1,0:T(8,128)} %bitcast.26, f32[2048,344]{1,0:T(8,128)} %get-tuple-element.67.states.states_before, ...), custom_call_target="tpu_custom_call" | custom-call | tf_op jit(solution)/shard_map/recur_back/pallas_call | solution.py:949
  588.4 89.3 %input_back.1 = (f32[256,2048]{1,0:T(8,128)}, f32[1,2048]{1,0:T(1,128)}) custom-call(bf16[8,256,344]{2,1,0:T(8,128)(2,1)} %bitcast.36, bf16[8,256,344]{2,1,0:T(8,128)(2,1)} %bitcast.35, bf16[2048,344]{1,0:T(8,128)(2,1)} %copy.52.w_in, bf16[2048,344]{1,0:T(8,128)(2,1)} %copy.53.w_br, bf16[256,2048]{1,0:T(8,128)(2,1)} %tokens.5, ...), custom_call_target="tpu_custom_call" | custom-call | flops 5771362304 | bytes 200000000 | tf_op jit(solution)/shard_map/input_back/pallas_call | solution.py:1012
  679.8 7.7 convolution_convert_fusion.1
  687.6 7.8 convolution_convert_fusion
  698.4 8.8 %reduce-scatter.4.cloned.1.call-done = f32[256,2]{1,0:T(8,128)} async-done(((f32[2048,2]{1,0:T(8,128)}), f32[256,2]{1,0:T(8,128)}) %reduce-scatter.4.cloned.1.call-update) | async-done | bytes 2064
  708.2 9.9 %psum.63 = f32[2,256]{1,0:T(2,128)S(1)} all-reduce(f32[2,256]{1,0:T(2,128)S(1)} %copy.63), channel_id=1, replica_groups=mesh['dp'=4,'tensor'=8] {'dp'}, use_global_device_ids=true, to_apply=%region_1.0 | all-reduce | flops 512 | bytes 4096 | tf_op jit(solution)/shard_map/psum | solution.py:1099
  718.8 8.7 %psum.69 = bf16[8,344]{1,0:T(8,128)(2,1)S(1)} all-reduce(bf16[8,344]{1,0:T(8,128)(2,1)S(1)} %convert_element_type.48), channel_id=1, replica_groups=mesh['dp'=4,'tensor'=8] {'dp'}, use_global_device_ids=true, to_apply=%region_7.0 | all-reduce | flops 2752 | bytes 11008 | tf_op jit(solution)/shard_map/psum | solution.py:1093
  728.6 3.2 convert_element_type.54
  731.8 3.2 convert_element_type.55
  735.0 3.6 convert_element_type.56
  739.2 69.1 %all-reduce.5.cloned.1.call-done = (bf16[2,2,172,172]{3,2,0,1:T(8,128)(2,1)}, bf16[2048,344]{0,1:T(8,128)(2,1)}, bf16[2048,344]{0,1:T(8,128)(2,1)}, bf16[344,2048]{1,0:T(8,128)(2,1)}) async-done(((bf16[2,2,172,172]{3,2,0,1:T(8,128)(2,1)}, bf16[2048,344]{0,1:T(8,128)(2,1)}, bf16[2048,344]{0,1:T(8,128)(2,1)}, bf16[344,2048]{1,0:T(8,128)(2,1)}), (bf16[2,2,172,172]{3,2,0,1:T(8,128)(2,1)}, ...) | async-done | bytes 4463760 | tf_op jit(solution)/shard_map/psum | solution.py:1093
  808.3 2.3 copy.61
  810.6 3.2 convert_element_type.49
  813.9 1.9 convert_element_type.50
  815.8 1.9 convert_element_type.53
  (72 shorter events, 20.9 us)
Async XLA Ops:
  8.0 10.3 %copy-start.4 = (bf16[2048,344]{0,1:T(8,128)(2,1)S(1)}, bf16[2048,344]{0,1:T(8,128)(2,1)}, u32[]{:S(2)}) copy-start(bf16[2048,344]{0,1:T(8,128)(2,1)} %param.23) | copy-start | bytes 4227076
  8.0 689.2 %all-reduce.7.cloned.1.call-start = ((), (), s32[]{:S(2)}) async-start(), calls=%async_computation.3 | async-start | bytes 18874368 | tf_op jit(solution)/shard_map/psum | solution.py:1077
  18.3 1.6 copy-start.5
  19.9 1.6 copy-start.8
  335.5 371.7 %reduce-scatter.4.cloned.1.call-start = ((), (), s32[]{:S(2)}) async-start(), calls=%async_computation.1 | async-start | bytes 1179648
  588.4 89.3 %copy-start.13 = (f32[1,2048]{1,0:T(1,128)S(1)}, f32[1,2048]{1,0:T(1,128)}, u32[]{:S(2)}) copy-start(f32[1,2048]{1,0:T(1,128)} %get-tuple-element.78) | copy-start | bytes 24580
  588.4 91.4 %copy-start.16 = (bf16[2048,344]{1,0:T(8,128)(2,1)S(1)}, bf16[2048,344]{1,0:T(8,128)(2,1)}, u32[]{:S(2)}) copy-start(bf16[2048,344]{1,0:T(8,128)(2,1)} %get-tuple-element.71) | copy-start | bytes 4227076
  679.8 128.6 %all-reduce.5.cloned.1.call-start = ((), (), s32[]{:S(2)}) async-start(), calls=%async_computation.2 | async-start | bytes 9175040 | tf_op jit(solution)/shard_map/psum | solution.py:1093
  679.8 7.7 copy-start.15
  687.6 7.8 copy-start.9
  695.3 1.8 copy-start.11
  696.4 0.9 copy-start.14
  696.4 1.4 copy-start.12
  697.2 31.4 %copy-start.2 = (bf16[2048,768]{1,0:T(8,128)(2,1)S(1)}, bf16[2048,768]{1,0:T(8,128)(2,1)}, u32[]{:S(2)}) copy-start(bf16[2048,768]{1,0:T(8,128)(2,1)} %get-tuple-element.91) | copy-start | bytes 9437188
  728.6 3.2 copy-start.1
  731.8 3.2 copy-start
  808.3 5.6 copy-start.7
  813.9 1.9 copy-start.6
  815.8 1.9 copy-start.10
  815.8 3.1 copy-start.3
Sparse Core Ops, SparseCore 0:
  335.7 211.7 all-reduce.6
  697.3 110.9 all-reduce.4
Sparse Core Ops, SparseCore 1:
  679.8 27.4 reduce-scatter.3

commit v2 on v1

--- a/solution.py
+++ b/solution.py
@@ -87,24 +87,20 @@
 class Gather:
     def __init__(self, place, full, sent, came):
         self.place, self.full, self.sent, self.came = place, full, sent, came
-        self.pieces = full.shape[1]
+        self.pieces = came.shape[1]
+        self.size = full.shape[1] // self.pieces
 
     @staticmethod
     def scratch(n, rows, width):
         return [
-            pltpu.VMEM((n, PIECES, rows // PIECES, width), BF16),
+            pltpu.VMEM((n, rows, width), BF16),
             pltpu.SemaphoreType.DMA((n, PIECES, 3)),
             pltpu.SemaphoreType.DMA((n, PIECES)),
         ]
 
     def copy(self, t, p, way, to):
-        return self.place.copy(
-            self.full.at[t, p],
-            self.full.at[t, p],
-            self.sent.at[t, p, way],
-            self.came.at[t, p],
-            to,
-        )
+        piece = self.full.at[t, pl.ds(p * self.size, self.size)]
+        return self.place.copy(piece, piece, self.sent.at[t, p, way], self.came.at[t, p], to)
 
     def start(self):
         g = self.place
@@ -339,19 +335,21 @@
 def project_kernel(n, tokens, gain, w_in, w_br, normed, recur, branch, full, sent, came, held_a, held_b, saved):
     g = Place(n)
     gather = Gather(g, full, sent, came)
-    size = full.shape[2]
-    for p in range(PIECES):
-        values = tokens[p * size : (p + 1) * size].astype(F32)
-        full[g.t, p] = (values * inv_rms(values) * gain[...].astype(F32)).astype(BF16)
+    part = 64
+
+    def normalize(i):
+        at = span(i, part)
+        values = tokens[at].astype(F32)
+        full[g.t, at] = (values * inv_rms(values) * gain[...].astype(F32)).astype(BF16)
+
+    loop(full.shape[1] // part, normalize)
     g.greet()
     gather.start()
 
     def use(t):
         pltpu.make_async_copy(full.at[t], normed.at[t], saved.at[t, 0]).start()
-        for p in range(PIECES):
-            rows = slice(p * size, (p + 1) * size)
-            held_a[t, rows] = dot(full[t, p], w_in[...])
-            held_b[t, rows] = dot(full[t, p], w_br[...])
+        held_a[t] = dot_nt(full[t], w_in[...])
+        held_b[t] = dot_nt(full[t], w_br[...])
         pltpu.make_async_copy(held_a.at[t], recur.at[t], saved.at[t, 1]).start()
         pltpu.make_async_copy(held_b.at[t], branch.at[t], saved.at[t, 2]).start()
 
@@ -374,11 +372,11 @@
 
 def project(n, tokens, gain, w_in, w_br):
     rows, width = tokens.shape
-    channels = w_in.shape[1]
+    channels = w_in.shape[0]
     return pl.pallas_call(
         functools.partial(project_kernel, n),
         out_shape=(
-            shape(n, PIECES, rows // PIECES, width, dtype=BF16),
+            shape(n, rows, width, dtype=BF16),
             shape(n, rows, channels),
             shape(n, rows, channels),
         ),
@@ -522,9 +520,7 @@
     g = Place(n)
     gather = Gather(g, full, sent, came)
     scatter = Scatter(g, lambda t, cols: dot(mixture[t], w_output[:, cols]), tile_of(residual.shape[1], 512), bufs)
-    size = full.shape[2]
-    for p in range(PIECES):
-        full[g.t, p] = cotangent[p * size : (p + 1) * size]
+    full[g.t] = cotangent[...]
     g.greet()
 
     def use(t):
@@ -562,7 +558,7 @@
     return pl.pallas_call(
         functools.partial(mixer_out_kernel, n),
         out_shape=(
-            shape(n, PIECES, rows // PIECES, width, dtype=BF16),
+            shape(n, rows, width, dtype=BF16),
             shape(rows, width),
             shape(rows, width, dtype=BF16),
         ),
@@ -583,55 +579,48 @@
 ):
     g = Place(n)
     gather = Gather(g, full, sent, came)
-    size = full.shape[2]
-    rows = PIECES * size
     columns = w_gelu.shape[1]
-    width = full.shape[3]
+    width = full.shape[2]
     tile = tile_of(columns, 256)
     wide = tile_of(width, 512)
-    for p in range(PIECES):
-        full[g.t, p] = normed[p * size : (p + 1) * size]
+    full[g.t] = normed[...]
+
+    def fetch(t):
+        return pltpu.make_async_copy(cot_full.at[t], cot.at[t], fetched.at[t])
+
+    loop(n, lambda t: fetch(t).start())
     g.greet()
     gather.start()
     acc_g[...] = jnp.zeros_like(acc_g)
     acc_l[...] = jnp.zeros_like(acc_l)
     acc_d[...] = jnp.zeros_like(acc_d)
 
-    def save(t, i, start):
+    def save(t, start):
         for q, (held, out) in enumerate(((keep_h, hidden), (keep_f, g_first), (keep_s, g_second))):
             copy = pltpu.make_async_copy(held.at[t], out.at[t], saved.at[t, q])
             copy.start() if start else copy.wait()
 
     def use(t):
-        fetch = pltpu.make_async_copy(cot_full.at[t], cot, fetched)
-        fetch.start()
-        fetch.wait()
-
-        def piece(p):
-            at = span(p, size)
-
-            def part(i):
-                cols = span(i, tile)
-                first = dot(full[t, p], w_gelu[:, cols])
-                second = dot(full[t, p], w_linear[:, cols])
-                back = dot_nt(cot[p], w_down[cols])
-                value, slope = gelu_parts(first)
-                keep_h[t, at, cols] = (value * second).astype(BF16)
-                keep_f[t, at, cols] = (back * second * slope).astype(BF16)
-                keep_s[t, at, cols] = (back * value).astype(BF16)
-
-            loop(columns // tile, part)
-
-        loop(PIECES, piece)
-        save(t, 0, True)
+        fetch(t).wait()
+
+        def part(i):
+            cols = span(i, tile)
+            first = dot(full[t], w_gelu[:, cols])
+            second = dot(full[t], w_linear[:, cols])
+            back = dot_nt(cot[t], w_down[cols])
+            value, slope = gelu_parts(first)
+            keep_h[t, :, cols] = (value * second).astype(BF16)
+            keep_f[t, :, cols] = (back * second * slope).astype(BF16)
+            keep_s[t, :, cols] = (back * value).astype(BF16)
+
+        loop(columns // tile, part)
+        save(t, True)
 
         def part(i):
             at = span(i, wide)
-            for p in range(PIECES):
-                rows_p = slice(p * size, (p + 1) * size)
-                acc_g[at] += dot_tn(full[t, p, :, at], keep_f[t, rows_p])
-                acc_l[at] += dot_tn(full[t, p, :, at], keep_s[t, rows_p])
-                acc_d[:, at] += dot_tn(keep_h[t, rows_p], cot[p, :, at])
+            acc_g[at] += dot_tn(full[t, :, at], keep_f[t])
+            acc_l[at] += dot_tn(full[t, :, at], keep_s[t])
+            acc_d[:, at] += dot_tn(keep_h[t], cot[t, :, at])
 
         loop(width // wide, part)
 
@@ -642,7 +631,7 @@
         gather.each(i + 1, use)
 
     loop(g.nz - 1, away)
-    loop(n, lambda t: save(t, 0, False))
+    loop(n, lambda t: save(t, False))
     gather.finish()
 
     def drain(acc, stage, out, sem):
@@ -678,13 +667,13 @@
         in_specs=[VM, ANY, VM, VM, VM],
         out_specs=(ANY,) * 6,
         scratch_shapes=Gather.scratch(n, rows, width)
-        + [pltpu.VMEM((PIECES, rows // PIECES, width), BF16)]
+        + [pltpu.VMEM((n, rows, width), BF16)]
         + [kept] * 3
         + [pltpu.VMEM((width, columns), F32)] * 2
         + [pltpu.VMEM((columns, width), F32)]
-        + [pltpu.VMEM((2, tile_of(width, 256), columns), BF16)]
-        + [pltpu.VMEM((2, tile_of(columns, 128), width), BF16)]
-        + [pltpu.SemaphoreType.DMA((n, 3)), pltpu.SemaphoreType.DMA, pltpu.SemaphoreType.DMA((2,))],
+        + [pltpu.VMEM((2, tile_of(width, 128), columns), BF16)]
+        + [pltpu.VMEM((2, tile_of(columns, 64), width), BF16)]
+        + [pltpu.SemaphoreType.DMA((n, 3)), pltpu.SemaphoreType.DMA((n,)), pltpu.SemaphoreType.DMA((2,))],
         compiler_params=comm_params(3),
         cost_estimate=cost(12 * n * rows * width * columns),
         name="mlp",
@@ -746,21 +735,15 @@
     width = residual.shape[1]
     wide = tile_of(width, 512)
     scatter = Scatter(g, lambda t, cols: dot(hidden[t], w_down[:, cols]), wide, bufs)
-    size = full.shape[2]
-    for p in range(PIECES):
-        full[g.t, p] = g_low[p * size : (p + 1) * size]
+    full[g.t] = g_low[...]
     g.greet()
 
     def use(t):
-        for p in range(PIECES):
-            rows = slice(p * size, (p + 1) * size)
-            g_mixture[t, rows] = dot_nt(full[t, p], w_output[...])
+        g_mixture[t] = dot_nt(full[t], w_output[...])
 
         def part(i):
             at = span(i, wide)
-            for p in range(PIECES):
-                rows = slice(p * size, (p + 1) * size)
-                acc_o[:, at] += dot_tn(mixture[t, rows], full[t, p, :, at])
+            acc_o[:, at] += dot_tn(mixture[t], full[t, :, at])
 
         loop(width // wide, part)
 
@@ -977,14 +960,108 @@
     )(g_mix, branch, states, states, u, u, conv_low, recall, ingate, start_state, start_conv, conv, gate_w, decay)
 
 
-def input_back_kernel(n, g_recur, g_branch, w_in, w_br, tokens, g_residual, gain, input_grad, g_gain, *bufs):
+class Spread:
+    def __init__(self, me, count, part, landed, summed, sems):
+        self.me, self.count, self.part, self.landed, self.summed = me, count, part, landed, summed
+        self.out_send, self.out_recv, self.back_send, self.back_recv = sems
+
+    def others(self, act):
+        loop(self.count, lambda i: pl.when(i != self.me)(lambda: act(i)))
+
+    def out(self, i, slot):
+        return pltpu.make_async_remote_copy(
+            src_ref=self.part(i),
+            dst_ref=self.landed.at[slot],
+            send_sem=self.out_send.at[i],
+            recv_sem=self.out_recv.at[slot],
+            device_id={"dp": i},
+            device_id_type=MESH,
+        )
+
+    def back(self, i, slot):
+        return pltpu.make_async_remote_copy(
+            src_ref=self.summed.at[slot],
+            dst_ref=self.summed.at[slot],
+            send_sem=self.back_send.at[i],
+            recv_sem=self.back_recv.at[slot],
+            device_id={"dp": i},
+            device_id_type=MESH,
+        )
+
+    def start(self):
+        self.others(lambda i: self.out(i, self.me).start())
+        self.landed[self.me] = self.part(self.me)[...]
+
+    def turn(self):
+        self.others(lambda i: self.out(i, i).wait_recv())
+        rows = self.landed.shape[1]
+        tile = tile_of(rows, 32)
+
+        def add(r):
+            at = span(r, tile)
+            value = self.landed[0, at].astype(F32)
+            for i in range(1, self.count):
+                value = value + self.landed[i, at].astype(F32)
+            self.summed[self.me, at] = value.astype(BF16)
+
+        loop(rows // tile, add)
+        self.others(lambda i: self.back(i, self.me).start())
+
+    def finish(self):
+        self.others(lambda i: self.back(i, i).wait_recv())
+        self.others(lambda i: self.out(i, i).wait_send())
+        self.others(lambda i: self.back(i, self.me).wait_send())
+
+
+def input_back_kernel(
+    n, copies, g_recur, g_branch, w_in, w_br, normed, tokens, g_residual, gain, second_gain, g_gates, small,
+    input_grad, pair_out, rest_out, gains_out,
+    pair, pair_in, pair_all, rest, rest_in, rest_all, gain_row, gain_parts, gain_in, gain_sum, gain_dp,
+    pair_sems, rest_sems, gain_sent, gain_came, gain_dp_sent, gain_dp_came, *bufs
+):
     g = Place(n)
+    me = lax.axis_index("dp")
+    rows, width = tokens.shape
+    channels = w_in.shape[0]
+    part_width = width // copies
+    padded = pair.shape[1] // 2
+    gain_width = width // n
+
+    def block(ref, t):
+        return ref[span(t, rows)]
 
     def partial(t, cols):
-        return dot_nt(g_recur[t], w_in[cols]) + dot_nt(g_branch[t], w_br[cols])
-
-    scatter = Scatter(g, partial, tile_of(tokens.shape[1], 512), bufs)
-    g.greet()
+        return dot(block(g_recur, t), w_in[:, cols]) + dot(block(g_branch, t), w_br[:, cols])
+
+    scatter = Scatter(g, partial, tile_of(width, 512), bufs)
+    pairs = Spread(me, copies, lambda i: pair.at[i], pair_in, pair_all, [pair_sems.at[q] for q in range(4)])
+    rests = Spread(me, copies, lambda i: rest.at[i], rest_in, rest_all, [rest_sems.at[q] for q in range(4)])
+
+    def gain_copy(t, slot):
+        return g.copy(gain_parts.at[t], gain_in.at[slot], gain_sent.at[t], gain_came.at[slot], t)
+
+    def gain_dp_copy(i, slot):
+        return pltpu.make_async_remote_copy(
+            src_ref=gain_sum,
+            dst_ref=gain_dp.at[slot],
+            send_sem=gain_dp_sent.at[i],
+            recv_sem=gain_dp_came.at[slot],
+            device_id={"dp": i},
+            device_id_type=MESH,
+        )
+
+    def others(act):
+        loop(n, lambda t: pl.when(t != g.t)(lambda: act(t)))
+
+    barrier = pltpu.get_barrier_semaphore()
+    others(
+        lambda t: pl.semaphore_signal(barrier, inc=1, device_id={"tensor": t}, device_id_type=MESH)
+    )
+    pairs.others(
+        lambda i: pl.semaphore_signal(barrier, inc=1, device_id={"dp": i}, device_id_type=MESH)
+    )
+    pl.semaphore_wait(barrier, n - 1 + copies - 1)
+
     scatter.offers(g.nz - 1)
 
     def around(i):
@@ -992,41 +1069,121 @@
         scatter.offers(d - 1)
         scatter.step(d)
 
-    loop(g.nz - 1, around)
+    pair[...] = jnp.zeros_like(pair)
+
+    def weigh(q):
+        cols = span(q, part_width)
+        first = dot_tn(g_recur[...], normed[:, cols])
+        pair[q, 0:channels] = first.astype(BF16)
+        terms = jnp.sum(w_in[:, cols].astype(F32) * first, axis=0, keepdims=True)
+        second = dot_tn(g_branch[...], normed[:, cols])
+        pair[q, padded : padded + channels] = second.astype(BF16)
+        terms += jnp.sum(w_br[:, cols].astype(F32) * second, axis=0, keepdims=True)
+        gain_row[0:1, cols] = terms / gain[0:1, cols].astype(F32)
+
+    loop(copies, weigh)
+    pairs.start()
+    gain_row[1:2] = second_gain[...]
+    for t in range(n):
+        gain_parts[t] = gain_row[:, t * gain_width : (t + 1) * gain_width]
+    others(lambda t: gain_copy(t, g.t).start())
+    gain_in[g.t] = gain_parts[g.t]
+
+    flat = jnp.concatenate(
+        [
+            g_gates[0],
+            g_gates[1],
+            small[...],
+            jnp.zeros((copies * rest.shape[1] - 2 * channels - 8, channels), F32),
+        ],
+        axis=0,
+    ).astype(BF16)
+    for i in range(copies):
+        rest[i] = flat[i * rest.shape[1] : (i + 1) * rest.shape[1]]
+    rests.start()
+
+    loop(g.nz - 2, around)
+
+    others(lambda t: gain_copy(t, t).wait_recv())
+    total = gain_in[0]
+    for t in range(1, n):
+        total = total + gain_in[t]
+    gain_sum[...] = total
+    pairs.others(lambda i: gain_dp_copy(i, me).start())
+    gain_dp[me] = total
+    pairs.turn()
+    rests.turn()
+
+    around(g.nz - 2)
     scatter.last()
     part = 32
-    g_gain[...] = jnp.zeros_like(g_gain)
 
     def rows_of(i):
         at = span(i, part)
-        back, terms = norm_grad(tokens[at].astype(F32), gain[...].astype(F32), scatter.acc[at])
+        back, _ = norm_grad(tokens[at].astype(F32), gain[...].astype(F32), scatter.acc[at])
         input_grad[at] = g_residual[at] + back
-        g_gain[...] += jnp.sum(terms, axis=0, keepdims=True)
-
-    loop(tokens.shape[0] // part, rows_of)
+
+    loop(rows // part, rows_of)
+    pairs.others(lambda i: gain_dp_copy(i, i).wait_recv())
+    total = gain_dp[0]
+    for i in range(1, copies):
+        total = total + gain_dp[i]
+    gains_out[...] = total
+    pairs.finish()
+    rests.finish()
+    pair_out[...] = pair_all[...]
+    rest_out[...] = rest_all[...]
+    others(lambda t: gain_copy(t, t).wait_send())
+    pairs.others(lambda i: gain_dp_copy(i, i).wait_send())
     scatter.finish()
 
 
-def input_back(n, g_recur, g_branch, w_in, w_br, tokens, g_residual, gain):
+def up_to(extent, multiple):
+    return (extent + multiple - 1) // multiple * multiple
+
+
+def input_back(n, copies, g_recur, g_branch, w_in, w_br, normed, tokens, g_residual, gain, second_gain, g_gates, small):
     rows, width = tokens.shape
+    channels = w_in.shape[0]
+    pair_shape = (copies, 2 * up_to(channels, 16), width // copies)
+    rest_shape = (copies, up_to(2 * channels + 8, 16 * copies) // copies, channels)
+    gain_shape = (8, width // n)
+    sems = pltpu.SemaphoreType.DMA
     return pl.pallas_call(
-        functools.partial(input_back_kernel, n),
-        out_shape=(shape(rows, width), shape(1, width)),
-        in_specs=[VM] * 7,
-        out_specs=(VM,) * 2,
-        scratch_shapes=Scatter.scratch(n, rows, width),
+        functools.partial(input_back_kernel, n, copies),
+        out_shape=(
+            shape(rows, width),
+            shape(*pair_shape, dtype=BF16),
+            shape(*rest_shape, dtype=BF16),
+            shape(*gain_shape),
+        ),
+        in_specs=[VM] * 11,
+        out_specs=(VM,) * 4,
+        scratch_shapes=[pltpu.VMEM(pair_shape, BF16)] * 3
+        + [pltpu.VMEM(rest_shape, BF16)] * 3
+        + [
+            pltpu.VMEM((8, width), F32),
+            pltpu.VMEM((n, *gain_shape), F32),
+            pltpu.VMEM((n, *gain_shape), F32),
+            pltpu.VMEM(gain_shape, F32),
+            pltpu.VMEM((copies, *gain_shape), F32),
+            sems((4, copies)),
+            sems((4, copies)),
+            sems((n,)),
+            sems((n,)),
+            sems((copies,)),
+            sems((copies,)),
+        ]
+        + Scatter.scratch(n, rows, width),
         compiler_params=comm_params(6),
-        cost_estimate=cost(4 * n * rows * width * w_in.shape[1]),
+        cost_estimate=cost(8 * n * rows * width * channels),
         name="input_back",
-    )(g_recur, g_branch, w_in, w_br, tokens, g_residual, gain)
-
-
-def after(first, *rest):
-    return lax.optimization_barrier((first, *rest))[1:]
+    )(g_recur, g_branch, w_in, w_br, normed, tokens, g_residual, gain, second_gain, g_gates, small)
 
 
 def body(
     n,
+    copies,
     tokens,
     cotangent,
     resets,
@@ -1057,6 +1214,7 @@
         2, channels, channels
     )
     decay = decay_rate[None]
+    w_in, w_br = w_input.T, w_branch.T
 
     def flat(x):
         return x.reshape(total, x.shape[-1])
@@ -1064,7 +1222,7 @@
     def blocked(x):
         return x.reshape(n, rows, x.shape[-1])
 
-    normed, recur, branch = project(n, tokens, gain_first, w_input, w_branch)
+    normed, recur, branch = project(n, tokens, gain_first, w_in, w_br)
     recur, branch = flat(recur), flat(branch)
     states, mixture, conv_low, recall, ingate, final_state, final_conv = recur_forward(
         recur, branch, start_state, start_conv, conv_params, gate_w, gate_bias, decay
@@ -1083,30 +1241,31 @@
         flat(g_mixture), branch, states, recur, conv_low, recall, ingate, start_state, start_conv,
         conv_params, gate_w, decay,
     )
-    whole = normed.reshape(total, width)
-    grad_input = dot_tn(whole, g_recur).astype(BF16)
-    grad_branch = dot_tn(whole, g_branch).astype(BF16)
-    gates = g_gates.reshape(2, blocks, block, blocks, block)
+    mlp_sums, grad_output = lax.optimization_barrier((mlp_sums, grad_output))
+    output_sum = lax.psum(grad_output, "dp")
+    input_grad, pair, rest, gains = input_back(
+        n, copies, g_recur, g_branch, w_in, w_br, flat(normed), tokens, g_residual, gain_first,
+        gain_second_grad, g_gates, small,
+    )
+    padded = pair.shape[1] // 2
+
+    def whole(part):
+        return part[:, :channels].astype(F32).transpose(1, 0, 2).reshape(channels, width).T
+
+    rest = rest.astype(F32).reshape(-1, channels)
+    gates = rest[: 2 * channels].reshape(2, blocks, block, blocks, block)
     gates = jnp.stack([gates[:, i, :, i] for i in range(blocks)], axis=1)
-    late = (grad_output, grad_input, grad_branch, gates.astype(BF16), small.astype(BF16))
-    mlp_sums, late = lax.optimization_barrier((mlp_sums, late))
-    late_sums = lax.psum(late, "dp")
-    input_grad, gain_first_grad = input_back(
-        n, blocked(g_recur), blocked(g_branch), w_input, w_branch, tokens, g_residual, gain_first
-    )
-    gains = jnp.concatenate([gain_first_grad, gain_second_grad], axis=0)
-    gains = lax.psum_scatter(gains, "tensor", scatter_dimension=1, tiled=True)
-    gains = lax.psum(gains, "dp")
+    small = rest[2 * channels : 2 * channels + 8]
     grad_gelu, grad_linear, grad_down = (x.astype(F32) for x in mlp_sums)
-    grad_output, grad_input, grad_branch, gates, small = (x.astype(F32) for x in late_sums)
+    grad_output = output_sum.astype(F32)
     return (
         output,
         input_grad,
         final_state[:, 0],
         final_conv,
         gains[0],
-        grad_input,
-        grad_branch,
+        whole(pair[:, :padded]),
+        whole(pair[:, padded:]),
         small[:5],
         gates,
         small[5:7],
@@ -1158,7 +1317,7 @@
         P("tensor", None),
     )
     return jax.shard_map(
-        functools.partial(body, mesh.shape["tensor"]),
+        functools.partial(body, mesh.shape["tensor"], mesh.shape["dp"]),
         mesh=mesh,
         in_specs=in_specs,
         out_specs=out_specs,

time: 830 us -> 709 us (0.85)
  waiting for transfers between devices: 78 us -> 0.06 us
  blocking collectives: 18.6 us -> 0 us
  matrix products: 15.5 us -> 0 us
    psum x1, waiting for transfers between devices: 69.1 us -> 0.01 us  [body(): output_sum = lax.psum(grad_output, 'dp')]
    pallas_call x1, Pallas kernels: 89.3 us -> 112 us  [input_back(): pl.pallas_call(functools.partial(input_back_kernel, n, copies), out_shape...]
    psum x2 -> x0, blocking collectives: 18.6 us -> none  [the longest x1 9.95 us: body(): gains = lax.psum(gains, 'dp')]
    pallas_call x1, Pallas kernels: 114 us -> 95.2 us  [mlp(): pl.pallas_call(functools.partial(mlp_kernel, n), out_shape=(shape(n, rows...]
    dot_general x2 -> x0, matrix products: 15.5 us -> none  [dot_tn(): lax.dot_general(a, b, (((0,), (0,)), ((), ())), preferred_element_type=F32)]
    unnamed x4 -> x2, waiting for transfers between devices: 8.88 us -> 0.03 us
    pallas_call x1, Pallas kernels: 116 us -> 108 us  [mlp_back(): pl.pallas_call(functools.partial(mlp_back_kernel, n), out_shape=(shape(ro...]
  transfers between devices with their start and end apart: 3 -> 2, of which waited for: 2 -> 0; matrix products, arithmetic and copies ran while one was open for 4% -> 4% of each run, Pallas kernels for 41% -> 50%
where the time goes in v2:
time: 709 us; the launch traced here: 704 us
  Pallas kernels  648 us (91%)
  other arithmetic  22.3 us (3%)
  local copies, waits for them, and re-layouts  19 us (3%)
  between operations  14.2 us (2%)
    pallas_call x1, Pallas kernels, input_back(): pl.pallas_call(functools.partial(input_back_kernel, n, copies), out_shape...  112 us
    pallas_call x1, Pallas kernels, mlp_back(): pl.pallas_call(functools.partial(mlp_back_kernel, n), out_shape=(shape(ro...  108 us
    pallas_call x1, Pallas kernels, mixer_out(): pl.pallas_call(functools.partial(mixer_out_kernel, n), out_shape=(shape(n...  108 us
    pallas_call x1, Pallas kernels, down(): pl.pallas_call(functools.partial(down_kernel, n), out_shape=(shape(rows,...  105 us
    pallas_call x1, Pallas kernels, mlp(): pl.pallas_call(functools.partial(mlp_kernel, n), out_shape=(shape(n, rows...  95.2 us
    pallas_call x1, Pallas kernels, project(): pl.pallas_call(functools.partial(project_kernel, n), out_shape=(shape(n,...  72.5 us
    pallas_call x1, Pallas kernels, recur_back(): pl.pallas_call(recur_back_kernel, grid=(sequences, chunks), out_shape=(sh...  28.7 us
    pallas_call x1, Pallas kernels, recur_forward(): pl.pallas_call(recur_kernel, grid=(sequences, chunks), out_shape=(shape(t...  19.4 us
  transfers between devices with their start and end apart: 2, of which 0 were waited for; matrix products, arithmetic and copies ran while one was open for 4% of the time, Pallas kernels for 50%

profile of v2, /device:TPU:8, one launch (start us, length us, event | category | flops | bytes accessed | tf_op | source)
XLA Modules:
  0.0 704.0 jit_solution(1386562687493093217)
XLA Ops:
  7.9 1.2 broadcast_in_dim.18.decay
  10.5 1.3 broadcast_in_dim.16.gain
  11.8 1.3 broadcast_in_dim.19.gain
  13.1 1.4 copy_multiply_fusion.start_conv
  17.6 72.5 %project.1 = (bf16[8,256,2048]{2,1,0:T(8,128)(2,1)}, f32[8,256,344]{2,1,0:T(8,128)}, f32[8,256,344]{2,1,0:T(8,128)}) custom-call(bf16[256,2048]{1,0:T(8,128)(2,1)} %tokens.5, bf16[1,2048]{1,0:T(2,128)(2,1)} %broadcast_in_dim.16.gain, bf16[344,2048]{1,0:T(8,128)(2,1)} %bitcast.48, bf16[344,2048]{1,0:T(8,128)(2,1)} %bitcast.50), custom_call_target="tpu_custom_call" | custom-call | flops 5771362304 | bytes 200000000 | tf_op jit(solution)/shard_map/project/pallas_call | solution.py:376
  90.1 19.4 %recur_forward.1 = (f32[2048,344]{1,0:T(8,128)}, bf16[2048,344]{1,0:T(8,128)(2,1)}, bf16[2048,344]{1,0:T(8,128)(2,1)}, f32[2048,344]{1,0:T(8,128)}, f32[2048,344...) custom-call(f32[2048,344]{1,0:T(8,128)} %bitcast.35, f32[2048,344]{1,0:T(8,128)} %bitcast.38, ...), custom_call_target="tpu_custom_call" | custom-call | tf_op jit(solution)/shard_map/recur_forward/pallas_call | solution.py:478
  109.5 107.8 %mixer_out.1 = (bf16[8,256,2048]{2,1,0:T(8,128)(2,1)}, f32[256,2048]{1,0:T(8,128)}, bf16[256,2048]{1,0:T(8,128)(2,1)}) custom-call(bf16[8,256,344]{2,1,0:T(8,128)(2,1)} %bitcast.46, bf16[344,2048]{1,0:T(8,128)(2,1)} %w_output.3, bf16[256,2048]{1,0:T(8,128)(2,1)} %cotangent.3, bf16[256,2048]{1,0:T(8,128)(2,1)} %tokens.5, bf16[1,2048]{1,0:T(2,128)(2,1)} %broadcast_in_dim.19.gain), custom_call_target="tpu_custom_call" | custom-call | flops 2885681152 | bytes 200000000 | tf_op jit(solution)/shard_map/mixer_out/pallas_call | solution.py:558
  217.3 95.2 %mlp.1 = (bf16[8,256,768]{2,1,0:T(8,128)(2,1)}, bf16[8,256,768]{2,1,0:T(8,128)(2,1)}, bf16[8,256,768]{2,1,0:T(8,128)(2,1)}, bf16[2048,768]{1,0:T(8,128)(2,1)}, b...) custom-call(bf16[256,2048]{1,0:T(8,128)(2,1)} %get-tuple-element.56.normed, ...), custom_call_target="tpu_custom_call" | custom-call | flops 38654705664 | bytes 200000000 | tf_op jit(solution)/shard_map/mlp/pallas_call | solution.py:662
  312.5 108.0 %mlp_back.1 = (f32[256,2048]{1,0:T(8,128)}, bf16[256,2048]{1,0:T(8,128)(2,1)}, f32[1,2048]{1,0:T(1,128)}) custom-call(bf16[8,256,768]{2,1,0:T(8,128)(2,1)} %get-tuple-element.60.g_first, bf16[8,256,768]{2,1,0:T(8,128)(2,1)} %get-tuple-element.61.g_second, bf16[2048,768]{1,0:T(8,128)(2,1)} %w_gelu.3, bf16[2048,768]{1,0:T(8,128)(2,1)} %w_linear.3, ...), custom_call_target="tpu_custom_call" | custom-call | flops 12884901888 | bytes 200000000 | tf_op jit(solution)/shard_map/mlp_back/pallas_call | solution.py:717
  420.5 104.9 %down.1 = (bf16[256,2048]{1,0:T(8,128)(2,1)}, f32[8,256,344]{2,1,0:T(8,128)}, bf16[344,2048]{1,0:T(8,128)(2,1)}) custom-call(bf16[8,256,768]{2,1,0:T(8,128)(2,1)} %get-tuple-element.58.hidden, bf16[768,2048]{1,0:T(8,128)(2,1)} %w_down.3, f32[256,2048]{1,0:T(8,128)} %get-tuple-element.59.residual, bf16[256,2048]{1,0:T(8,128)(2,1)} %get-tuple-element.62.g_low, ...), custom_call_target="tpu_custom_call" | custom-call | flops 12213813248 | bytes 200000000 | tf_op jit(solution)/shard_map/down/pallas_call | solution.py:773
  525.5 28.7 %recur_back.1 = (bf16[2048,344]{1,0:T(8,128)(2,1)}, bf16[2048,344]{1,0:T(8,128)(2,1)}, f32[8,344]{1,0:T(8,128)}, f32[2,344,344]{2,1,0:T(8,128)}) custom-call(f32[2048,344]{1,0:T(8,128)} %bitcast.40, f32[2048,344]{1,0:T(8,128)} %bitcast.39, f32[2048,344]{1,0:T(8,128)} %get-tuple-element.65.states.states_before, ...), custom_call_target="tpu_custom_call" | custom-call | tf_op jit(solution)/shard_map/recur_back/pallas_call | solution.py:932
  554.2 112.0 %input_back.1 = (f32[256,2048]{1,0:T(8,128)}, bf16[4,704,512]{2,1,0:T(8,128)(2,1)}, bf16[4,176,344]{2,1,0:T(8,128)(2,1)}, f32[8,256]{1,0:T(8,128)}) custom-call(bf16[2048,344]{1,0:T(8,128)(2,1)} %get-tuple-element.69.g_recur, bf16[2048,344]{1,0:T(8,128)(2,1)} %get-tuple-element.70.g_branch, bf16[344,2048]{1,0:T(8,128)(2,1)} %bitcast.49, ...), custom_call_target="tpu_custom_call" | custom-call | flops 11542724608 | bytes 200000000 | tf_op jit(solution)/shard_map/input_back/pallas_call | solution.py:1152
  666.2 1.1 bitcast_convert_fusion
  669.8 1.2 reshape.87
  671.0 2.6 convert_bitcast_fusion
  673.6 1.9 copy.49
  675.5 1.9 copy.48
  678.7 1.6 pad_maximum_fusion
  680.2 1.3 fusion
  681.6 3.2 convert_element_type.28
  684.8 3.2 convert_element_type.29
  687.9 3.6 convert_element_type.30
  691.5 3.4 convert_element_type.27
  695.9 1.3 copy.60
  (38 shorter events, 9.9 us)
Async XLA Ops:
  7.2 547.0 %all-reduce.6.cloned.1.call-start = ((), (), s32[]{:S(2)}) async-start(), calls=%async_computation.1 | async-start | bytes 18874368 | tf_op jit(solution)/shard_map/psum | solution.py:1235
  312.5 379.0 %all-reduce.4.cloned.1.call-start = ((), (), s32[]{:S(2)}) async-start(), calls=%async_computation | async-start | bytes 2818048 | tf_op jit(solution)/shard_map/psum | solution.py:1245
  666.2 2.4 copy-start.6
  666.2 3.0 copy-start.5
  675.5 6.1 copy-start.2
  681.6 3.2 copy-start.1
  684.8 3.2 copy-start
  691.5 3.4 copy-start.4
  691.5 4.4 copy-start.3
Sparse Core Ops, SparseCore 0:
  312.6 203.8 all-reduce.5
  554.4 103.9 all-reduce.3

commit v3 on v2

--- a/solution.py
+++ b/solution.py
@@ -110,9 +110,9 @@
         for p in range(self.pieces):
             self.copy(g.t, p, 2, g.sib).start()
 
-    def forward(self, d):
+    def forward(self, d, pieces=None):
         g = self.place
-        for p in range(self.pieces):
+        for p in range(self.pieces) if pieces is None else pieces:
 
             @pl.when(g.j - d >= 0)
             def _():
@@ -573,157 +573,267 @@
     )(mixture, w_output, cotangent, tokens, gain)
 
 
+PARTS = 8
+
+
 def mlp_kernel(
-    n, normed, cot_full, w_gelu, w_linear, w_down, hidden, g_first, g_second, grad_gelu, grad_linear, grad_down,
-    full, sent, came, cot, keep_h, keep_f, keep_s, acc_g, acc_l, acc_d, stage_c, stage_w, saved, fetched, drained,
+    n, normed, cot_full, w_gelu, w_linear, w_down, residual, cotangent, gain,
+    hidden, grad_gelu, grad_linear, grad_down, g_residual, g_low, g_gain,
+    full, sent, came, cot, keep_h, keep_f, keep_s, acc_g, acc_l, acc_d,
+    to_sib, sums, line, acc, saved, fetched, drained, sib_sent, sib_came, line_sent, line_came,
 ):
     g = Place(n)
     gather = Gather(g, full, sent, came)
     columns = w_gelu.shape[1]
-    width = full.shape[2]
+    rows, width = acc.shape
     tile = tile_of(columns, 256)
     wide = tile_of(width, 512)
+    strip = rows // PARTS
     full[g.t] = normed[...]
-
-    def fetch(t):
-        return pltpu.make_async_copy(cot_full.at[t], cot.at[t], fetched.at[t])
-
-    loop(n, lambda t: fetch(t).start())
     g.greet()
     gather.start()
     acc_g[...] = jnp.zeros_like(acc_g)
     acc_l[...] = jnp.zeros_like(acc_l)
     acc_d[...] = jnp.zeros_like(acc_d)
 
-    def save(t, start):
-        for q, (held, out) in enumerate(((keep_h, hidden), (keep_f, g_first), (keep_s, g_second))):
-            copy = pltpu.make_async_copy(held.at[t], out.at[t], saved.at[t, q])
-            copy.start() if start else copy.wait()
-
-    def use(t):
-        fetch(t).wait()
+    def fetch(t, q):
+        return pltpu.make_async_copy(cot_full.at[t], cot.at[q], fetched.at[q])
+
+    def save(t, q):
+        return pltpu.make_async_copy(keep_h.at[q], hidden.at[t], saved.at[q])
+
+    def layer(t, q):
+        fetch(t, q).wait()
 
         def part(i):
             cols = span(i, tile)
             first = dot(full[t], w_gelu[:, cols])
             second = dot(full[t], w_linear[:, cols])
-            back = dot_nt(cot[t], w_down[cols])
+            back = dot_nt(cot[q], w_down[cols])
             value, slope = gelu_parts(first)
-            keep_h[t, :, cols] = (value * second).astype(BF16)
-            keep_f[t, :, cols] = (back * second * slope).astype(BF16)
-            keep_s[t, :, cols] = (back * value).astype(BF16)
+            keep_h[q, :, cols] = (value * second).astype(BF16)
+            keep_f[q, :, cols] = (back * second * slope).astype(BF16)
+            keep_s[q, :, cols] = (back * value).astype(BF16)
 
         loop(columns // tile, part)
-        save(t, True)
+        save(t, q).start()
+
+    def partial(q, cols):
+        return dot_nt(keep_f[q], w_gelu[cols]) + dot_nt(keep_s[q], w_linear[cols])
+
+    def sib_copy(k):
+        return g.copy(to_sib, sums.at[k], sib_sent, sib_came.at[k], g.sib)
+
+    def line_copy(k, slot, p, to):
+        at = pl.ds(pl.multiple_of(p * strip, strip), strip)
+        return g.copy(
+            sums.at[k, at], line.at[slot, at], line_sent.at[k, p], line_came.at[slot, p], to
+        )
+
+    def chip(d, way):
+        k = g.j + way * d
+        mine, its = g.c, 1 - g.c
+        own, other = 2 * k + mine, 2 * k + its
+        fetch(other, its).start()
+        fetch(own, mine).start()
+        for p in range(gather.pieces):
+            gather.copy(other, p, 2, g.sib).wait_recv()
+        layer(other, its)
+
+        def offer(i):
+            cols = span(i, wide)
+            to_sib[:, cols] = partial(its, cols).astype(BF16)
+
+        loop(width // wide, offer)
+        sib_copy(k).start()
+        layer(own, mine)
+        sib_copy(k).wait()
+
+        @pl.when(d == 0)
+        def _():
+            def part(i):
+                cols = span(i, wide)
+                acc[:, cols] = partial(mine, cols) + sums[k, :, cols].astype(F32)
+
+            loop(width // wide, part)
+
+        @pl.when(d > 0)
+        def _():
+            def part(i):
+                cols = span(i, wide)
+                sums[k, :, cols] = (partial(mine, cols) + sums[k, :, cols].astype(F32)).astype(BF16)
+
+            loop(width // wide, part)
+            first = jnp.logical_or(
+                jnp.logical_and(way > 0, jnp.logical_not(g.has_down)),
+                jnp.logical_and(way < 0, jnp.logical_not(g.has_up)),
+            )
+
+            @pl.when(first)
+            def _():
+                slot = jnp.where(jnp.logical_and(way < 0, d == 1), g.nz, k)
+                for p in range(PARTS):
+                    line_copy(k, slot, p, g.t + 2 * way).start()
 
         def part(i):
             at = span(i, wide)
-            acc_g[at] += dot_tn(full[t, :, at], keep_f[t])
-            acc_l[at] += dot_tn(full[t, :, at], keep_s[t])
-            acc_d[:, at] += dot_tn(keep_h[t], cot[t, :, at])
+            both = full[pl.ds(2 * k, 2), :, at].reshape(2 * rows, wide)
+            acc_g[at] += dot_tn(both, keep_f[...].reshape(2 * rows, columns))
+            acc_l[at] += dot_tn(both, keep_s[...].reshape(2 * rows, columns))
+            acc_d[:, at] += dot_tn(
+                keep_h[...].reshape(2 * rows, columns), cot[:, :, at].reshape(2 * rows, wide)
+            )
 
         loop(width // wide, part)
-
-    gather.each(0, use)
-
-    def away(i):
-        gather.forward(i + 1)
-        gather.each(i + 1, use)
-
-    loop(g.nz - 1, away)
-    loop(n, lambda t: save(t, False))
+        save(other, its).wait()
+        save(own, mine).wait()
+
+    def relay(m):
+        def take(k, slot, sign, p):
+            at = pl.ds(pl.multiple_of(p * strip, strip), strip)
+            line_copy(k, slot, p, g.sib).wait_recv()
+
+            @pl.when(k == g.j)
+            def _():
+                acc[at] += line[slot, at].astype(F32)
+
+            @pl.when(k != g.j)
+            def _():
+                sums[k, at] = (sums[k, at].astype(F32) + line[slot, at].astype(F32)).astype(BF16)
+                there = jnp.where(jnp.logical_and(sign < 0, k == g.j - 1), g.nz, k)
+                line_copy(k, there, p, g.t + 2 * sign).start()
+
+        def rise(p):
+            pl.when(jnp.logical_and(g.has_down, m >= g.j))(lambda: take(m, m, 1, p))
+
+        def fall(p):
+            k = g.nz - 1 - m
+            pl.when(jnp.logical_and(g.has_up, k <= g.j))(
+                lambda: take(k, jnp.where(k == g.j, g.nz, k), -1, p)
+            )
+
+        lower = 2 * g.j < g.nz
+
+        def strips(i):
+            @pl.when(i < PARTS)
+            def _():
+                pl.when(lower)(lambda: rise(i))
+                pl.when(jnp.logical_not(lower))(lambda: fall(i))
+
+            @pl.when(i > 0)
+            def _():
+                pl.when(lower)(lambda: fall(i - 1))
+                pl.when(jnp.logical_not(lower))(lambda: rise(i - 1))
+
+        loop(PARTS + 1, strips)
+
+    def step(d):
+        up, down = g.j + d < g.nz, g.j - d >= 0
+
+        def way_of(w):
+            both = jnp.logical_and(up, down)
+            way = jnp.where(jnp.logical_and(w == 0, up), 1, -1)
+            wanted = jnp.where(w == 0, jnp.logical_or(up, down), jnp.logical_and(both, d > 0))
+            pl.when(wanted)(lambda: chip(d, way))
+
+            @pl.when(d < g.nz - 1)
+            def _():
+                for p in range(gather.pieces):
+                    pl.when(w == min(p, 1))(lambda: gather.forward(d + 1, (p,)))
+
+        loop(2, way_of)
+        pl.when(d > 1)(lambda: relay(d - 1))
+
+    loop(g.nz, step)
     gather.finish()
 
-    def drain(acc, stage, out, sem):
-        part = stage.shape[1]
-
-        def move(i):
-            slot = lax.rem(i, 2)
-            at = span(i, part)
-            copy = pltpu.make_async_copy(stage.at[slot], out.at[at], sem.at[slot])
-            pl.when(i >= 2)(copy.wait)
-            stage[slot] = acc[at].astype(BF16)
-            copy.start()
-
-        count = acc.shape[0] // part
-        loop(count, move)
-        for slot in range(min(count, 2)):
-            pltpu.make_async_copy(stage.at[slot], out.at[0:part], sem.at[slot]).wait()
-
-    drain(acc_g, stage_c, grad_gelu, drained)
-    drain(acc_l, stage_c, grad_linear, drained)
-    drain(acc_d, stage_w, grad_down, drained)
-
-
-def mlp(n, normed, cot_full, w_gelu, w_linear, w_down):
-    rows, width = normed.shape
-    columns = w_gelu.shape[1]
-    kept = pltpu.VMEM((n, rows, columns), BF16)
-    return pl.pallas_call(
-        functools.partial(mlp_kernel, n),
-        out_shape=(shape(n, rows, columns, dtype=BF16),) * 3
-        + (shape(width, columns, dtype=BF16),) * 2
-        + (shape(columns, width, dtype=BF16),),
-        in_specs=[VM, ANY, VM, VM, VM],
-        out_specs=(ANY,) * 6,
-        scratch_shapes=Gather.scratch(n, rows, width)
-        + [pltpu.VMEM((n, rows, width), BF16)]
-        + [kept] * 3
-        + [pltpu.VMEM((width, columns), F32)] * 2
-        + [pltpu.VMEM((columns, width), F32)]
-        + [pltpu.VMEM((2, tile_of(width, 128), columns), BF16)]
-        + [pltpu.VMEM((2, tile_of(columns, 64), width), BF16)]
-        + [pltpu.SemaphoreType.DMA((n, 3)), pltpu.SemaphoreType.DMA((n,)), pltpu.SemaphoreType.DMA((2,))],
-        compiler_params=comm_params(3),
-        cost_estimate=cost(12 * n * rows * width * columns),
-        name="mlp",
-    )(normed, cot_full, w_gelu, w_linear, w_down)
-
-
-def mlp_back_kernel(n, g_first, g_second, w_gelu, w_linear, residual, cotangent, gain, g_residual, g_low, g_gain, *bufs):
-    g = Place(n)
-
-    def partial(t, cols):
-        return dot_nt(g_first[t], w_gelu[cols]) + dot_nt(g_second[t], w_linear[cols])
-
-    scatter = Scatter(g, partial, tile_of(residual.shape[1], 512), bufs)
-    g.greet()
-    scatter.offers(g.nz - 1)
-
-    def around(i):
-        d = g.nz - 1 - i
-        scatter.offers(d - 1)
-        scatter.step(d)
-
-    loop(g.nz - 1, around)
-    scatter.last()
-    part = 32
+    stages = [held.at[q] for held in (keep_h, keep_f, keep_s) for q in (0, 1)]
+    leaving = []
+
+    def leave(i, value, out):
+        slot = i % len(stages)
+        if len(leaving) >= len(stages):
+            leaving[i - len(stages)].wait()
+        stages[slot][...] = value.astype(BF16)
+        copy = pltpu.make_async_copy(stages[slot], out, drained.at[slot])
+        copy.start()
+        leaving.append(copy)
+
+    count = width // rows
+    for i in range(count):
+        at = pl.ds(i * rows, rows)
+        leave(2 * i, acc_g[at], grad_gelu.at[at])
+        leave(2 * i + 1, acc_l[at], grad_linear.at[at])
+    wider = []
+    for i in range(columns // rows):
+        at = pl.ds(i * rows, rows)
+        full[i] = acc_d[at].astype(BF16)
+        wider.append(pltpu.make_async_copy(full.at[i], grad_down.at[at], drained.at[len(stages) + i]))
+        wider[-1].start()
+    relay(g.nz - 1)
+    lines = 32
     g_gain[...] = jnp.zeros_like(g_gain)
 
     def rows_of(i):
-        at = span(i, part)
-        back, terms = norm_grad(residual[at], gain[...].astype(F32), scatter.acc[at])
+        at = span(i, lines)
+        back, terms = norm_grad(residual[at], gain[...].astype(F32), acc[at])
         value = cotangent[at].astype(F32) + back
         g_residual[at] = value
         g_low[at] = value.astype(BF16)
         g_gain[...] += jnp.sum(terms, axis=0, keepdims=True)
 
-    loop(residual.shape[0] // part, rows_of)
-    scatter.finish()
-
-
-def mlp_back(n, g_first, g_second, w_gelu, w_linear, residual, cotangent, gain):
-    rows, width = residual.shape
+    loop(rows // lines, rows_of)
+    for copy in leaving[-len(stages):] + wider:
+        copy.wait()
+
+    def done(k):
+        @pl.when(k != g.j)
+        def _():
+            for p in range(PARTS):
+                line_copy(k, k, p, g.sib).wait_send()
+
+    loop(g.nz, done)
+
+
+def mlp(n, normed, cot_full, w_gelu, w_linear, w_down, residual, cotangent, gain):
+    rows, width = normed.shape
+    columns = w_gelu.shape[1]
+    kept = pltpu.VMEM((2, rows, columns), BF16)
+    sems = pltpu.SemaphoreType.DMA
     return pl.pallas_call(
-        functools.partial(mlp_back_kernel, n),
-        out_shape=(shape(rows, width), shape(rows, width, dtype=BF16), shape(1, width)),
-        in_specs=[VM] * 7,
-        out_specs=(VM,) * 3,
-        scratch_shapes=Scatter.scratch(n, rows, width),
-        compiler_params=comm_params(4),
-        cost_estimate=cost(4 * n * rows * width * w_gelu.shape[1]),
-        name="mlp_back",
-    )(g_first, g_second, w_gelu, w_linear, residual, cotangent, gain)
+        functools.partial(mlp_kernel, n),
+        out_shape=(shape(n, rows, columns, dtype=BF16),)
+        + (shape(width, columns, dtype=BF16),) * 2
+        + (
+            shape(columns, width, dtype=BF16),
+            shape(rows, width),
+            shape(rows, width, dtype=BF16),
+            shape(1, width),
+        ),
+        in_specs=[VM, ANY] + [VM] * 6,
+        out_specs=(ANY,) * 4 + (VM,) * 3,
+        scratch_shapes=Gather.scratch(n, rows, width)
+        + [pltpu.VMEM((2, rows, width), BF16)]
+        + [kept] * 3
+        + [pltpu.VMEM((width, columns), F32)] * 2
+        + [
+            pltpu.VMEM((columns, width), F32),
+            pltpu.VMEM((rows, width), BF16),
+            pltpu.VMEM((n // 2, rows, width), BF16),
+            pltpu.VMEM((n // 2 + 1, rows, width), BF16),
+            pltpu.VMEM((rows, width), F32),
+            sems((2,)),
+            sems((2,)),
+            sems((6 + columns // rows,)),
+            sems,
+            sems((n // 2,)),
+            sems((n // 2, PARTS)),
+            sems((n // 2 + 1, PARTS)),
+        ],
+        compiler_params=comm_params(3),
+        cost_estimate=cost(16 * n * rows * width * columns),
+        name="mlp",
+    )(normed, cot_full, w_gelu, w_linear, w_down, residual, cotangent, gain)
 
 
 def down_kernel(
@@ -1229,13 +1339,10 @@
     )
     mixture = blocked(mixture)
     cot_full, residual, normed_mlp = mixer_out(n, mixture, w_output, cotangent, tokens, gain_second)
-    hidden, g_first, g_second, grad_gelu, grad_linear, grad_down = mlp(
-        n, normed_mlp, cot_full, w_gelu, w_linear, w_down
+    hidden, grad_gelu, grad_linear, grad_down, g_residual, g_low, gain_second_grad = mlp(
+        n, normed_mlp, cot_full, w_gelu, w_linear, w_down, residual, cotangent, gain_second
     )
     mlp_sums = lax.psum((grad_gelu, grad_linear, grad_down), "dp")
-    g_residual, g_low, gain_second_grad = mlp_back(
-        n, g_first, g_second, w_gelu, w_linear, residual, cotangent, gain_second
-    )
     output, g_mixture, grad_output = down(n, hidden, w_down, residual, g_low, w_output, mixture)
     g_recur, g_branch, small, g_gates = recur_back(
         flat(g_mixture), branch, states, recur, conv_low, recall, ingate, start_state, start_conv,

time: 709 us -> 709 us (level)
  Pallas kernels: 648 us -> 593 us
  waiting for transfers between devices: 0.06 us -> 53.7 us
    pallas_call x1 -> x0, Pallas kernels: 108 us -> none  [mlp_back(): pl.pallas_call(functools.partial(mlp_back_kernel, n), out_shape=(shape(ro...]
    psum x1, waiting for transfers between devices: 0.02 us -> 53.6 us  [body(): mlp_sums = lax.psum((grad_gelu, grad_linear, grad_down), 'dp')]
    pallas_call x1, Pallas kernels: 95.2 us -> 144 us  [mlp(): pl.pallas_call(functools.partial(mlp_kernel, n), out_shape=(shape(n, rows...]
  transfers between devices with their start and end apart: 2 -> 2, of which waited for: 0 -> 1; matrix products, arithmetic and copies ran while one was open for 4% -> 4% of each run, Pallas kernels for 50% -> 36%
where the time goes in v3:
time: 709 us; the launch traced here: 702 us
  Pallas kernels  593 us (84%)
  waiting for transfers between devices  53.7 us (8%)
  other arithmetic  22.3 us (3%)
  local copies, waits for them, and re-layouts  19 us (3%)
  between operations  14.2 us (2%)
    pallas_call x1, Pallas kernels, mlp(): pl.pallas_call(functools.partial(mlp_kernel, n), out_shape=(shape(n, rows...  144 us
    pallas_call x1, Pallas kernels, down(): pl.pallas_call(functools.partial(down_kernel, n), out_shape=(shape(rows,...  112 us
    pallas_call x1, Pallas kernels, input_back(): pl.pallas_call(functools.partial(input_back_kernel, n, copies), out_shape...  109 us
    pallas_call x1, Pallas kernels, mixer_out(): pl.pallas_call(functools.partial(mixer_out_kernel, n), out_shape=(shape(n...  108 us
    pallas_call x1, Pallas kernels, project(): pl.pallas_call(functools.partial(project_kernel, n), out_shape=(shape(n,...  72.5 us
    psum x1, waiting for transfers between devices, body(): mlp_sums = lax.psum((grad_gelu, grad_linear, grad_down), 'dp')  53.6 us
    pallas_call x1, Pallas kernels, recur_back(): pl.pallas_call(recur_back_kernel, grid=(sequences, chunks), out_shape=(sh...  29 us
    pallas_call x1, Pallas kernels, recur_forward(): pl.pallas_call(recur_kernel, grid=(sequences, chunks), out_shape=(shape(t...  19.4 us
  transfers between devices with their start and end apart: 2, of which 1 were waited for; matrix products, arithmetic and copies ran while one was open for 4% of the time, Pallas kernels for 36%

profile of v3, /device:TPU:8, one launch (start us, length us, event | category | flops | bytes accessed | tf_op | source)
XLA Modules:
  0.0 702.4 jit_solution(16752305431367732561)
XLA Ops:
  7.9 1.2 broadcast_in_dim.18.decay
  10.5 1.3 broadcast_in_dim.16.gain
  11.8 1.3 broadcast_in_dim.19.gain
  13.1 1.4 copy_multiply_fusion.start_conv
  17.6 72.5 %project.1 = (bf16[8,256,2048]{2,1,0:T(8,128)(2,1)}, f32[8,256,344]{2,1,0:T(8,128)}, f32[8,256,344]{2,1,0:T(8,128)}) custom-call(bf16[256,2048]{1,0:T(8,128)(2,1)} %tokens.5, bf16[1,2048]{1,0:T(2,128)(2,1)} %broadcast_in_dim.16.gain, bf16[344,2048]{1,0:T(8,128)(2,1)} %bitcast.48, bf16[344,2048]{1,0:T(8,128)(2,1)} %bitcast.50), custom_call_target="tpu_custom_call" | custom-call | flops 5771362304 | bytes 200000000 | tf_op jit(solution)/shard_map/project/pallas_call | solution.py:376
  90.1 19.4 %recur_forward.1 = (f32[2048,344]{1,0:T(8,128)}, bf16[2048,344]{1,0:T(8,128)(2,1)}, bf16[2048,344]{1,0:T(8,128)(2,1)}, f32[2048,344]{1,0:T(8,128)}, f32[2048,344...) custom-call(f32[2048,344]{1,0:T(8,128)} %bitcast.35, f32[2048,344]{1,0:T(8,128)} %bitcast.38, ...), custom_call_target="tpu_custom_call" | custom-call | tf_op jit(solution)/shard_map/recur_forward/pallas_call | solution.py:478
  109.5 107.7 %mixer_out.1 = (bf16[8,256,2048]{2,1,0:T(8,128)(2,1)}, f32[256,2048]{1,0:T(8,128)}, bf16[256,2048]{1,0:T(8,128)(2,1)}) custom-call(bf16[8,256,344]{2,1,0:T(8,128)(2,1)} %bitcast.46, bf16[344,2048]{1,0:T(8,128)(2,1)} %w_output.3, bf16[256,2048]{1,0:T(8,128)(2,1)} %cotangent.3, bf16[256,2048]{1,0:T(8,128)(2,1)} %tokens.5, bf16[1,2048]{1,0:T(2,128)(2,1)} %broadcast_in_dim.19.gain), custom_call_target="tpu_custom_call" | custom-call | flops 2885681152 | bytes 200000000 | tf_op jit(solution)/shard_map/mixer_out/pallas_call | solution.py:558
  217.2 144.0 %mlp.1 = (bf16[8,256,768]{2,1,0:T(8,128)(2,1)}, bf16[2048,768]{1,0:T(8,128)(2,1)}, bf16[2048,768]{1,0:T(8,128)(2,1)}, bf16[768,2048]{1,0:T(8,128)(2,1)}, f32[256...) custom-call(bf16[256,2048]{1,0:T(8,128)(2,1)} %get-tuple-element.54.normed, ...), custom_call_target="tpu_custom_call" | custom-call | flops 51539607552 | bytes 200000000 | tf_op jit(solution)/shard_map/mlp/pallas_call | solution.py:803
  361.3 111.9 %down.1 = (bf16[256,2048]{1,0:T(8,128)(2,1)}, f32[8,256,344]{2,1,0:T(8,128)}, bf16[344,2048]{1,0:T(8,128)(2,1)}) custom-call(bf16[8,256,768]{2,1,0:T(8,128)(2,1)} %get-tuple-element.57.hidden, bf16[768,2048]{1,0:T(8,128)(2,1)} %w_down.3, f32[256,2048]{1,0:T(8,128)} %get-tuple-element.56.residual, bf16[256,2048]{1,0:T(8,128)(2,1)} %get-tuple-element.58.g_low, ...), custom_call_target="tpu_custom_call" | custom-call | flops 12213813248 | bytes 200000000 | tf_op jit(solution)/shard_map/down/pallas_call | solution.py:883
  473.2 29.0 %recur_back.1 = (bf16[2048,344]{1,0:T(8,128)(2,1)}, bf16[2048,344]{1,0:T(8,128)(2,1)}, f32[8,344]{1,0:T(8,128)}, f32[2,344,344]{2,1,0:T(8,128)}) custom-call(f32[2048,344]{1,0:T(8,128)} %bitcast.40, f32[2048,344]{1,0:T(8,128)} %bitcast.39, f32[2048,344]{1,0:T(8,128)} %get-tuple-element.61.states.states_before, ...), custom_call_target="tpu_custom_call" | custom-call | tf_op jit(solution)/shard_map/recur_back/pallas_call | solution.py:1042
  502.2 53.6 %all-reduce.6.cloned.1.call-done = (bf16[2048,768]{1,0:T(8,128)(2,1)}, bf16[2048,768]{1,0:T(8,128)(2,1)}, bf16[768,2048]{1,0:T(8,128)(2,1)}) async-done(((bf16[2048,768]{1,0:T(8,128)(2,1)}, bf16[2048,768]{1,0:T(8,128)(2,1)}, bf16[768,2048]{1,0:T(8,128)(2,1)}), (bf16[2048,768]{1,0:T(8,128)(2,1)}, bf16[2048,768]{1,0:T(8,128)(2,1)}, bf16[768,2048]{1,0:T(8,128)(2,1)})) %all-reduce.6.cloned.1.call-update) | async-done | bytes 9437200 | tf_op jit(solution)/shard_map/psum | solution.py:1345
  555.8 108.7 %input_back.1 = (f32[256,2048]{1,0:T(8,128)}, bf16[4,704,512]{2,1,0:T(8,128)(2,1)}, bf16[4,176,344]{2,1,0:T(8,128)(2,1)}, f32[8,256]{1,0:T(8,128)}) custom-call(bf16[2048,344]{1,0:T(8,128)(2,1)} %get-tuple-element.65.g_recur, bf16[2048,344]{1,0:T(8,128)(2,1)} %get-tuple-element.66.g_branch, bf16[344,2048]{1,0:T(8,128)(2,1)} %bitcast.49, ...), custom_call_target="tpu_custom_call" | custom-call | flops 11542724608 | bytes 200000000 | tf_op jit(solution)/shard_map/input_back/pallas_call | solution.py:1262
  664.6 1.1 bitcast_convert_fusion
  668.2 1.2 reshape.87
  669.4 2.6 convert_bitcast_fusion
  671.9 1.9 copy.49
  673.9 1.9 copy.48
  677.0 1.6 pad_maximum_fusion
  678.6 1.3 fusion
  679.9 3.2 convert_element_type.28
  683.1 3.2 convert_element_type.29
  686.3 3.6 convert_element_type.30
  689.9 3.4 convert_element_type.27
  694.2 1.3 copy.60
  (37 shorter events, 9.9 us)
Async XLA Ops:
  7.2 548.6 %all-reduce.6.cloned.1.call-start = ((), (), s32[]{:S(2)}) async-start(), calls=%async_computation.1 | async-start | bytes 18874368 | tf_op jit(solution)/shard_map/psum | solution.py:1345
  361.3 328.6 %all-reduce.4.cloned.1.call-start = ((), (), s32[]{:S(2)}) async-start(), calls=%async_computation | async-start | bytes 2818048 | tf_op jit(solution)/shard_map/psum | solution.py:1352
  664.6 2.4 copy-start.6
  664.6 3.0 copy-start.5
  673.9 6.1 copy-start.2
  679.9 3.2 copy-start.1
  683.1 3.2 copy-start
  689.9 3.4 copy-start.4
  689.9 4.4 copy-start.3
Sparse Core Ops, SparseCore 0:
  361.4 194.3 all-reduce.5
  558.9 104.0 all-reduce.3

commit v4 on v3

--- a/solution.py
+++ b/solution.py
@@ -170,8 +170,9 @@
 class Scatter:
     def __init__(self, place, partial, tile, bufs):
         self.place, self.partial, self.tile = place, partial, tile
-        self.to_sib, self.from_sib, self.line, self.out, self.acc = bufs[:5]
-        self.sib_send, self.sib_recv, self.line_send, self.line_recv = bufs[5:]
+        self.to_sib, self.from_sib, self.line, self.acc = bufs[:4]
+        self.sib_send, self.sib_recv, self.line_send, self.line_recv = bufs[4:]
+        self.out = self.from_sib
         self.tiles = self.acc.shape[1] // tile
 
     @staticmethod
@@ -181,7 +182,6 @@
             pltpu.VMEM((nz, rows, width), BF16),
             pltpu.VMEM((nz, rows, width), BF16),
             pltpu.VMEM((nz + 1, rows, width), BF16),
-            pltpu.VMEM((nz, rows, width), BF16),
             pltpu.VMEM((rows, width), F32),
             pltpu.SemaphoreType.DMA((nz,)),
             pltpu.SemaphoreType.DMA((nz,)),
@@ -1070,72 +1070,119 @@
     )(g_mix, branch, states, states, u, u, conv_low, recall, ingate, start_state, start_conv, conv, gate_w, decay)
 
 
-class Spread:
-    def __init__(self, me, count, part, landed, summed, sems):
-        self.me, self.count, self.part, self.landed, self.summed = me, count, part, landed, summed
-        self.out_send, self.out_recv, self.back_send, self.back_recv = sems
-
-    def others(self, act):
-        loop(self.count, lambda i: pl.when(i != self.me)(lambda: act(i)))
-
-    def out(self, i, slot):
+class Halving:
+    def __init__(self, me, count, data, landed, final, sems):
+        self.me, self.count = me, count
+        self.data, self.landed, self.final = data, landed, final
+        self.out_send, self.out_recv, self.back_send, self.back_recv = (sems.at[q] for q in range(4))
+        self.bits = count.bit_length() - 1
+        assert count == 1 << self.bits
+
+    @staticmethod
+    def scratch(count, rows, columns):
+        slots = max(count - 1, 1)
+        return [
+            pltpu.VMEM((2, count, rows, columns), BF16),
+            pltpu.VMEM((2, slots, rows, columns), BF16),
+            pltpu.VMEM((2, count, rows, columns), BF16),
+            pltpu.SemaphoreType.DMA((4, 2, slots)),
+        ]
+
+    def own(self, bit):
+        return lax.rem(lax.div(self.me, 1 << bit), 2)
+
+    def swaps(self, s):
+        for track in (0, 1):
+            order = [(i + track) % self.bits for i in range(self.bits)]
+            bit = order[s]
+            partner = self.me + (1 - 2 * self.own(bit)) * (1 << bit)
+            fixed = sum(self.own(b) * (1 << b) for b in order[:s])
+            for u in range(self.count >> (s + 1)):
+                free = sum(((u >> i) & 1) << b for i, b in enumerate(order[s + 1 :]))
+                slot = self.count - (self.count >> s) + u
+                kept = fixed + free + self.own(bit) * (1 << bit)
+                yield track, slot, partner, fixed + free + (1 - self.own(bit)) * (1 << bit), kept
+
+    def out(self, track, slot, partner, given):
         return pltpu.make_async_remote_copy(
-            src_ref=self.part(i),
-            dst_ref=self.landed.at[slot],
-            send_sem=self.out_send.at[i],
-            recv_sem=self.out_recv.at[slot],
-            device_id={"dp": i},
+            src_ref=self.data.at[track, given],
+            dst_ref=self.landed.at[track, slot],
+            send_sem=self.out_send.at[track, slot],
+            recv_sem=self.out_recv.at[track, slot],
+            device_id={"dp": partner},
             device_id_type=MESH,
         )
 
-    def back(self, i, slot):
+    def back(self, track, slot, partner, segment):
         return pltpu.make_async_remote_copy(
-            src_ref=self.summed.at[slot],
-            dst_ref=self.summed.at[slot],
-            send_sem=self.back_send.at[i],
-            recv_sem=self.back_recv.at[slot],
-            device_id={"dp": i},
+            src_ref=self.final.at[track, segment],
+            dst_ref=self.final.at[track, segment],
+            send_sem=self.back_send.at[track, slot],
+            recv_sem=self.back_recv.at[track, slot],
+            device_id={"dp": partner},
             device_id_type=MESH,
         )
 
-    def start(self):
-        self.others(lambda i: self.out(i, self.me).start())
-        self.landed[self.me] = self.part(self.me)[...]
-
-    def turn(self):
-        self.others(lambda i: self.out(i, i).wait_recv())
-        rows = self.landed.shape[1]
+    def start(self, s=0):
+        for track, slot, partner, given, _ in self.swaps(s):
+            self.out(track, slot, partner, given).start()
+
+    def turn(self, s):
+        rows = self.data.shape[2]
         tile = tile_of(rows, 32)
-
-        def add(r):
-            at = span(r, tile)
-            value = self.landed[0, at].astype(F32)
-            for i in range(1, self.count):
-                value = value + self.landed[i, at].astype(F32)
-            self.summed[self.me, at] = value.astype(BF16)
-
-        loop(rows // tile, add)
-        self.others(lambda i: self.back(i, self.me).start())
+        for track, slot, partner, given, kept in self.swaps(s):
+            self.out(track, slot, partner, given).wait_recv()
+            result = self.final if s == self.bits - 1 else self.data
+
+            def add(r):
+                at = span(r, tile)
+                value = self.data[track, kept, at].astype(F32) + self.landed[track, slot, at].astype(F32)
+                result[track, kept, at] = value.astype(BF16)
+
+            loop(rows // tile, add)
+        if s < self.bits - 1:
+            self.start(s + 1)
+        else:
+            self.start_back(s)
+
+    def start_back(self, s):
+        for track, slot, partner, _, kept in self.swaps(s):
+            self.back(track, slot, partner, kept).start()
+
+    def turn_back(self, s):
+        for track, slot, partner, given, _ in self.swaps(s):
+            self.back(track, slot, partner, given).wait_recv()
+        if s > 0:
+            self.start_back(s - 1)
+
+    def events(self):
+        steps = [functools.partial(self.turn, s) for s in range(self.bits)]
+        return steps + [functools.partial(self.turn_back, s) for s in range(self.bits - 1, 0, -1)]
 
     def finish(self):
-        self.others(lambda i: self.back(i, i).wait_recv())
-        self.others(lambda i: self.out(i, i).wait_send())
-        self.others(lambda i: self.back(i, self.me).wait_send())
+        self.turn_back(0)
+        for s in range(self.bits):
+            for track, slot, partner, given, kept in self.swaps(s):
+                self.out(track, slot, partner, given).wait_send()
+                self.back(track, slot, partner, kept).wait_send()
 
 
 def input_back_kernel(
-    n, copies, g_recur, g_branch, w_in, w_br, normed, tokens, g_residual, gain, second_gain, g_gates, small,
-    input_grad, pair_out, rest_out, gains_out,
-    pair, pair_in, pair_all, rest, rest_in, rest_all, gain_row, gain_parts, gain_in, gain_sum, gain_dp,
-    pair_sems, rest_sems, gain_sent, gain_came, gain_dp_sent, gain_dp_came, *bufs
+    n, copies, g_recur, g_branch, w_in, w_br, normed, tokens, g_residual, gain, second_gain, g_gates, small, g_out,
+    input_grad, in_out, br_out, out_out, gates_out, conv_out, bias_out, decay_out, gains_out,
+    gain_row, gain_parts, gain_in, gain_sum, gain_dp, gain_sent, gain_came, gain_dp_sent, gain_dp_came, *bufs
 ):
     g = Place(n)
     me = lax.axis_index("dp")
     rows, width = tokens.shape
     channels = w_in.shape[0]
-    part_width = width // copies
-    padded = pair.shape[1] // 2
+    blocks, block_width = gates_out.shape[1], gates_out.shape[2]
+    segment = width // (2 * copies)
     gain_width = width // n
+    weights = Halving(me, copies, *bufs[:4])
+    rest = Halving(me, copies, *bufs[4:8])
+    padded = bufs[0].shape[2] // 3
+    rest_rows = bufs[4].shape[2]
 
     def block(ref, t):
         return ref[span(t, rows)]
@@ -1143,9 +1190,7 @@
     def partial(t, cols):
         return dot(block(g_recur, t), w_in[:, cols]) + dot(block(g_branch, t), w_br[:, cols])
 
-    scatter = Scatter(g, partial, tile_of(width, 512), bufs)
-    pairs = Spread(me, copies, lambda i: pair.at[i], pair_in, pair_all, [pair_sems.at[q] for q in range(4)])
-    rests = Spread(me, copies, lambda i: rest.at[i], rest_in, rest_all, [rest_sems.at[q] for q in range(4)])
+    scatter = Scatter(g, partial, tile_of(width, 512), bufs[8:])
 
     def gain_copy(t, slot):
         return g.copy(gain_parts.at[t], gain_in.at[slot], gain_sent.at[t], gain_came.at[slot], t)
@@ -1163,13 +1208,14 @@
     def others(act):
         loop(n, lambda t: pl.when(t != g.t)(lambda: act(t)))
 
+    def copies_of(act):
+        loop(copies, lambda i: pl.when(i != me)(lambda: act(i)))
+
     barrier = pltpu.get_barrier_semaphore()
     others(
         lambda t: pl.semaphore_signal(barrier, inc=1, device_id={"tensor": t}, device_id_type=MESH)
     )
-    pairs.others(
-        lambda i: pl.semaphore_signal(barrier, inc=1, device_id={"dp": i}, device_id_type=MESH)
-    )
+    copies_of(lambda i: pl.semaphore_signal(barrier, inc=1, device_id={"dp": i}, device_id_type=MESH))
     pl.semaphore_wait(barrier, n - 1 + copies - 1)
 
     scatter.offers(g.nz - 1)
@@ -1179,21 +1225,32 @@
         scatter.offers(d - 1)
         scatter.step(d)
 
-    pair[...] = jnp.zeros_like(pair)
+    around(0)
+
+    data = bufs[0]
 
     def weigh(q):
-        cols = span(q, part_width)
+        cols = span(q, 2 * segment)
         first = dot_tn(g_recur[...], normed[:, cols])
-        pair[q, 0:channels] = first.astype(BF16)
-        terms = jnp.sum(w_in[:, cols].astype(F32) * first, axis=0, keepdims=True)
         second = dot_tn(g_branch[...], normed[:, cols])
-        pair[q, padded : padded + channels] = second.astype(BF16)
-        terms += jnp.sum(w_br[:, cols].astype(F32) * second, axis=0, keepdims=True)
+        third = g_out[:, cols]
+        for half in (0, 1):
+            index = 2 * q + half
+            track, part = lax.div(index, copies), lax.rem(index, copies)
+            for i, value in enumerate((first, second, third)):
+                piece = value[:, half * segment : (half + 1) * segment].astype(BF16)
+                data[track, part, i * padded : i * padded + channels] = piece
+                if padded > channels:
+                    data[track, part, i * padded + channels : (i + 1) * padded] = jnp.zeros(
+                        (padded - channels, segment), BF16
+                    )
+        terms = jnp.sum(w_in[:, cols].astype(F32) * first + w_br[:, cols].astype(F32) * second, axis=0, keepdims=True)
         gain_row[0:1, cols] = terms / gain[0:1, cols].astype(F32)
 
     loop(copies, weigh)
-    pairs.start()
+    weights.start()
     gain_row[1:2] = second_gain[...]
+    gain_row[2:8] = jnp.zeros((6, width), F32)
     for t in range(n):
         gain_parts[t] = gain_row[:, t * gain_width : (t + 1) * gain_width]
     others(lambda t: gain_copy(t, g.t).start())
@@ -1204,27 +1261,29 @@
             g_gates[0],
             g_gates[1],
             small[...],
-            jnp.zeros((copies * rest.shape[1] - 2 * channels - 8, channels), F32),
+            jnp.zeros((2 * copies * rest_rows - 2 * channels - 8, channels), F32),
         ],
         axis=0,
     ).astype(BF16)
-    for i in range(copies):
-        rest[i] = flat[i * rest.shape[1] : (i + 1) * rest.shape[1]]
-    rests.start()
-
-    loop(g.nz - 2, around)
-
-    others(lambda t: gain_copy(t, t).wait_recv())
-    total = gain_in[0]
-    for t in range(1, n):
-        total = total + gain_in[t]
-    gain_sum[...] = total
-    pairs.others(lambda i: gain_dp_copy(i, me).start())
-    gain_dp[me] = total
-    pairs.turn()
-    rests.turn()
-
-    around(g.nz - 2)
+    for i in range(2 * copies):
+        bufs[4][i // copies, i % copies] = flat[i * rest_rows : (i + 1) * rest_rows]
+    rest.start()
+
+    events = [lambda a=a, b=b: (a(), b()) for a, b in zip(weights.events(), rest.events())]
+    for i in range(1, g.nz - 1):
+        around(i)
+        if events:
+            events.pop(0)()
+        if i == 1:
+            others(lambda t: gain_copy(t, t).wait_recv())
+            total = gain_in[0]
+            for t in range(1, n):
+                total = total + gain_in[t]
+            gain_sum[...] = total
+            copies_of(lambda i: gain_dp_copy(i, me).start())
+            gain_dp[me] = total
+    for event in events:
+        event()
     scatter.last()
     part = 32
 
@@ -1234,17 +1293,28 @@
         input_grad[at] = g_residual[at] + back
 
     loop(rows // part, rows_of)
-    pairs.others(lambda i: gain_dp_copy(i, i).wait_recv())
+    copies_of(lambda i: gain_dp_copy(i, i).wait_recv())
     total = gain_dp[0]
     for i in range(1, copies):
         total = total + gain_dp[i]
     gains_out[...] = total
-    pairs.finish()
-    rests.finish()
-    pair_out[...] = pair_all[...]
-    rest_out[...] = rest_all[...]
+    rest.finish()
+    flat = jnp.concatenate([bufs[6][i // copies, i % copies].astype(F32) for i in range(2 * copies)], axis=0)
+    for q in (0, 1):
+        for i in range(blocks):
+            start = q * channels + i * block_width
+            gates_out[q, i] = flat[start : start + block_width, i * block_width : (i + 1) * block_width]
+    conv_out[...] = flat[2 * channels : 2 * channels + 5]
+    bias_out[...] = flat[2 * channels + 5 : 2 * channels + 7]
+    decay_out[...] = flat[2 * channels + 7 : 2 * channels + 8]
+    weights.finish()
+    for i in range(2 * copies):
+        for q, out in enumerate((in_out, br_out, out_out)):
+            out[:, i * segment : (i + 1) * segment] = bufs[2][
+                i // copies, i % copies, q * padded : q * padded + channels
+            ]
     others(lambda t: gain_copy(t, t).wait_send())
-    pairs.others(lambda i: gain_dp_copy(i, i).wait_send())
+    copies_of(lambda i: gain_dp_copy(i, i).wait_send())
     scatter.finish()
 
 
@@ -1252,43 +1322,47 @@
     return (extent + multiple - 1) // multiple * multiple
 
 
-def input_back(n, copies, g_recur, g_branch, w_in, w_br, normed, tokens, g_residual, gain, second_gain, g_gates, small):
+def input_back(
+    n, copies, g_recur, g_branch, w_in, w_br, normed, tokens, g_residual, gain, second_gain, g_gates, small, g_out,
+    blocks,
+):
     rows, width = tokens.shape
     channels = w_in.shape[0]
-    pair_shape = (copies, 2 * up_to(channels, 16), width // copies)
-    rest_shape = (copies, up_to(2 * channels + 8, 16 * copies) // copies, channels)
+    block = channels // blocks
+    rest_rows = up_to((2 * channels + 8 + 2 * copies - 1) // (2 * copies), 16)
     gain_shape = (8, width // n)
     sems = pltpu.SemaphoreType.DMA
     return pl.pallas_call(
         functools.partial(input_back_kernel, n, copies),
-        out_shape=(
-            shape(rows, width),
-            shape(*pair_shape, dtype=BF16),
-            shape(*rest_shape, dtype=BF16),
+        out_shape=(shape(rows, width),)
+        + (shape(channels, width, dtype=BF16),) * 3
+        + (
+            shape(2, blocks, block, block),
+            shape(5, channels),
+            shape(2, channels),
+            shape(1, channels),
             shape(*gain_shape),
         ),
-        in_specs=[VM] * 11,
-        out_specs=(VM,) * 4,
-        scratch_shapes=[pltpu.VMEM(pair_shape, BF16)] * 3
-        + [pltpu.VMEM(rest_shape, BF16)] * 3
-        + [
+        in_specs=[VM] * 12,
+        out_specs=(VM,) * 9,
+        scratch_shapes=[
             pltpu.VMEM((8, width), F32),
             pltpu.VMEM((n, *gain_shape), F32),
             pltpu.VMEM((n, *gain_shape), F32),
             pltpu.VMEM(gain_shape, F32),
             pltpu.VMEM((copies, *gain_shape), F32),
-            sems((4, copies)),
-            sems((4, copies)),
             sems((n,)),
             sems((n,)),
             sems((copies,)),
             sems((copies,)),
         ]
+        + Halving.scratch(copies, 3 * up_to(channels, 16), width // (2 * copies))
+        + Halving.scratch(copies, rest_rows, channels)
         + Scatter.scratch(n, rows, width),
         compiler_params=comm_params(6),
         cost_estimate=cost(8 * n * rows * width * channels),
         name="input_back",
-    )(g_recur, g_branch, w_in, w_br, normed, tokens, g_residual, gain, second_gain, g_gates, small)
+    )(g_recur, g_branch, w_in, w_br, normed, tokens, g_residual, gain, second_gain, g_gates, small, g_out)
 
 
 def body(
@@ -1348,36 +1422,24 @@
         flat(g_mixture), branch, states, recur, conv_low, recall, ingate, start_state, start_conv,
         conv_params, gate_w, decay,
     )
-    mlp_sums, grad_output = lax.optimization_barrier((mlp_sums, grad_output))
-    output_sum = lax.psum(grad_output, "dp")
-    input_grad, pair, rest, gains = input_back(
+    input_grad, grad_input, grad_branch, grad_output, gates, g_conv, g_bias, g_decay, gains = input_back(
         n, copies, g_recur, g_branch, w_in, w_br, flat(normed), tokens, g_residual, gain_first,
-        gain_second_grad, g_gates, small,
+        gain_second_grad, g_gates, small, grad_output, blocks,
     )
-    padded = pair.shape[1] // 2
-
-    def whole(part):
-        return part[:, :channels].astype(F32).transpose(1, 0, 2).reshape(channels, width).T
-
-    rest = rest.astype(F32).reshape(-1, channels)
-    gates = rest[: 2 * channels].reshape(2, blocks, block, blocks, block)
-    gates = jnp.stack([gates[:, i, :, i] for i in range(blocks)], axis=1)
-    small = rest[2 * channels : 2 * channels + 8]
     grad_gelu, grad_linear, grad_down = (x.astype(F32) for x in mlp_sums)
-    grad_output = output_sum.astype(F32)
     return (
         output,
         input_grad,
         final_state[:, 0],
         final_conv,
         gains[0],
-        whole(pair[:, :padded]),
-        whole(pair[:, padded:]),
-        small[:5],
+        grad_input.astype(F32).T,
+        grad_branch.astype(F32).T,
+        g_conv,
         gates,
-        small[5:7],
-        small[7],
-        grad_output,
+        g_bias,
+        g_decay[0],
+        grad_output.astype(F32),
         gains[1],
         grad_gelu,
         grad_linear,

time: 709 us -> 677 us (0.955)
  waiting for transfers between devices: 53.7 us -> 0.02 us
  Pallas kernels: 593 us -> 621 us
    psum x1, waiting for transfers between devices: 53.6 us -> 0.01 us  [body(): mlp_sums = lax.psum((grad_gelu, grad_linear, grad_down), 'dp')]
    pallas_call x1, Pallas kernels: 109 us -> 135 us  [input_back(): pl.pallas_call(functools.partial(input_back_kernel, n, copies), out_shape...]
  transfers between devices with their start and end apart: 2 -> 1, of which waited for: 1 -> 0; matrix products, arithmetic and copies ran while one was open for 4% -> 2% of each run, Pallas kernels for 36% -> 41%
where the time goes in v4:
time: 677 us; the launch traced here: 675 us
  Pallas kernels  621 us (92%)
  other arithmetic  22.7 us (3%)
  local copies, waits for them, and re-layouts  16.9 us (2%)
  between operations  14.2 us (2%)
    pallas_call x1, Pallas kernels, mlp(): pl.pallas_call(functools.partial(mlp_kernel, n), out_shape=(shape(n, rows...  144 us
    pallas_call x1, Pallas kernels, input_back(): pl.pallas_call(functools.partial(input_back_kernel, n, copies), out_shape...  135 us
    pallas_call x1, Pallas kernels, down(): pl.pallas_call(functools.partial(down_kernel, n), out_shape=(shape(rows,...  113 us
    pallas_call x1, Pallas kernels, mixer_out(): pl.pallas_call(functools.partial(mixer_out_kernel, n), out_shape=(shape(n...  108 us
    pallas_call x1, Pallas kernels, project(): pl.pallas_call(functools.partial(project_kernel, n), out_shape=(shape(n,...  72.5 us
    pallas_call x1, Pallas kernels, recur_back(): pl.pallas_call(recur_back_kernel, grid=(sequences, chunks), out_shape=(sh...  28.9 us
    pallas_call x1, Pallas kernels, recur_forward(): pl.pallas_call(recur_kernel, grid=(sequences, chunks), out_shape=(shape(t...  19.4 us
  transfers between devices with their start and end apart: 1, of which 0 were waited for; matrix products, arithmetic and copies ran while one was open for 2% of the time, Pallas kernels for 41%

profile of v4, /device:TPU:8, one launch (start us, length us, event | category | flops | bytes accessed | tf_op | source)
XLA Modules:
  0.0 674.8 jit_solution(15491385809444746133)
XLA Ops:
  7.9 1.2 broadcast_in_dim.18.decay
  9.1 0.8 broadcast_multiply_fusion.1
  10.5 1.3 broadcast_in_dim.16.gain
  11.8 1.3 broadcast_in_dim.19.gain
  13.1 1.4 copy_multiply_fusion.start_conv
  14.9 1.0 copy.34
  16.7 0.9 broadcast_multiply_fusion.gate_w
  17.6 72.5 %project.1 = (bf16[8,256,2048]{2,1,0:T(8,128)(2,1)}, f32[8,256,344]{2,1,0:T(8,128)}, f32[8,256,344]{2,1,0:T(8,128)}) custom-call(bf16[256,2048]{1,0:T(8,128)(2,1)} %tokens.5, bf16[1,2048]{1,0:T(2,128)(2,1)} %broadcast_in_dim.16.gain, bf16[344,2048]{1,0:T(8,128)(2,1)} %bitcast.27, bf16[344,2048]{1,0:T(8,128)(2,1)} %bitcast.29), custom_call_target="tpu_custom_call" | custom-call | flops 5771362304 | bytes 200000000 | tf_op jit(solution)/shard_map/project/pallas_call | solution.py:376
  90.1 19.4 %recur_forward.1 = (f32[2048,344]{1,0:T(8,128)}, bf16[2048,344]{1,0:T(8,128)(2,1)}, bf16[2048,344]{1,0:T(8,128)(2,1)}, f32[2048,344]{1,0:T(8,128)}, f32[2048,344...) custom-call(f32[2048,344]{1,0:T(8,128)} %bitcast.16, f32[2048,344]{1,0:T(8,128)} %bitcast.19, ...), custom_call_target="tpu_custom_call" | custom-call | tf_op jit(solution)/shard_map/recur_forward/pallas_call | solution.py:478
  109.5 107.7 %mixer_out.1 = (bf16[8,256,2048]{2,1,0:T(8,128)(2,1)}, f32[256,2048]{1,0:T(8,128)}, bf16[256,2048]{1,0:T(8,128)(2,1)}) custom-call(bf16[8,256,344]{2,1,0:T(8,128)(2,1)} %bitcast.25, bf16[344,2048]{1,0:T(8,128)(2,1)} %w_output.3, bf16[256,2048]{1,0:T(8,128)(2,1)} %cotangent.3, bf16[256,2048]{1,0:T(8,128)(2,1)} %tokens.5, bf16[1,2048]{1,0:T(2,128)(2,1)} %broadcast_in_dim.19.gain), custom_call_target="tpu_custom_call" | custom-call | flops 2885681152 | bytes 200000000 | tf_op jit(solution)/shard_map/mixer_out/pallas_call | solution.py:558
  217.2 144.3 %mlp.1 = (bf16[8,256,768]{2,1,0:T(8,128)(2,1)}, bf16[2048,768]{1,0:T(8,128)(2,1)}, bf16[2048,768]{1,0:T(8,128)(2,1)}, bf16[768,2048]{1,0:T(8,128)(2,1)}, f32[256...) custom-call(bf16[256,2048]{1,0:T(8,128)(2,1)} %get-tuple-element.55.normed, ...), custom_call_target="tpu_custom_call" | custom-call | flops 51539607552 | bytes 200000000 | tf_op jit(solution)/shard_map/mlp/pallas_call | solution.py:803
  363.5 112.5 %down.1 = (bf16[256,2048]{1,0:T(8,128)(2,1)}, f32[8,256,344]{2,1,0:T(8,128)}, bf16[344,2048]{1,0:T(8,128)(2,1)}) custom-call(bf16[8,256,768]{2,1,0:T(8,128)(2,1)} %get-tuple-element.58.hidden, bf16[768,2048]{1,0:T(8,128)(2,1)} %w_down.3, f32[256,2048]{1,0:T(8,128)} %get-tuple-element.57.residual, bf16[256,2048]{1,0:T(8,128)(2,1)} %get-tuple-element.59.g_low, ...), custom_call_target="tpu_custom_call" | custom-call | flops 12213813248 | bytes 200000000 | tf_op jit(solution)/shard_map/down/pallas_call | solution.py:883
  476.0 28.9 %recur_back.1 = (bf16[2048,344]{1,0:T(8,128)(2,1)}, bf16[2048,344]{1,0:T(8,128)(2,1)}, f32[8,344]{1,0:T(8,128)}, f32[2,344,344]{2,1,0:T(8,128)}) custom-call(f32[2048,344]{1,0:T(8,128)} %bitcast.21, f32[2048,344]{1,0:T(8,128)} %bitcast.20, f32[2048,344]{1,0:T(8,128)} %get-tuple-element.62.states.states_before, ...), custom_call_target="tpu_custom_call" | custom-call | tf_op jit(solution)/shard_map/recur_back/pallas_call | solution.py:1042
  504.9 135.4 %input_back.1 = (f32[256,2048]{1,0:T(8,128)}, bf16[344,2048]{1,0:T(8,128)(2,1)}, bf16[344,2048]{1,0:T(8,128)(2,1)}, bf16[344,2048]{1,0:T(8,128)(2,1)}, f32[2,2,1...) custom-call(bf16[2048,344]{1,0:T(8,128)(2,1)} %get-tuple-element.66.g_recur, ...), custom_call_target="tpu_custom_call" | custom-call | flops 11542724608 | bytes 200000000 | tf_op jit(solution)/shard_map/input_back/pallas_call | solution.py:1335
  640.4 2.7 copy.36
  643.1 3.2 convert_element_type.26
  646.9 1.3 fusion
  648.2 3.2 convert_bitcast_fusion
  651.5 5.2 convert_element_type.27
  656.7 3.2 convert_element_type.28
  659.9 3.6 convert_element_type.29
  663.5 1.0 copy.48
  664.5 1.0 copy-done.2
  665.4 1.3 copy.49
  (36 shorter events, 6.1 us)
Async XLA Ops:
  7.2 644.3 %all-reduce.3.cloned.1.call-start = ((), (), s32[]{:S(2)}) async-start(), calls=%async_computation | async-start | bytes 18874368 | tf_op jit(solution)/shard_map/psum | solution.py:1419
  361.6 0.7 copy-start.9
  361.6 1.3 copy-start.7
  640.4 5.9 copy-start.10
  640.4 7.9 %copy-start.3 = (bf16[344,2048]{1,0:T(8,128)(2,1)S(1)}, bf16[344,2048]{1,0:T(8,128)(2,1)}, u32[]{:S(2)}) copy-start(bf16[344,2048]{1,0:T(8,128)(2,1)} %get-tuple-element.78) | copy-start | bytes 4227076
  640.4 7.9 %copy-start.4 = (bf16[344,2048]{1,0:T(8,128)(2,1)S(1)}, bf16[344,2048]{1,0:T(8,128)(2,1)}, u32[]{:S(2)}) copy-start(bf16[344,2048]{1,0:T(8,128)(2,1)} %get-tuple-element.79) | copy-start | bytes 4227076
  651.5 5.2 copy-start.1
  656.7 3.2 copy-start
  659.9 3.6 copy-start.5
  663.5 2.0 copy-start.2
  663.5 3.3 copy-start.6
  663.5 3.9 copy-start.8
Sparse Core Ops, SparseCore 0:
  361.8 222.3 all-reduce.2

commit v5 on v4

--- a/solution.py
+++ b/solution.py
@@ -11,6 +11,8 @@
 KAPPA = 0.7978845608028654
 CUBIC = 0.044715
 PIECES = 2
+STRIPS = 4
+PARTS = 8
 F32 = jnp.float32
 BF16 = jnp.bfloat16
 ANY = pl.BlockSpec(memory_space=pl.ANY)
@@ -60,17 +62,21 @@
         self.has_up = self.j < self.nz - 1
         self.has_down = self.j > 0
 
-    def greet(self):
+    def greet(self, partners=()):
         barrier = pltpu.get_barrier_semaphore()
 
         def signal(t):
             pl.semaphore_signal(barrier, inc=1, device_id={"tensor": t}, device_id_type=MESH)
+
+        for i in partners:
+            pl.semaphore_signal(barrier, inc=1, device_id={"dp": i}, device_id_type=MESH)
 
         signal(self.sib)
         pl.when(self.has_up)(lambda: signal(self.t + 2))
         pl.when(self.has_down)(lambda: signal(self.t - 2))
         pl.semaphore_wait(
-            barrier, 1 + self.has_up.astype(jnp.int32) + self.has_down.astype(jnp.int32)
+            barrier,
+            1 + len(partners) + self.has_up.astype(jnp.int32) + self.has_down.astype(jnp.int32),
         )
 
     def copy(self, src, dst, send, recv, t):
@@ -185,8 +191,8 @@
             pltpu.VMEM((rows, width), F32),
             pltpu.SemaphoreType.DMA((nz,)),
             pltpu.SemaphoreType.DMA((nz,)),
-            pltpu.SemaphoreType.DMA((nz,)),
-            pltpu.SemaphoreType.DMA((nz + 1,)),
+            pltpu.SemaphoreType.DMA((nz, STRIPS)),
+            pltpu.SemaphoreType.DMA((nz + 1, STRIPS)),
         ]
 
     def sib_copy(self, k):
@@ -198,10 +204,14 @@
             self.place.sib,
         )
 
-    def line_copy(self, k, slot, to):
+    def line_copy(self, k, slot, p, to):
+        at = self.strip(p)
         return self.place.copy(
-            self.out.at[k], self.line.at[slot], self.line_send.at[k], self.line_recv.at[slot], to
+            self.out.at[k, at], self.line.at[slot, at], self.line_send.at[k, p], self.line_recv.at[slot, p], to
         )
+
+    def strip(self, p):
+        return span(p, self.acc.shape[0] // STRIPS)
 
     def offer(self, k):
         t = 2 * k + 1 - self.place.c
@@ -248,17 +258,23 @@
                 upstream = g.j - sign
                 more = jnp.logical_and(upstream >= 0, upstream < g.nz)
 
-                @pl.when(more)
-                def _():
-                    self.line_copy(k, k, g.sib).wait_recv()
-                    self.out[k] = (self.acc[...] + self.line[k].astype(F32)).astype(BF16)
-
-                @pl.when(jnp.logical_not(more))
-                def _():
-                    self.out[k] = self.acc[...].astype(BF16)
-
                 slot = jnp.where(jnp.logical_and(d == 1, w == 1), g.nz, k)
-                self.line_copy(k, slot, g.t + 2 * sign).start()
+
+                def pass_on(p):
+                    at = self.strip(p)
+
+                    @pl.when(more)
+                    def _():
+                        self.line_copy(k, k, p, g.sib).wait_recv()
+                        self.out[k, at] = (self.acc[at] + self.line[k, at].astype(F32)).astype(BF16)
+
+                    @pl.when(jnp.logical_not(more))
+                    def _():
+                        self.out[k, at] = self.acc[at].astype(BF16)
+
+                    self.line_copy(k, slot, p, g.t + 2 * sign).start()
+
+                loop(STRIPS, pass_on)
 
         loop(2, way_of)
 
@@ -266,24 +282,164 @@
         g = self.place
         self.pair(g.j)
 
-        @pl.when(g.has_down)
-        def _():
-            self.line_copy(g.j, g.j, g.sib).wait_recv()
-            self.acc[...] += self.line[g.j].astype(F32)
-
-        @pl.when(g.has_up)
-        def _():
-            self.line_copy(g.j, g.nz, g.sib).wait_recv()
-            self.acc[...] += self.line[g.nz].astype(F32)
+        def take(p):
+            at = self.strip(p)
+
+            @pl.when(g.has_down)
+            def _():
+                self.line_copy(g.j, g.j, p, g.sib).wait_recv()
+                self.acc[at] += self.line[g.j, at].astype(F32)
+
+            @pl.when(g.has_up)
+            def _():
+                self.line_copy(g.j, g.nz, p, g.sib).wait_recv()
+                self.acc[at] += self.line[g.nz, at].astype(F32)
+
+        loop(STRIPS, take)
 
     def finish(self):
         g = self.place
 
         def done(k):
             self.sib_copy(k).wait_send()
-            pl.when(g.j != k)(lambda: self.line_copy(k, k, g.sib).wait_send())
+            pl.when(g.j != k)(
+                lambda: loop(STRIPS, lambda p: self.line_copy(k, k, p, g.sib).wait_send())
+            )
 
         loop(g.nz, done)
+
+
+class Halving:
+    def __init__(self, me, count, data, landed, final, sems):
+        self.me, self.count = me, count
+        self.data, self.landed, self.final = data, landed, final
+        self.out_send, self.out_recv, self.back_send, self.back_recv = (sems.at[q] for q in range(4))
+        self.bits = count.bit_length() - 1
+        assert count == 1 << self.bits
+
+    @staticmethod
+    def scratch(count, rows, columns):
+        return [
+            pltpu.VMEM((2, count, 1, rows, columns), BF16),
+            pltpu.VMEM((2, count - 1, 1, rows, columns), BF16),
+            pltpu.VMEM((2, count, 1, rows, columns), BF16),
+            pltpu.SemaphoreType.DMA((4, 2, count - 1)),
+        ]
+
+    @staticmethod
+    def over(me, count, data, landed, final, sems):
+        def at(ref):
+            return lambda track, index: ref.at[track, index]
+
+        return Halving(me, count, at(data), at(landed), at(final), sems)
+
+    def partners(self):
+        return [self.me + (1 - 2 * self.own(b)) * (1 << b) for b in range(self.bits)]
+
+    def own(self, bit):
+        return lax.rem(lax.div(self.me, 1 << bit), 2)
+
+    def swaps(self, s):
+        for track in (0, 1):
+            order = [(i + track) % self.bits for i in range(self.bits)]
+            bit = order[s]
+            partner = self.me + (1 - 2 * self.own(bit)) * (1 << bit)
+            fixed = sum(self.own(b) * (1 << b) for b in order[:s])
+            for u in range(self.count >> (s + 1)):
+                free = sum(((u >> i) & 1) << b for i, b in enumerate(order[s + 1 :]))
+                slot = self.count - (self.count >> s) + u
+                kept = fixed + free + self.own(bit) * (1 << bit)
+                yield track, slot, partner, fixed + free + (1 - self.own(bit)) * (1 << bit), kept
+
+    def out(self, track, slot, partner, given):
+        return pltpu.make_async_remote_copy(
+            src_ref=self.data(track, given),
+            dst_ref=self.landed(track, slot),
+            send_sem=self.out_send.at[track, slot],
+            recv_sem=self.out_recv.at[track, slot],
+            device_id={"dp": partner},
+            device_id_type=MESH,
+        )
+
+    def back(self, track, slot, partner, segment):
+        return pltpu.make_async_remote_copy(
+            src_ref=self.final(track, segment),
+            dst_ref=self.final(track, segment),
+            send_sem=self.back_send.at[track, slot],
+            recv_sem=self.back_recv.at[track, slot],
+            device_id={"dp": partner},
+            device_id_type=MESH,
+        )
+
+    def start(self, s=0):
+        for track, slot, partner, given, _ in self.swaps(s):
+            self.out(track, slot, partner, given).start()
+
+    def turn(self, s):
+        for track, slot, partner, given, kept in self.swaps(s):
+            self.out(track, slot, partner, given).wait_recv()
+            mine, theirs = self.data(track, kept), self.landed(track, slot)
+            result = self.final(track, kept) if s == self.bits - 1 else mine
+            blocks, rows, _ = mine.shape
+            tile = tile_of(rows, 32)
+
+            def add(r):
+                block, at = lax.div(r, rows // tile), span(lax.rem(r, rows // tile), tile)
+                result[block, at] = (mine[block, at].astype(F32) + theirs[block, at].astype(F32)).astype(BF16)
+
+            loop(blocks * (rows // tile), add)
+        if s < self.bits - 1:
+            self.start(s + 1)
+        else:
+            self.start_back(s)
+
+    def start_back(self, s):
+        for track, slot, partner, _, kept in self.swaps(s):
+            self.back(track, slot, partner, kept).start()
+
+    def turn_back(self, s):
+        for track, slot, partner, given, _ in self.swaps(s):
+            self.back(track, slot, partner, given).wait_recv()
+        if s > 0:
+            self.start_back(s - 1)
+
+    def events(self):
+        steps = [functools.partial(self.turn, s) for s in range(self.bits)]
+        return steps + [functools.partial(self.turn_back, s) for s in range(self.bits - 1, 0, -1)]
+
+    def finish(self):
+        self.turn_back(0)
+        for s in range(self.bits):
+            for track, slot, partner, given, kept in self.swaps(s):
+                self.out(track, slot, partner, given).wait_send()
+                self.back(track, slot, partner, kept).wait_send()
+
+
+def fetching(kernel, which):
+    def wrapped(*refs):
+        refs = list(refs)
+        sems = refs.pop()
+        kept = refs[len(refs) - len(which) :]
+        del refs[len(refs) - len(which) :]
+        copies = {}
+        for q, i in enumerate(which):
+            copies[i] = pltpu.make_async_copy(refs[i], kept[q], sems.at[q])
+            copies[i].start()
+            refs[i] = kept[q]
+
+        def arrive(*wanted):
+            for i in wanted:
+                copies[i].wait()
+
+        return kernel(arrive, *refs)
+
+    return wrapped
+
+
+def fetched_specs(inputs, which, plain=()):
+    specs = [ANY if i in which or i in plain else VM for i in range(len(inputs))]
+    scratch = [pltpu.VMEM(inputs[i].shape, inputs[i].dtype) for i in which]
+    return specs, scratch + [pltpu.SemaphoreType.DMA((len(which),))]
 
 
 def comm_params(collective_id):
@@ -332,7 +488,7 @@
     return jnp.where(m < 0.35, series, 1.0 - decay * decay)
 
 
-def project_kernel(n, tokens, gain, w_in, w_br, normed, recur, branch, full, sent, came, held_a, held_b, saved):
+def project_kernel(n, arrive, tokens, gain, w_in, w_br, normed, recur, branch, full, sent, came, held_a, held_b, saved):
     g = Place(n)
     gather = Gather(g, full, sent, came)
     part = 64
@@ -345,6 +501,7 @@
     loop(full.shape[1] // part, normalize)
     g.greet()
     gather.start()
+    arrive(2, 3)
 
     def use(t):
         pltpu.make_async_copy(full.at[t], normed.at[t], saved.at[t, 0]).start()
@@ -373,22 +530,25 @@
 def project(n, tokens, gain, w_in, w_br):
     rows, width = tokens.shape
     channels = w_in.shape[0]
+    inputs = (tokens, gain, w_in, w_br)
+    specs, kept = fetched_specs(inputs, (2, 3))
     return pl.pallas_call(
-        functools.partial(project_kernel, n),
+        fetching(functools.partial(project_kernel, n), (2, 3)),
         out_shape=(
             shape(n, rows, width, dtype=BF16),
             shape(n, rows, channels),
             shape(n, rows, channels),
         ),
-        in_specs=[VM] * 4,
+        in_specs=specs,
         out_specs=(ANY,) * 3,
         scratch_shapes=Gather.scratch(n, rows, width)
         + [pltpu.VMEM((n, rows, channels), F32)] * 2
-        + [pltpu.SemaphoreType.DMA((n, 3))],
+        + [pltpu.SemaphoreType.DMA((n, 3))]
+        + kept,
         compiler_params=comm_params(1),
         cost_estimate=cost(4 * n * rows * width * channels),
         name="project",
-    )(tokens, gain, w_in, w_br)
+    )(*inputs)
 
 
 def recur_kernel(
@@ -514,20 +674,23 @@
 
 
 def mixer_out_kernel(
-    n, mixture, w_output, cotangent, tokens, gain, cot_full, residual, normed,
+    n, arrive, mixture, w_output, cotangent, tokens, gain, cot_full, residual, normed,
     full, sent, came, saved, *bufs
 ):
     g = Place(n)
     gather = Gather(g, full, sent, came)
     scatter = Scatter(g, lambda t, cols: dot(mixture[t], w_output[:, cols]), tile_of(residual.shape[1], 512), bufs)
-    full[g.t] = cotangent[...]
+    first = pltpu.make_async_copy(cotangent, full.at[g.t], saved.at[0])
+    first.start()
     g.greet()
+    first.wait()
+    gather.start()
+    arrive(0, 1)
 
     def use(t):
         pltpu.make_async_copy(full.at[t], cot_full.at[t], saved.at[t]).start()
 
     scatter.offers(g.nz - 1)
-    gather.start()
 
     def around(i):
         d = g.nz - 1 - i
@@ -538,6 +701,7 @@
 
     loop(g.nz - 1, around)
     scatter.last()
+    arrive(3)
     part = 64
 
     def rows_of(i):
@@ -555,32 +719,32 @@
 
 def mixer_out(n, mixture, w_output, cotangent, tokens, gain):
     rows, width = tokens.shape
+    inputs, which = (mixture, w_output, cotangent, tokens, gain), (0, 1, 3)
+    specs, kept = fetched_specs(inputs, which, (2,))
     return pl.pallas_call(
-        functools.partial(mixer_out_kernel, n),
+        fetching(functools.partial(mixer_out_kernel, n), which),
         out_shape=(
             shape(n, rows, width, dtype=BF16),
             shape(rows, width),
             shape(rows, width, dtype=BF16),
         ),
-        in_specs=[VM] * 5,
+        in_specs=specs,
         out_specs=(ANY, VM, VM),
         scratch_shapes=Gather.scratch(n, rows, width)
         + [pltpu.SemaphoreType.DMA((n,))]
-        + Scatter.scratch(n, rows, width),
+        + Scatter.scratch(n, rows, width)
+        + kept,
         compiler_params=comm_params(2),
         cost_estimate=cost(2 * n * rows * width * mixture.shape[-1]),
         name="mixer_out",
-    )(mixture, w_output, cotangent, tokens, gain)
-
-
-PARTS = 8
+    )(*inputs)
 
 
 def mlp_kernel(
-    n, normed, cot_full, w_gelu, w_linear, w_down, residual, cotangent, gain,
+    n, copies, arrive, normed, cot_full, w_gelu, w_linear, w_down, residual, gain,
     hidden, grad_gelu, grad_linear, grad_down, g_residual, g_low, g_gain,
     full, sent, came, cot, keep_h, keep_f, keep_s, acc_g, acc_l, acc_d,
-    to_sib, sums, line, acc, saved, fetched, drained, sib_sent, sib_came, line_sent, line_came,
+    to_sib, sums, line, acc, landed, swap_sems, saved, fetched, drained, sib_sent, sib_came, line_sent, line_came,
 ):
     g = Place(n)
     gather = Gather(g, full, sent, came)
@@ -589,15 +753,35 @@
     tile = tile_of(columns, 256)
     wide = tile_of(width, 512)
     strip = rows // PARTS
-    full[g.t] = normed[...]
-    g.greet()
+    me = lax.axis_index("dp")
+    start = pltpu.make_async_copy(normed, full.at[g.t], saved.at[0])
+    start.start()
+    part_width = width // (2 * copies)
+    depth = columns // rows
+
+    def segment(track, index):
+        return pl.ds(pl.multiple_of((track * copies + index) * part_width, part_width), part_width)
+
+    swap = Halving(
+        me,
+        copies,
+        lambda track, index: full.at[0:depth, :, segment(track, index)],
+        lambda track, slot: landed.at[track, slot],
+        lambda track, index: full.at[depth : 2 * depth, :, segment(track, index)],
+        swap_sems,
+    )
+    def fetch(t, q):
+        return pltpu.make_async_copy(cot_full.at[t], cot.at[q], fetched.at[q])
+
+    g.greet(swap.partners())
+    start.wait()
     gather.start()
+    fetch(2 * g.j, 0).start()
+    fetch(2 * g.j + 1, 1).start()
+    arrive(2, 3, 4)
     acc_g[...] = jnp.zeros_like(acc_g)
     acc_l[...] = jnp.zeros_like(acc_l)
     acc_d[...] = jnp.zeros_like(acc_d)
-
-    def fetch(t, q):
-        return pltpu.make_async_copy(cot_full.at[t], cot.at[q], fetched.at[q])
 
     def save(t, q):
         return pltpu.make_async_copy(keep_h.at[q], hidden.at[t], saved.at[q])
@@ -634,8 +818,6 @@
         k = g.j + way * d
         mine, its = g.c, 1 - g.c
         own, other = 2 * k + mine, 2 * k + its
-        fetch(other, its).start()
-        fetch(own, mine).start()
         for p in range(gather.pieces):
             gather.copy(other, p, 2, g.sib).wait_recv()
         layer(other, its)
@@ -685,10 +867,20 @@
             )
 
         loop(width // wide, part)
+        both_ways = jnp.logical_and(g.j + d < g.nz, g.j - d >= 0)
+        again = jnp.logical_and(both_ways, jnp.logical_and(way > 0, d > 0))
+        later = jnp.where(g.j + d + 1 < g.nz, g.j + d + 1, g.j - d - 1)
+        following = jnp.where(again, g.j - d, later)
+
+        @pl.when(following >= 0)
+        def _():
+            fetch(2 * following, 0).start()
+            fetch(2 * following + 1, 1).start()
+
         save(other, its).wait()
         save(own, mine).wait()
 
-    def relay(m):
+    def relay(m, events=()):
         def take(k, slot, sign, p):
             at = pl.ds(pl.multiple_of(p * strip, strip), strip)
             line_copy(k, slot, p, g.sib).wait_recv()
@@ -725,9 +917,14 @@
                 pl.when(lower)(lambda: fall(i - 1))
                 pl.when(jnp.logical_not(lower))(lambda: rise(i - 1))
 
-        loop(PARTS + 1, strips)
-
-    def step(d):
+        def between(i):
+            strips(i)
+            for q, event in enumerate(events):
+                pl.when(i == (q + 1) * PARTS // len(events))(event)
+
+        loop(PARTS + 1, between)
+
+    def cores(d):
         up, down = g.j + d < g.nz, g.j - d >= 0
 
         def way_of(w):
@@ -742,10 +939,22 @@
                     pl.when(w == min(p, 1))(lambda: gather.forward(d + 1, (p,)))
 
         loop(2, way_of)
+
+    def step(d):
+        @pl.when(d < g.nz)
+        def _():
+            cores(d)
+
+        @pl.when(d == g.nz - 1)
+        def _():
+            gather.finish()
+            for i in range(depth):
+                full[i] = acc_d[pl.ds(i * rows, rows)].astype(BF16)
+            swap.start()
+
         pl.when(d > 1)(lambda: relay(d - 1))
 
     loop(g.nz, step)
-    gather.finish()
 
     stages = [held.at[q] for held in (keep_h, keep_f, keep_s) for q in (0, 1)]
     leaving = []
@@ -759,31 +968,40 @@
         copy.start()
         leaving.append(copy)
 
-    count = width // rows
-    for i in range(count):
+    for i in range(width // rows):
         at = pl.ds(i * rows, rows)
         leave(2 * i, acc_g[at], grad_gelu.at[at])
         leave(2 * i + 1, acc_l[at], grad_linear.at[at])
-    wider = []
-    for i in range(columns // rows):
-        at = pl.ds(i * rows, rows)
-        full[i] = acc_d[at].astype(BF16)
-        wider.append(pltpu.make_async_copy(full.at[i], grad_down.at[at], drained.at[len(stages) + i]))
-        wider[-1].start()
-    relay(g.nz - 1)
+    events = swap.events()
+    events.pop(0)()
+    relay(g.nz - 1, events)
+    own = pltpu.make_async_copy(cot_full.at[g.t], cot.at[0], fetched.at[0])
+    own.start()
+    own.wait()
+    arrive(5)
     lines = 32
     g_gain[...] = jnp.zeros_like(g_gain)
 
     def rows_of(i):
         at = span(i, lines)
         back, terms = norm_grad(residual[at], gain[...].astype(F32), acc[at])
-        value = cotangent[at].astype(F32) + back
-        g_residual[at] = value
-        g_low[at] = value.astype(BF16)
+        value = cot[0, at].astype(F32) + back
+        acc[at] = value
+        cot[1, at] = value.astype(BF16)
         g_gain[...] += jnp.sum(terms, axis=0, keepdims=True)
 
     loop(rows // lines, rows_of)
-    for copy in leaving[-len(stages):] + wider:
+    last = [
+        pltpu.make_async_copy(acc, g_residual, saved.at[0]),
+        pltpu.make_async_copy(cot.at[1], g_low, saved.at[1]),
+    ]
+    swap.finish()
+    for i in range(depth):
+        at = pl.ds(i * rows, rows)
+        last.append(pltpu.make_async_copy(full.at[depth + i], grad_down.at[at], drained.at[len(stages) + i]))
+    for copy in last:
+        copy.start()
+    for copy in leaving[-len(stages) :] + last:
         copy.wait()
 
     def done(k):
@@ -795,13 +1013,15 @@
     loop(g.nz, done)
 
 
-def mlp(n, normed, cot_full, w_gelu, w_linear, w_down, residual, cotangent, gain):
+def mlp(n, copies, normed, cot_full, w_gelu, w_linear, w_down, residual, gain):
     rows, width = normed.shape
     columns = w_gelu.shape[1]
     kept = pltpu.VMEM((2, rows, columns), BF16)
     sems = pltpu.SemaphoreType.DMA
+    inputs, which = (normed, cot_full, w_gelu, w_linear, w_down, residual, gain), (2, 3, 4, 5)
+    specs, held = fetched_specs(inputs, which, (0, 1))
     return pl.pallas_call(
-        functools.partial(mlp_kernel, n),
+        fetching(functools.partial(mlp_kernel, n, copies), which),
         out_shape=(shape(n, rows, columns, dtype=BF16),)
         + (shape(width, columns, dtype=BF16),) * 2
         + (
@@ -810,8 +1030,8 @@
             shape(rows, width, dtype=BF16),
             shape(1, width),
         ),
-        in_specs=[VM, ANY] + [VM] * 6,
-        out_specs=(ANY,) * 4 + (VM,) * 3,
+        in_specs=specs,
+        out_specs=(ANY,) * 6 + (VM,),
         scratch_shapes=Gather.scratch(n, rows, width)
         + [pltpu.VMEM((2, rows, width), BF16)]
         + [kept] * 3
@@ -822,6 +1042,8 @@
             pltpu.VMEM((n // 2, rows, width), BF16),
             pltpu.VMEM((n // 2 + 1, rows, width), BF16),
             pltpu.VMEM((rows, width), F32),
+            pltpu.VMEM((2, copies - 1, columns // rows, rows, width // (2 * copies)), BF16),
+            sems((4, 2, copies - 1)),
             sems((2,)),
             sems((2,)),
             sems((6 + columns // rows,)),
@@ -829,24 +1051,27 @@
             sems((n // 2,)),
             sems((n // 2, PARTS)),
             sems((n // 2 + 1, PARTS)),
-        ],
+        ]
+        + held,
         compiler_params=comm_params(3),
         cost_estimate=cost(16 * n * rows * width * columns),
         name="mlp",
-    )(normed, cot_full, w_gelu, w_linear, w_down, residual, cotangent, gain)
+    )(*inputs)
 
 
 def down_kernel(
-    n, hidden, w_down, residual, g_low, w_output, mixture, output, g_mixture, grad_output,
-    full, sent, came, acc_o, *bufs
+    n, arrive, hidden, w_down, residual, g_low, w_output, mixture, output, g_mixture, grad_output,
+    full, sent, came, acc_o, start_sem, *bufs
 ):
     g = Place(n)
     gather = Gather(g, full, sent, came)
     width = residual.shape[1]
     wide = tile_of(width, 512)
     scatter = Scatter(g, lambda t, cols: dot(hidden[t], w_down[:, cols]), wide, bufs)
-    full[g.t] = g_low[...]
+    first = pltpu.make_async_copy(g_low, full.at[g.t], start_sem)
+    first.start()
     g.greet()
+    first.wait()
 
     def use(t):
         g_mixture[t] = dot_nt(full[t], w_output[...])
@@ -859,7 +1084,9 @@
 
     gather.start()
     acc_o[...] = jnp.zeros_like(acc_o)
+    arrive(0, 1)
     scatter.offers(g.nz - 1)
+    arrive(4, 5)
 
     def around(i):
         d = g.nz - 1 - i
@@ -872,6 +1099,7 @@
     gather.each(g.nz - 1, use)
     grad_output[...] = acc_o[...].astype(BF16)
     scatter.last()
+    arrive(2)
     output[...] = (scatter.acc[...] + residual[...]).astype(BF16)
     scatter.finish()
     gather.finish()
@@ -880,22 +1108,25 @@
 def down(n, hidden, w_down, residual, g_low, w_output, mixture):
     rows, width = residual.shape
     channels = w_output.shape[0]
+    inputs, which = (hidden, w_down, residual, g_low, w_output, mixture), (0, 1, 4, 5, 2)
+    specs, kept = fetched_specs(inputs, which, (3,))
     return pl.pallas_call(
-        functools.partial(down_kernel, n),
+        fetching(functools.partial(down_kernel, n), which),
         out_shape=(
             shape(rows, width, dtype=BF16),
             shape(n, rows, channels),
             shape(channels, width, dtype=BF16),
         ),
-        in_specs=[VM] * 6,
+        in_specs=specs,
         out_specs=(VM,) * 3,
         scratch_shapes=Gather.scratch(n, rows, width)
-        + [pltpu.VMEM((channels, width), F32)]
-        + Scatter.scratch(n, rows, width),
+        + [pltpu.VMEM((channels, width), F32), pltpu.SemaphoreType.DMA]
+        + Scatter.scratch(n, rows, width)
+        + kept,
         compiler_params=comm_params(5),
         cost_estimate=cost(2 * n * rows * width * (hidden.shape[-1] + 2 * channels)),
         name="down",
-    )(hidden, w_down, residual, g_low, w_output, mixture)
+    )(*inputs)
 
 
 def recur_back_kernel(
@@ -1070,105 +1301,8 @@
     )(g_mix, branch, states, states, u, u, conv_low, recall, ingate, start_state, start_conv, conv, gate_w, decay)
 
 
-class Halving:
-    def __init__(self, me, count, data, landed, final, sems):
-        self.me, self.count = me, count
-        self.data, self.landed, self.final = data, landed, final
-        self.out_send, self.out_recv, self.back_send, self.back_recv = (sems.at[q] for q in range(4))
-        self.bits = count.bit_length() - 1
-        assert count == 1 << self.bits
-
-    @staticmethod
-    def scratch(count, rows, columns):
-        slots = max(count - 1, 1)
-        return [
-            pltpu.VMEM((2, count, rows, columns), BF16),
-            pltpu.VMEM((2, slots, rows, columns), BF16),
-            pltpu.VMEM((2, count, rows, columns), BF16),
-            pltpu.SemaphoreType.DMA((4, 2, slots)),
-        ]
-
-    def own(self, bit):
-        return lax.rem(lax.div(self.me, 1 << bit), 2)
-
-    def swaps(self, s):
-        for track in (0, 1):
-            order = [(i + track) % self.bits for i in range(self.bits)]
-            bit = order[s]
-            partner = self.me + (1 - 2 * self.own(bit)) * (1 << bit)
-            fixed = sum(self.own(b) * (1 << b) for b in order[:s])
-            for u in range(self.count >> (s + 1)):
-                free = sum(((u >> i) & 1) << b for i, b in enumerate(order[s + 1 :]))
-                slot = self.count - (self.count >> s) + u
-                kept = fixed + free + self.own(bit) * (1 << bit)
-                yield track, slot, partner, fixed + free + (1 - self.own(bit)) * (1 << bit), kept
-
-    def out(self, track, slot, partner, given):
-        return pltpu.make_async_remote_copy(
-            src_ref=self.data.at[track, given],
-            dst_ref=self.landed.at[track, slot],
-            send_sem=self.out_send.at[track, slot],
-            recv_sem=self.out_recv.at[track, slot],
-            device_id={"dp": partner},
-            device_id_type=MESH,
-        )
-
-    def back(self, track, slot, partner, segment):
-        return pltpu.make_async_remote_copy(
-            src_ref=self.final.at[track, segment],
-            dst_ref=self.final.at[track, segment],
-            send_sem=self.back_send.at[track, slot],
-            recv_sem=self.back_recv.at[track, slot],
-            device_id={"dp": partner},
-            device_id_type=MESH,
-        )
-
-    def start(self, s=0):
-        for track, slot, partner, given, _ in self.swaps(s):
-            self.out(track, slot, partner, given).start()
-
-    def turn(self, s):
-        rows = self.data.shape[2]
-        tile = tile_of(rows, 32)
-        for track, slot, partner, given, kept in self.swaps(s):
-            self.out(track, slot, partner, given).wait_recv()
-            result = self.final if s == self.bits - 1 else self.data
-
-            def add(r):
-                at = span(r, tile)
-                value = self.data[track, kept, at].astype(F32) + self.landed[track, slot, at].astype(F32)
-                result[track, kept, at] = value.astype(BF16)
-
-            loop(rows // tile, add)
-        if s < self.bits - 1:
-            self.start(s + 1)
-        else:
-            self.start_back(s)
-
-    def start_back(self, s):
-        for track, slot, partner, _, kept in self.swaps(s):
-            self.back(track, slot, partner, kept).start()
-
-    def turn_back(self, s):
-        for track, slot, partner, given, _ in self.swaps(s):
-            self.back(track, slot, partner, given).wait_recv()
-        if s > 0:
-            self.start_back(s - 1)
-
-    def events(self):
-        steps = [functools.partial(self.turn, s) for s in range(self.bits)]
-        return steps + [functools.partial(self.turn_back, s) for s in range(self.bits - 1, 0, -1)]
-
-    def finish(self):
-        self.turn_back(0)
-        for s in range(self.bits):
-            for track, slot, partner, given, kept in self.swaps(s):
-                self.out(track, slot, partner, given).wait_send()
-                self.back(track, slot, partner, kept).wait_send()
-
-
 def input_back_kernel(
-    n, copies, g_recur, g_branch, w_in, w_br, normed, tokens, g_residual, gain, second_gain, g_gates, small, g_out,
+    n, copies, arrive, g_recur, g_branch, w_in, w_br, normed, tokens, g_residual, gain, second_gain, g_gates, small, g_out,
     input_grad, in_out, br_out, out_out, gates_out, conv_out, bias_out, decay_out, gains_out,
     gain_row, gain_parts, gain_in, gain_sum, gain_dp, gain_sent, gain_came, gain_dp_sent, gain_dp_came, *bufs
 ):
@@ -1179,10 +1313,10 @@
     blocks, block_width = gates_out.shape[1], gates_out.shape[2]
     segment = width // (2 * copies)
     gain_width = width // n
-    weights = Halving(me, copies, *bufs[:4])
-    rest = Halving(me, copies, *bufs[4:8])
-    padded = bufs[0].shape[2] // 3
-    rest_rows = bufs[4].shape[2]
+    weights = Halving.over(me, copies, *bufs[:4])
+    rest = Halving.over(me, copies, *bufs[4:8])
+    padded = bufs[0].shape[3] // 3
+    rest_rows = bufs[4].shape[3]
 
     def block(ref, t):
         return ref[span(t, rows)]
@@ -1218,6 +1352,7 @@
     copies_of(lambda i: pl.semaphore_signal(barrier, inc=1, device_id={"dp": i}, device_id_type=MESH))
     pl.semaphore_wait(barrier, n - 1 + copies - 1)
 
+    arrive(0, 1, 2, 3)
     scatter.offers(g.nz - 1)
 
     def around(i):
@@ -1226,6 +1361,7 @@
         scatter.step(d)
 
     around(0)
+    arrive(4, 11, 9)
 
     data = bufs[0]
 
@@ -1239,9 +1375,9 @@
             track, part = lax.div(index, copies), lax.rem(index, copies)
             for i, value in enumerate((first, second, third)):
                 piece = value[:, half * segment : (half + 1) * segment].astype(BF16)
-                data[track, part, i * padded : i * padded + channels] = piece
+                data[track, part, 0, i * padded : i * padded + channels] = piece
                 if padded > channels:
-                    data[track, part, i * padded + channels : (i + 1) * padded] = jnp.zeros(
+                    data[track, part, 0, i * padded + channels : (i + 1) * padded] = jnp.zeros(
                         (padded - channels, segment), BF16
                     )
         terms = jnp.sum(w_in[:, cols].astype(F32) * first + w_br[:, cols].astype(F32) * second, axis=0, keepdims=True)
@@ -1266,7 +1402,7 @@
         axis=0,
     ).astype(BF16)
     for i in range(2 * copies):
-        bufs[4][i // copies, i % copies] = flat[i * rest_rows : (i + 1) * rest_rows]
+        bufs[4][i // copies, i % copies, 0] = flat[i * rest_rows : (i + 1) * rest_rows]
     rest.start()
 
     events = [lambda a=a, b=b: (a(), b()) for a, b in zip(weights.events(), rest.events())]
@@ -1285,6 +1421,7 @@
     for event in events:
         event()
     scatter.last()
+    arrive(5, 6)
     part = 32
 
     def rows_of(i):
@@ -1299,7 +1436,7 @@
         total = total + gain_dp[i]
     gains_out[...] = total
     rest.finish()
-    flat = jnp.concatenate([bufs[6][i // copies, i % copies].astype(F32) for i in range(2 * copies)], axis=0)
+    flat = jnp.concatenate([bufs[6][i // copies, i % copies, 0].astype(F32) for i in range(2 * copies)], axis=0)
     for q in (0, 1):
         for i in range(blocks):
             start = q * channels + i * block_width
@@ -1311,7 +1448,7 @@
     for i in range(2 * copies):
         for q, out in enumerate((in_out, br_out, out_out)):
             out[:, i * segment : (i + 1) * segment] = bufs[2][
-                i // copies, i % copies, q * padded : q * padded + channels
+                i // copies, i % copies, 0, q * padded : q * padded + channels
             ]
     others(lambda t: gain_copy(t, t).wait_send())
     copies_of(lambda i: gain_dp_copy(i, i).wait_send())
@@ -1332,8 +1469,11 @@
     rest_rows = up_to((2 * channels + 8 + 2 * copies - 1) // (2 * copies), 16)
     gain_shape = (8, width // n)
     sems = pltpu.SemaphoreType.DMA
+    inputs = (g_recur, g_branch, w_in, w_br, normed, tokens, g_residual, gain, second_gain, g_gates, small, g_out)
+    which = (0, 1, 2, 3, 4, 11, 9, 5, 6)
+    specs, kept = fetched_specs(inputs, which)
     return pl.pallas_call(
-        functools.partial(input_back_kernel, n, copies),
+        fetching(functools.partial(input_back_kernel, n, copies), which),
         out_shape=(shape(rows, width),)
         + (shape(channels, width, dtype=BF16),) * 3
         + (
@@ -1343,7 +1483,7 @@
             shape(1, channels),
             shape(*gain_shape),
         ),
-        in_specs=[VM] * 12,
+        in_specs=specs,
         out_specs=(VM,) * 9,
         scratch_shapes=[
             pltpu.VMEM((8, width), F32),
@@ -1358,11 +1498,12 @@
         ]
         + Halving.scratch(copies, 3 * up_to(channels, 16), width // (2 * copies))
         + Halving.scratch(copies, rest_rows, channels)
-        + Scatter.scratch(n, rows, width),
+        + Scatter.scratch(n, rows, width)
+        + kept,
         compiler_params=comm_params(6),
         cost_estimate=cost(8 * n * rows * width * channels),
         name="input_back",
-    )(g_recur, g_branch, w_in, w_br, normed, tokens, g_residual, gain, second_gain, g_gates, small, g_out)
+    )(*inputs)
 
 
 def body(
@@ -1414,9 +1555,9 @@
     mixture = blocked(mixture)
     cot_full, residual, normed_mlp = mixer_out(n, mixture, w_output, cotangent, tokens, gain_second)
     hidden, grad_gelu, grad_linear, grad_down, g_residual, g_low, gain_second_grad = mlp(
-        n, normed_mlp, cot_full, w_gelu, w_linear, w_down, residual, cotangent, gain_second
+        n, copies, normed_mlp, cot_full, w_gelu, w_linear, w_down, residual, gain_second
     )
-    mlp_sums = lax.psum((grad_gelu, grad_linear, grad_down), "dp")
+    mlp_sums = lax.psum((grad_gelu, grad_linear), "dp")
     output, g_mixture, grad_output = down(n, hidden, w_down, residual, g_low, w_output, mixture)
     g_recur, g_branch, small, g_gates = recur_back(
         flat(g_mixture), branch, states, recur, conv_low, recall, ingate, start_state, start_conv,
@@ -1426,7 +1567,8 @@
         n, copies, g_recur, g_branch, w_in, w_br, flat(normed), tokens, g_residual, gain_first,
         gain_second_grad, g_gates, small, grad_output, blocks,
     )
-    grad_gelu, grad_linear, grad_down = (x.astype(F32) for x in mlp_sums)
+    grad_gelu, grad_linear = (x.astype(F32) for x in mlp_sums)
+    grad_down = grad_down.astype(F32)
     return (
         output,
         input_grad,

time: 677 us -> 659 us (0.973)
  Pallas kernels: 621 us -> 605 us
    pallas_call x5, Pallas kernels: 573 us -> 556 us  [the longest x1 164 us: mlp(): pl.pallas_call(fetching(functools.partial(mlp_kernel, n, copies), which),...]
  transfers between devices with their start and end apart: 1 -> 1, of which waited for: 0 -> 0; matrix products, arithmetic and copies ran while one was open for 2% -> 2% of each run, Pallas kernels for 41% -> 37%
where the time goes in v5:
time: 659 us; the launch traced here: 658 us
  Pallas kernels  605 us (92%)
  other arithmetic  22.7 us (3%)
  local copies, waits for them, and re-layouts  16.9 us (3%)
  between operations  14.2 us (2%)
    pallas_call x1, Pallas kernels, mlp(): pl.pallas_call(fetching(functools.partial(mlp_kernel, n, copies), which),...  164 us
    pallas_call x1, Pallas kernels, input_back(): pl.pallas_call(fetching(functools.partial(input_back_kernel, n, copies),...  109 us
    pallas_call x1, Pallas kernels, down(): pl.pallas_call(fetching(functools.partial(down_kernel, n), which), out_sh...  106 us
    pallas_call x1, Pallas kernels, mixer_out(): pl.pallas_call(fetching(functools.partial(mixer_out_kernel, n), which), o...  105 us
    pallas_call x1, Pallas kernels, project(): pl.pallas_call(fetching(functools.partial(project_kernel, n), (2, 3)), ou...  71.6 us
    pallas_call x1, Pallas kernels, recur_back(): pl.pallas_call(recur_back_kernel, grid=(sequences, chunks), out_shape=(sh...  29 us
    pallas_call x1, Pallas kernels, recur_forward(): pl.pallas_call(recur_kernel, grid=(sequences, chunks), out_shape=(shape(t...  19.4 us
  transfers between devices with their start and end apart: 1, of which 0 were waited for; matrix products, arithmetic and copies ran while one was open for 2% of the time, Pallas kernels for 37%

profile of v5, /device:TPU:8, one launch (start us, length us, event | category | flops | bytes accessed | tf_op | source)
XLA Modules:
  0.0 658.4 jit_solution(13466899495324203321)
XLA Ops:
  7.9 1.2 broadcast_in_dim.18.decay
  9.1 0.8 broadcast_multiply_fusion.1
  10.5 1.3 broadcast_in_dim.16.refs_1_.refs_7_
  11.8 1.3 broadcast_in_dim.19.refs_4_.refs_6_
  13.1 1.4 copy_multiply_fusion.start_conv
  14.9 1.0 copy.34
  16.7 0.9 broadcast_multiply_fusion.gate_w
  17.6 71.6 %project.1 = (bf16[8,256,2048]{2,1,0:T(8,128)(2,1)}, f32[8,256,344]{2,1,0:T(8,128)}, f32[8,256,344]{2,1,0:T(8,128)}) custom-call(bf16[256,2048]{1,0:T(8,128)(2,1)} %refs_5_.1, bf16[1,2048]{1,0:T(2,128)(2,1)} %broadcast_in_dim.16.refs_1_.refs_7_, bf16[344,2048]{1,0:T(8,128)(2,1)} %bitcast.27, bf16[344,2048]{1,0:T(8,128)(2,1)} %bitcast.29), custom_call_target="tpu_custom_call" | custom-call | flops 5771362304 | bytes 200000000 | tf_op jit(solution)/shard_map/project/pallas_call | solution.py:535
  89.2 19.4 %recur_forward.1 = (f32[2048,344]{1,0:T(8,128)}, bf16[2048,344]{1,0:T(8,128)(2,1)}, bf16[2048,344]{1,0:T(8,128)(2,1)}, f32[2048,344]{1,0:T(8,128)}, f32[2048,344...) custom-call(f32[2048,344]{1,0:T(8,128)} %bitcast.16, f32[2048,344]{1,0:T(8,128)} %bitcast.19, ...), custom_call_target="tpu_custom_call" | custom-call | tf_op jit(solution)/shard_map/recur_forward/pallas_call | solution.py:638
  108.6 105.5 %mixer_out.1 = (bf16[8,256,2048]{2,1,0:T(8,128)(2,1)}, f32[256,2048]{1,0:T(8,128)}, bf16[256,2048]{1,0:T(8,128)(2,1)}) custom-call(bf16[8,256,344]{2,1,0:T(8,128)(2,1)} %bitcast.25, bf16[344,2048]{1,0:T(8,128)(2,1)} %refs_4_.3, bf16[256,2048]{1,0:T(8,128)(2,1)} %refs_2_.2, bf16[256,2048]{1,0:T(8,128)(2,1)} %refs_5_.1, ...), custom_call_target="tpu_custom_call" | custom-call | flops 2885681152 | bytes 200000000 | tf_op jit(solution)/shard_map/mixer_out/pallas_call | solution.py:724
  214.1 163.8 %mlp.1 = (bf16[8,256,768]{2,1,0:T(8,128)(2,1)}, bf16[2048,768]{1,0:T(8,128)(2,1)}, bf16[2048,768]{1,0:T(8,128)(2,1)}, bf16[768,2048]{1,0:T(8,128)(2,1)}, f32[256...) custom-call(bf16[256,2048]{1,0:T(8,128)(2,1)} %get-tuple-element.55.refs_0_, ...), custom_call_target="tpu_custom_call" | custom-call | flops 51539607552 | bytes 200000000 | tf_op jit(solution)/shard_map/mlp/pallas_call | solution.py:1023
  379.8 106.0 %down.1 = (bf16[256,2048]{1,0:T(8,128)(2,1)}, f32[8,256,344]{2,1,0:T(8,128)}, bf16[344,2048]{1,0:T(8,128)(2,1)}) custom-call(bf16[8,256,768]{2,1,0:T(8,128)(2,1)} %get-tuple-element.58.refs_0_, bf16[768,2048]{1,0:T(8,128)(2,1)} %refs_1_.3, f32[256,2048]{1,0:T(8,128)} %get-tuple-element.57.refs_5_.refs_2_, bf16[256,2048]{1,0:T(8,128)(2,1)} %get-tuple-element.59.refs_3_, ...), custom_call_target="tpu_custom_call" | custom-call | flops 12213813248 | bytes 200000000 | tf_op jit(solution)/shard_map/down/pallas_call | solution.py:1113
  485.8 29.0 %recur_back.1 = (bf16[2048,344]{1,0:T(8,128)(2,1)}, bf16[2048,344]{1,0:T(8,128)(2,1)}, f32[8,344]{1,0:T(8,128)}, f32[2,344,344]{2,1,0:T(8,128)}) custom-call(f32[2048,344]{1,0:T(8,128)} %bitcast.21, f32[2048,344]{1,0:T(8,128)} %bitcast.20, f32[2048,344]{1,0:T(8,128)} %get-tuple-element.62.states.states_before, ...), custom_call_target="tpu_custom_call" | custom-call | tf_op jit(solution)/shard_map/recur_back/pallas_call | solution.py:1273
  514.8 109.2 %input_back.1 = (f32[256,2048]{1,0:T(8,128)}, bf16[344,2048]{1,0:T(8,128)(2,1)}, bf16[344,2048]{1,0:T(8,128)(2,1)}, bf16[344,2048]{1,0:T(8,128)(2,1)}, f32[2,2,1...) custom-call(bf16[2048,344]{1,0:T(8,128)(2,1)} %get-tuple-element.66.refs_0_, ...), custom_call_target="tpu_custom_call" | custom-call | flops 11542724608 | bytes 200000000 | tf_op jit(solution)/shard_map/input_back/pallas_call | solution.py:1475
  624.0 2.7 copy.36
  626.7 3.2 convert_element_type.26
  629.9 3.6 convert_element_type.29
  634.1 1.3 fusion
  635.4 3.2 convert_bitcast_fusion
  638.7 5.2 convert_element_type.27
  643.9 3.2 convert_element_type.28
  647.1 1.0 copy.47
  648.1 1.0 copy-done.2
  649.1 1.3 copy.48
  (36 shorter events, 6.1 us)
Async XLA Ops:
  7.2 631.5 %all-reduce.3.cloned.1.call-start = ((), (), s32[]{:S(2)}) async-start(), calls=%async_computation | async-start | bytes 12582912 | tf_op jit(solution)/shard_map/psum | solution.py:1560
  378.0 0.7 copy-start.9
  378.0 1.3 copy-start.7
  624.0 5.9 copy-start.1
  629.9 3.6 copy-start.10
  629.9 5.5 copy-start.3
  629.9 5.5 copy-start.4
  638.7 5.2 copy-start
  643.9 3.2 copy-start.5
  647.1 2.0 copy-start.2
  647.1 3.3 copy-start.6
  647.1 3.9 copy-start.8
Sparse Core Ops, SparseCore 0:
  378.1 141.9 all-reduce.2

commit v6 on v5

--- a/solution.py
+++ b/solution.py
@@ -551,19 +551,26 @@
     )(*inputs)
 
 
+def starts(reset, here, init_state, init_conv, state, hist):
+    keep = (1 - reset).astype(F32)
+    state[...] = jnp.broadcast_to(init_state[here] * keep, state.shape)
+    before = [init_conv[q, here] * keep for q in range(3)]
+    hist[0:8] = jnp.concatenate([jnp.zeros((5, hist.shape[1]), F32)] + before, axis=0)
+
+
 def recur_kernel(
-    u, branch, start_state, start_conv, conv, gate_w, bias, decay,
+    resets, u, branch, init_state, init_conv, conv, gate_w, bias, decay,
     states, mixture, conv_low, recall, ingate, final_state, final_conv,
     hist, decay_buf, drive_buf, carry,
 ):
-    chunk = pl.program_id(1)
+    sequence, chunk = pl.program_id(0), pl.program_id(1)
     rows, channels = u.shape
     tile = 32
+    here = pl.ds(sequence, 1)
 
     @pl.when(chunk == 0)
     def _():
-        carry[...] = jnp.broadcast_to(start_state[0], (8, channels))
-        hist[0:8] = jnp.concatenate([jnp.zeros((5, channels), F32), start_conv[0]], axis=0)
+        starts(resets[sequence], here, init_state, init_conv, carry, hist)
 
     @pl.when(chunk > 0)
     def _():
@@ -588,7 +595,7 @@
         k = sigmoid(ingate[at] + bias[1:2])
         recall[at] = r
         ingate[at] = k
-        log_decay = -8.0 * r * decay[...]
+        log_decay = -8.0 * r * decay[...][None]
         step = jnp.exp(log_decay)
         decay_buf[at] = step
         drive_buf[at] = jnp.sqrt(one_minus_square(log_decay, step)) * k * conv_low[at].astype(F32)
@@ -620,13 +627,14 @@
 
     @pl.when(chunk == pl.num_programs(1) - 1)
     def _():
-        final_state[0] = carry[0:1]
-        final_conv[0] = hist[rows + 5 : rows + 8]
-
-
-def recur_forward(u, branch, start_state, start_conv, conv, gate_w, bias, decay):
+        final_state[here] = carry[0:1]
+        for q in range(3):
+            final_conv[q, here] = hist[rows + 5 + q : rows + 6 + q]
+
+
+def recur_forward(resets, u, branch, init_state, init_conv, conv, gate_w, bias, decay):
     total, channels = u.shape
-    sequences = start_state.shape[0]
+    sequences = init_state.shape[0]
     length = total // sequences
     rows = tile_of(length, 256)
     chunks = length // rows
@@ -644,14 +652,15 @@
             shape(total, channels, dtype=BF16),
             shape(total, channels),
             shape(total, channels),
-            shape(sequences, 1, channels),
-            shape(sequences, 3, channels),
+            shape(sequences, channels),
+            shape(3, sequences, channels),
         ),
         in_specs=[
+            pl.BlockSpec(memory_space=pltpu.SMEM),
             block,
             block,
-            pl.BlockSpec((1, 1, channels), lambda s, c: (s, 0, 0)),
-            pl.BlockSpec((1, 3, channels), lambda s, c: (s, 0, 0)),
+            whole(init_state),
+            whole(init_conv),
             whole(conv),
             whole(gate_w),
             whole(bias),
@@ -659,8 +668,8 @@
         ],
         out_specs=(block,) * 5
         + (
-            pl.BlockSpec((1, 1, channels), lambda s, c: (s, 0, 0)),
-            pl.BlockSpec((1, 3, channels), lambda s, c: (s, 0, 0)),
+            whole(init_state),
+            whole(init_conv),
         ),
         scratch_shapes=[
             pltpu.VMEM((rows + 8, channels), F32),
@@ -670,7 +679,7 @@
         ],
         compiler_params=pltpu.CompilerParams(vmem_limit_bytes=VMEM_LIMIT),
         name="recur_forward",
-    )(u, branch, start_state, start_conv, conv, gate_w, bias, decay)
+    )(resets, u, branch, init_state, init_conv, conv, gate_w, bias, decay)
 
 
 def mixer_out_kernel(
@@ -1060,7 +1069,7 @@
 
 
 def down_kernel(
-    n, arrive, hidden, w_down, residual, g_low, w_output, mixture, output, g_mixture, grad_output,
+    n, copies, arrive, hidden, w_down, residual, g_low, w_output, mixture, output, g_mixture, grad_output,
     full, sent, came, acc_o, start_sem, *bufs
 ):
     g = Place(n)
@@ -1097,7 +1106,9 @@
 
     loop(g.nz - 1, around)
     gather.each(g.nz - 1, use)
-    grad_output[...] = acc_o[...].astype(BF16)
+    for i in range(copies):
+        part = width // copies
+        grad_output[i] = acc_o[:, i * part : (i + 1) * part].astype(BF16)
     scatter.last()
     arrive(2)
     output[...] = (scatter.acc[...] + residual[...]).astype(BF16)
@@ -1105,17 +1116,17 @@
     gather.finish()
 
 
-def down(n, hidden, w_down, residual, g_low, w_output, mixture):
+def down(n, copies, hidden, w_down, residual, g_low, w_output, mixture):
     rows, width = residual.shape
     channels = w_output.shape[0]
     inputs, which = (hidden, w_down, residual, g_low, w_output, mixture), (0, 1, 4, 5, 2)
     specs, kept = fetched_specs(inputs, which, (3,))
     return pl.pallas_call(
-        fetching(functools.partial(down_kernel, n), which),
+        fetching(functools.partial(down_kernel, n, copies), which),
         out_shape=(
             shape(rows, width, dtype=BF16),
             shape(n, rows, channels),
-            shape(channels, width, dtype=BF16),
+            shape(copies, channels, width // copies, dtype=BF16),
         ),
         in_specs=specs,
         out_specs=(VM,) * 3,
@@ -1130,15 +1141,16 @@
 
 
 def recur_back_kernel(
-    g_mix, branch, states, states_before, u, u_before, conv_low, recall, ingate, start_state, start_conv,
-    conv, gate_w, decay,
-    g_recur, g_branch, small, g_gates,
+    resets, g_mix, branch, states, states_before, u, u_before, conv_low, recall, ingate, init_state, init_conv,
+    conv, gate_w, decay, narrow_in,
+    g_recur, g_branch, small, g_gates, wide_out,
     g_state, step_buf, root_buf, g_conv, pre_r, pre_i, carry, hist_s, hist_u, sums,
 ):
     sequence, back = pl.program_id(0), pl.program_id(1)
     last = pl.num_programs(1) - 1
     rows, channels = u.shape
     tile = 32
+    wide_out[...] = narrow_in[...].astype(F32)
 
     @pl.when(jnp.logical_and(sequence == 0, back == 0))
     def _():
@@ -1156,8 +1168,9 @@
 
     @pl.when(back == last)
     def _():
-        hist_s[0:8] = jnp.broadcast_to(start_state[0], (8, channels))
-        hist_u[0:8] = jnp.concatenate([jnp.zeros((5, channels), F32), start_conv[0]], axis=0)
+        starts(
+            resets[sequence], pl.ds(sequence, 1), init_state, init_conv, hist_s.at[0:8], hist_u
+        )
 
     @pl.when(back < last)
     def _():
@@ -1173,7 +1186,7 @@
         gm = g_mix[at]
         g_state[at] = gm * value
         g_branch[at] = (gm * states[at] * slope).astype(BF16)
-        log_decay = -8.0 * recall[at] * decay[...]
+        log_decay = -8.0 * recall[at] * decay[...][None]
         step = jnp.exp(log_decay)
         step_buf[at] = step
         root_buf[at] = jnp.sqrt(one_minus_square(log_decay, step))
@@ -1212,7 +1225,7 @@
         g_log = g * (before * step - kc * (step * step) / root)
         slow = -8.0 * r
         sums[7] += fold(g_log * slow)
-        low_r = (g_log * (slow * decay[...]) * (1.0 - r)).astype(BF16)
+        low_r = (g_log * (slow * decay[...][None]) * (1.0 - r)).astype(BF16)
         low_i = (g * root * kc * (1.0 - k)).astype(BF16)
         pre_r[at] = low_r
         pre_i[at] = low_i
@@ -1247,12 +1260,16 @@
         small[...] = jnp.sum(sums[...], axis=1)
 
 
-def recur_back(g_mix, branch, states, u, conv_low, recall, ingate, start_state, start_conv, conv, gate_w, decay):
+def recur_back(
+    resets, g_mix, branch, states, u, conv_low, recall, ingate, init_state, init_conv, conv, gate_w, decay, narrow_in
+):
     total, channels = u.shape
-    sequences = start_state.shape[0]
+    sequences = init_state.shape[0]
     length = total // sequences
     rows = tile_of(length, 256)
     chunks = length // rows
+    extra_rows = narrow_in.shape[0] // (sequences * chunks)
+    extra = pl.BlockSpec((extra_rows, narrow_in.shape[1]), lambda s, c: (s * chunks + c, 0))
     eights = rows // 8
 
     def at(s, c):
@@ -1278,18 +1295,19 @@
             shape(total, channels, dtype=BF16),
             shape(8, channels),
             shape(2, channels, channels),
+            shape(*narrow_in.shape),
         ),
         in_specs=[
+            pl.BlockSpec(memory_space=pltpu.SMEM),
             block, block, block, before, block, before, block, block, block,
-            pl.BlockSpec((1, 1, channels), lambda s, c: (s, 0, 0)),
-            pl.BlockSpec((1, 3, channels), lambda s, c: (s, 0, 0)),
-            whole(conv), whole(gate_w), whole(decay),
+            whole(init_state), whole(init_conv), whole(conv), whole(gate_w), whole(decay), extra,
         ],
         out_specs=(
             block,
             block,
             pl.BlockSpec((8, channels), lambda s, c: (0, 0)),
             pl.BlockSpec((2, channels, channels), lambda s, c: (0, 0, 0)),
+            extra,
         ),
         scratch_shapes=[
             wide, wide, wide, long, narrow, narrow,
@@ -1298,12 +1316,15 @@
         ],
         compiler_params=pltpu.CompilerParams(vmem_limit_bytes=VMEM_LIMIT),
         name="recur_back",
-    )(g_mix, branch, states, states, u, u, conv_low, recall, ingate, start_state, start_conv, conv, gate_w, decay)
+    )(
+        resets, g_mix, branch, states, states, u, u, conv_low, recall, ingate, init_state, init_conv,
+        conv, gate_w, decay, narrow_in,
+    )
 
 
 def input_back_kernel(
-    n, copies, arrive, g_recur, g_branch, w_in, w_br, normed, tokens, g_residual, gain, second_gain, g_gates, small, g_out,
-    input_grad, in_out, br_out, out_out, gates_out, conv_out, bias_out, decay_out, gains_out,
+    n, copies, arrive, g_recur, g_branch, w_in, w_br, normed, tokens, g_residual, gain, second_gain, g_gates, small,
+    input_grad, in_out, br_out, gates_out, conv_out, bias_out, decay_out, gains_out,
     gain_row, gain_parts, gain_in, gain_sum, gain_dp, gain_sent, gain_came, gain_dp_sent, gain_dp_came, *bufs
 ):
     g = Place(n)
@@ -1315,7 +1336,7 @@
     gain_width = width // n
     weights = Halving.over(me, copies, *bufs[:4])
     rest = Halving.over(me, copies, *bufs[4:8])
-    padded = bufs[0].shape[3] // 3
+    padded = bufs[0].shape[3] // 2
     rest_rows = bufs[4].shape[3]
 
     def block(ref, t):
@@ -1361,7 +1382,7 @@
         scatter.step(d)
 
     around(0)
-    arrive(4, 11, 9)
+    arrive(4, 9)
 
     data = bufs[0]
 
@@ -1369,11 +1390,10 @@
         cols = span(q, 2 * segment)
         first = dot_tn(g_recur[...], normed[:, cols])
         second = dot_tn(g_branch[...], normed[:, cols])
-        third = g_out[:, cols]
         for half in (0, 1):
             index = 2 * q + half
             track, part = lax.div(index, copies), lax.rem(index, copies)
-            for i, value in enumerate((first, second, third)):
+            for i, value in enumerate((first, second)):
                 piece = value[:, half * segment : (half + 1) * segment].astype(BF16)
                 data[track, part, 0, i * padded : i * padded + channels] = piece
                 if padded > channels:
@@ -1446,7 +1466,7 @@
     decay_out[...] = flat[2 * channels + 7 : 2 * channels + 8]
     weights.finish()
     for i in range(2 * copies):
-        for q, out in enumerate((in_out, br_out, out_out)):
+        for q, out in enumerate((in_out, br_out)):
             out[:, i * segment : (i + 1) * segment] = bufs[2][
                 i // copies, i % copies, 0, q * padded : q * padded + channels
             ]
@@ -1460,8 +1480,7 @@
 
 
 def input_back(
-    n, copies, g_recur, g_branch, w_in, w_br, normed, tokens, g_residual, gain, second_gain, g_gates, small, g_out,
-    blocks,
+    n, copies, g_recur, g_branch, w_in, w_br, normed, tokens, g_residual, gain, second_gain, g_gates, small, blocks
 ):
     rows, width = tokens.shape
     channels = w_in.shape[0]
@@ -1469,13 +1488,13 @@
     rest_rows = up_to((2 * channels + 8 + 2 * copies - 1) // (2 * copies), 16)
     gain_shape = (8, width // n)
     sems = pltpu.SemaphoreType.DMA
-    inputs = (g_recur, g_branch, w_in, w_br, normed, tokens, g_residual, gain, second_gain, g_gates, small, g_out)
-    which = (0, 1, 2, 3, 4, 11, 9, 5, 6)
+    inputs = (g_recur, g_branch, w_in, w_br, normed, tokens, g_residual, gain, second_gain, g_gates, small)
+    which = (0, 1, 2, 3, 4, 9, 5, 6)
     specs, kept = fetched_specs(inputs, which)
     return pl.pallas_call(
         fetching(functools.partial(input_back_kernel, n, copies), which),
         out_shape=(shape(rows, width),)
-        + (shape(channels, width, dtype=BF16),) * 3
+        + (shape(channels, width, dtype=BF16),) * 2
         + (
             shape(2, blocks, block, block),
             shape(5, channels),
@@ -1484,7 +1503,7 @@
             shape(*gain_shape),
         ),
         in_specs=specs,
-        out_specs=(VM,) * 9,
+        out_specs=(VM,) * 8,
         scratch_shapes=[
             pltpu.VMEM((8, width), F32),
             pltpu.VMEM((n, *gain_shape), F32),
@@ -1496,7 +1515,7 @@
             sems((copies,)),
             sems((copies,)),
         ]
-        + Halving.scratch(copies, 3 * up_to(channels, 16), width // (2 * copies))
+        + Halving.scratch(copies, 2 * up_to(channels, 16), width // (2 * copies))
         + Halving.scratch(copies, rest_rows, channels)
         + Scatter.scratch(n, rows, width)
         + kept,
@@ -1504,6 +1523,38 @@
         cost_estimate=cost(8 * n * rows * width * channels),
         name="input_back",
     )(*inputs)
+
+
+def widen_kernel(*refs):
+    half = len(refs) // 2
+    for narrow, wide in zip(refs[:half], refs[half:]):
+        wide[...] = narrow[...].reshape(wide.shape).astype(F32)
+
+
+def widen(by_rows, by_columns, in_parts):
+    steps = 8
+    width = by_columns[0].shape[1]
+    tile = width // steps
+    per_part = in_parts.shape[2] // tile
+    specs, outs = [], []
+    for x in by_rows:
+        specs.append(pl.BlockSpec((x.shape[0] // steps, x.shape[1]), lambda i: (i, 0)))
+        outs.append(shape(*x.shape))
+    for x in by_columns:
+        specs.append(pl.BlockSpec((x.shape[0], tile), lambda i: (0, i)))
+        outs.append(shape(*x.shape))
+    last = pl.BlockSpec((1, in_parts.shape[1], tile), lambda i: (i // per_part, 0, i % per_part))
+    outs.append(shape(in_parts.shape[1], width))
+    wide = pl.BlockSpec((in_parts.shape[1], tile), lambda i: (0, i))
+    return pl.pallas_call(
+        widen_kernel,
+        grid=(steps,),
+        out_shape=tuple(outs),
+        in_specs=specs + [last],
+        out_specs=tuple(specs) + (wide,),
+        compiler_params=pltpu.CompilerParams(vmem_limit_bytes=VMEM_LIMIT),
+        name="widen",
+    )(*by_rows, *by_columns, in_parts)
 
 
 def body(
@@ -1531,14 +1582,11 @@
     total = rows * n
     channels = w_input.shape[1]
     blocks, block = gate_weights.shape[1], gate_weights.shape[2]
-    survive = (1 - resets).astype(F32)
-    start_state = (init_state * survive[:, None])[:, None]
-    start_conv = init_conv * survive[:, None, None]
+    before_conv = init_conv.transpose(1, 0, 2)
     gain_first, gain_second = norm_gain[None], mlp_gain[None]
     gate_w = (gate_weights[:, :, :, None] * jnp.eye(blocks, dtype=BF16)[None, :, None, :, None]).reshape(
         2, channels, channels
     )
-    decay = decay_rate[None]
     w_in, w_br = w_input.T, w_branch.T
 
     def flat(x):
@@ -1550,7 +1598,7 @@
     normed, recur, branch = project(n, tokens, gain_first, w_in, w_br)
     recur, branch = flat(recur), flat(branch)
     states, mixture, conv_low, recall, ingate, final_state, final_conv = recur_forward(
-        recur, branch, start_state, start_conv, conv_params, gate_w, gate_bias, decay
+        resets, recur, branch, init_state, before_conv, conv_params, gate_w, gate_bias, decay_rate
     )
     mixture = blocked(mixture)
     cot_full, residual, normed_mlp = mixer_out(n, mixture, w_output, cotangent, tokens, gain_second)
@@ -1558,30 +1606,33 @@
         n, copies, normed_mlp, cot_full, w_gelu, w_linear, w_down, residual, gain_second
     )
     mlp_sums = lax.psum((grad_gelu, grad_linear), "dp")
-    output, g_mixture, grad_output = down(n, hidden, w_down, residual, g_low, w_output, mixture)
-    g_recur, g_branch, small, g_gates = recur_back(
-        flat(g_mixture), branch, states, recur, conv_low, recall, ingate, start_state, start_conv,
-        conv_params, gate_w, decay,
+    output, g_mixture, grad_output = down(n, copies, hidden, w_down, residual, g_low, w_output, mixture)
+    g_recur, g_branch, small, g_gates, grad_down = recur_back(
+        resets, flat(g_mixture), branch, states, recur, conv_low, recall, ingate, init_state, before_conv,
+        conv_params, gate_w, decay_rate, grad_down,
     )
-    input_grad, grad_input, grad_branch, grad_output, gates, g_conv, g_bias, g_decay, gains = input_back(
+    mlp_sums, grad_output, small = lax.optimization_barrier((mlp_sums, grad_output, small))
+    grad_output = lax.psum(grad_output, "dp")
+    input_grad, grad_input, grad_branch, gates, g_conv, g_bias, g_decay, gains = input_back(
         n, copies, g_recur, g_branch, w_in, w_br, flat(normed), tokens, g_residual, gain_first,
-        gain_second_grad, g_gates, small, grad_output, blocks,
+        gain_second_grad, g_gates, small, blocks,
     )
-    grad_gelu, grad_linear = (x.astype(F32) for x in mlp_sums)
-    grad_down = grad_down.astype(F32)
+    grad_gelu, grad_linear, grad_input, grad_branch, grad_output = widen(
+        mlp_sums, (grad_input, grad_branch), grad_output
+    )
     return (
         output,
         input_grad,
-        final_state[:, 0],
-        final_conv,
+        final_state,
+        final_conv.transpose(1, 0, 2),
         gains[0],
-        grad_input.astype(F32).T,
-        grad_branch.astype(F32).T,
+        grad_input.T,
+        grad_branch.T,
         g_conv,
         gates,
         g_bias,
         g_decay[0],
-        grad_output.astype(F32),
+        grad_output,
         gains[1],
         grad_gelu,
         grad_linear,

time: 659 us -> 647 us (0.982)
  other arithmetic: 22.7 us -> 2.17 us
    convert_element_type x5 -> x0, other arithmetic: 15.9 us -> none  [the longest x2 8.42 us: body(): grad_gelu, grad_linear = (x.astype(F32) for x in mlp_sums)]
    pallas_call x1 -> x2, Pallas kernels: 106 us -> 118 us  [the longest x1 106 us: down(): pl.pallas_call(fetching(functools.partial(down_kernel, n, copies), which)...]
    pallas_call x1, Pallas kernels: 109 us -> 102 us  [input_back(): pl.pallas_call(fetching(functools.partial(input_back_kernel, n, copies),...]
  transfers between devices with their start and end apart: 1 -> 2, of which waited for: 0 -> 1; matrix products, arithmetic and copies ran while one was open for 2% -> 1% of each run, Pallas kernels for 37% -> 37%
where the time goes in v6:
time: 647 us
  Pallas kernels  611 us (94%)
  between operations  14.2 us (2%)
  local copies, waits for them, and re-layouts  13.1 us (2%)
    pallas_call x1, Pallas kernels, mlp(): pl.pallas_call(fetching(functools.partial(mlp_kernel, n, copies), which),...  164 us
    pallas_call x1, Pallas kernels, down(): pl.pallas_call(fetching(functools.partial(down_kernel, n, copies), which)...  106 us
    pallas_call x1, Pallas kernels, mixer_out(): pl.pallas_call(fetching(functools.partial(mixer_out_kernel, n), which), o...  106 us
    pallas_call x1, Pallas kernels, input_back(): pl.pallas_call(fetching(functools.partial(input_back_kernel, n, copies),...  102 us
    pallas_call x1, Pallas kernels, project(): pl.pallas_call(fetching(functools.partial(project_kernel, n), (2, 3)), ou...  71.6 us
    pallas_call x1, Pallas kernels, recur_back(): pl.pallas_call(recur_back_kernel, grid=(sequences, chunks), out_shape=(sh...  30.4 us
    pallas_call x1, Pallas kernels, recur_forward(): pl.pallas_call(recur_kernel, grid=(sequences, chunks), out_shape=(shape(t...  19.4 us
  transfers between devices with their start and end apart: 2, of which 1 were waited for; matrix products, arithmetic and copies ran while one was open for 1% of the time, Pallas kernels for 37%

profile of v6, /device:TPU:8, one launch (start us, length us, event | category | flops | bytes accessed | tf_op | source)
XLA Modules:
  0.0 646.6 jit_solution(12343625707501395909)
XLA Ops:
  7.2 1.3 broadcast_in_dim.8.refs_1_.refs_7_
  8.5 1.3 broadcast_in_dim.9.refs_4_.refs_6_
  9.8 0.3 mul.22
  10.3 1.0 copy.33
  11.3 0.4 mul.20
  11.7 0.4 mul.21
  12.1 0.9 broadcast_multiply_fusion.gate_w
  13.0 71.6 %project.1 = (bf16[8,256,2048]{2,1,0:T(8,128)(2,1)}, f32[8,256,344]{2,1,0:T(8,128)}, f32[8,256,344]{2,1,0:T(8,128)}) custom-call(bf16[256,2048]{1,0:T(8,128)(2,1)} %refs_5_.1, bf16[1,2048]{1,0:T(2,128)(2,1)} %broadcast_in_dim.8.refs_1_.refs_7_, bf16[344,2048]{1,0:T(8,128)(2,1)} %bitcast.27, bf16[344,2048]{1,0:T(8,128)(2,1)} %bitcast.29), custom_call_target="tpu_custom_call" | custom-call | flops 5771362304 | bytes 200000000 | tf_op jit(solution)/shard_map/project/pallas_call | solution.py:535
  84.6 19.4 %recur_forward.1 = (f32[2048,344]{1,0:T(8,128)}, bf16[2048,344]{1,0:T(8,128)(2,1)}, bf16[2048,344]{1,0:T(8,128)(2,1)}, f32[2048,344]{1,0:T(8,128)}, f32[2048,344...) custom-call(s32[2]{0:T(128)} %resets.3, f32[2048,344]{1,0:T(8,128)} %bitcast.13, f32[2048,344]{1,0:T(8,128)} %bitcast.16, ...), custom_call_target="tpu_custom_call" | custom-call | tf_op jit(solution)/shard_map/recur_forward/pallas_call | solution.py:646
  104.0 105.5 %mixer_out.1 = (bf16[8,256,2048]{2,1,0:T(8,128)(2,1)}, f32[256,2048]{1,0:T(8,128)}, bf16[256,2048]{1,0:T(8,128)(2,1)}) custom-call(bf16[8,256,344]{2,1,0:T(8,128)(2,1)} %bitcast.25, bf16[344,2048]{1,0:T(8,128)(2,1)} %refs_4_.3, bf16[256,2048]{1,0:T(8,128)(2,1)} %refs_2_.2, bf16[256,2048]{1,0:T(8,128)(2,1)} %refs_5_.1, ...), custom_call_target="tpu_custom_call" | custom-call | flops 2885681152 | bytes 200000000 | tf_op jit(solution)/shard_map/mixer_out/pallas_call | solution.py:733
  209.6 164.0 %mlp.1 = (bf16[8,256,768]{2,1,0:T(8,128)(2,1)}, bf16[2048,768]{1,0:T(8,128)(2,1)}, bf16[2048,768]{1,0:T(8,128)(2,1)}, bf16[768,2048]{1,0:T(8,128)(2,1)}, f32[256...) custom-call(bf16[256,2048]{1,0:T(8,128)(2,1)} %get-tuple-element.64.refs_0_, ...), custom_call_target="tpu_custom_call" | custom-call | flops 51539607552 | bytes 200000000 | tf_op jit(solution)/shard_map/mlp/pallas_call | solution.py:1032
  373.7 106.0 %down.1 = (bf16[256,2048]{1,0:T(8,128)(2,1)}, f32[8,256,344]{2,1,0:T(8,128)}, bf16[4,344,512]{2,1,0:T(8,128)(2,1)}) custom-call(bf16[8,256,768]{2,1,0:T(8,128)(2,1)} %get-tuple-element.67.refs_0_, bf16[768,2048]{1,0:T(8,128)(2,1)} %refs_1_.3, f32[256,2048]{1,0:T(8,128)} %get-tuple-element.66.refs_5_.refs_2_, bf16[256,2048]{1,0:T(8,128)(2,1)} %get-tuple-element.68.refs_3_, ...), custom_call_target="tpu_custom_call" | custom-call | flops 12213813248 | bytes 200000000 | tf_op jit(solution)/shard_map/down/pallas_call | solution.py:1124
  479.7 30.4 %recur_back.1 = (bf16[2048,344]{1,0:T(8,128)(2,1)}, bf16[2048,344]{1,0:T(8,128)(2,1)}, f32[8,344]{1,0:T(8,128)}, f32[2,344,344]{2,1,0:T(8,128)}, f32[768,2048]{1,0:T(8,128)}) custom-call(s32[2]{0:T(128)} %resets.3, f32[2048,344]{1,0:T(8,128)} %bitcast.18, f32[2048,344]{1,0:T(8,128)} %bitcast.17, f32[2048,344]{1,0:T(8,128)} %get-tuple-element.71.states.states_before, ...), custom_call_target="tpu_custom_call" | custom-call | tf_op jit(solution)/shard_map/recur_back/pallas_call | solution.py:1290
  510.1 5.7 all-reduce.6.cloned.1.call-done
  515.8 102.4 %input_back.1 = (f32[256,2048]{1,0:T(8,128)}, bf16[344,2048]{1,0:T(8,128)(2,1)}, bf16[344,2048]{1,0:T(8,128)(2,1)}, f32[2,2,172,172]{3,2,1,0:T(8,128)}, f32[5,34...) custom-call(bf16[2048,344]{1,0:T(8,128)(2,1)} %get-tuple-element.76.refs_0_, ...), custom_call_target="tpu_custom_call" | custom-call | flops 11542724608 | bytes 200000000 | tf_op jit(solution)/shard_map/input_back/pallas_call | solution.py:1494
  618.2 2.5 copy.34
  620.8 1.3 reduce
  622.0 1.3 fusion
  623.4 11.9 %widen.1 = (f32[2048,768]{1,0:T(8,128)}, f32[2048,768]{1,0:T(8,128)}, f32[344,2048]{1,0:T(8,128)}, f32[344,2048]{1,0:T(8,128)}, f32[344,2048]{1,0:T(8,128)}) custom-call(bf16[2048,768]{1,0:T(8,128)(2,1)} %get-tuple-element.91.refs_0_, bf16[2048,768]{1,0:T(8,128)(2,1)} %get-tuple-element.92.refs_1_, bf16[344,2048]{1,0:T(8,128)(2,1)} %get-tuple-element.93.refs_2_, ...), custom_call_target="tpu_custom_call" | custom-call | tf_op jit(solution)/shard_map/widen/pallas_call | solution.py:1549
  635.3 1.0 copy.42
  636.3 1.0 copy-done
  637.3 1.3 copy.43
  638.6 0.6 copy.44
  639.2 0.6 copy.45
  (14 shorter events, 0.3 us)
Async XLA Ops:
  7.2 508.6 %all-reduce.6.cloned.1.call-start = ((), (), s32[]{:S(2)}) async-start(), calls=%async_computation.1 | async-start | bytes 12582912 | tf_op jit(solution)/shard_map/psum | solution.py:1608
  373.6 249.7 %all-reduce.4.cloned.1.call-start = ((), (), s32[]{:S(2)}) async-start(), calls=%async_computation | async-start | bytes 2818048 | tf_op jit(solution)/shard_map/psum | solution.py:1615
  623.4 11.9 %copy-start.1 = (bf16[256,2048]{1,0:T(8,128)(2,1)S(1)}, bf16[256,2048]{1,0:T(8,128)(2,1)}, u32[]{:S(2)}) copy-start(bf16[256,2048]{1,0:T(8,128)(2,1)} %get-tuple-element.142) | copy-start | bytes 3145732
  635.3 2.0 copy-start
  635.3 3.3 copy-start.2
  635.3 3.9 copy-start.3
Sparse Core Ops, SparseCore 0:
  373.7 142.0 all-reduce.5
  518.9 76.3 all-reduce.3

commit v7 on v6

--- a/solution.py
+++ b/solution.py
@@ -488,69 +488,6 @@
     return jnp.where(m < 0.35, series, 1.0 - decay * decay)
 
 
-def project_kernel(n, arrive, tokens, gain, w_in, w_br, normed, recur, branch, full, sent, came, held_a, held_b, saved):
-    g = Place(n)
-    gather = Gather(g, full, sent, came)
-    part = 64
-
-    def normalize(i):
-        at = span(i, part)
-        values = tokens[at].astype(F32)
-        full[g.t, at] = (values * inv_rms(values) * gain[...].astype(F32)).astype(BF16)
-
-    loop(full.shape[1] // part, normalize)
-    g.greet()
-    gather.start()
-    arrive(2, 3)
-
-    def use(t):
-        pltpu.make_async_copy(full.at[t], normed.at[t], saved.at[t, 0]).start()
-        held_a[t] = dot_nt(full[t], w_in[...])
-        held_b[t] = dot_nt(full[t], w_br[...])
-        pltpu.make_async_copy(held_a.at[t], recur.at[t], saved.at[t, 1]).start()
-        pltpu.make_async_copy(held_b.at[t], branch.at[t], saved.at[t, 2]).start()
-
-    gather.each(0, use)
-
-    def away(i):
-        gather.forward(i + 1)
-        gather.each(i + 1, use)
-
-    loop(g.nz - 1, away)
-
-    def done(t):
-        pltpu.make_async_copy(full.at[t], normed.at[t], saved.at[t, 0]).wait()
-        pltpu.make_async_copy(held_a.at[t], recur.at[t], saved.at[t, 1]).wait()
-        pltpu.make_async_copy(held_b.at[t], branch.at[t], saved.at[t, 2]).wait()
-
-    loop(n, done)
-    gather.finish()
-
-
-def project(n, tokens, gain, w_in, w_br):
-    rows, width = tokens.shape
-    channels = w_in.shape[0]
-    inputs = (tokens, gain, w_in, w_br)
-    specs, kept = fetched_specs(inputs, (2, 3))
-    return pl.pallas_call(
-        fetching(functools.partial(project_kernel, n), (2, 3)),
-        out_shape=(
-            shape(n, rows, width, dtype=BF16),
-            shape(n, rows, channels),
-            shape(n, rows, channels),
-        ),
-        in_specs=specs,
-        out_specs=(ANY,) * 3,
-        scratch_shapes=Gather.scratch(n, rows, width)
-        + [pltpu.VMEM((n, rows, channels), F32)] * 2
-        + [pltpu.SemaphoreType.DMA((n, 3))]
-        + kept,
-        compiler_params=comm_params(1),
-        cost_estimate=cost(4 * n * rows * width * channels),
-        name="project",
-    )(*inputs)
-
-
 def starts(reset, here, init_state, init_conv, state, hist):
     keep = (1 - reset).astype(F32)
     state[...] = jnp.broadcast_to(init_state[here] * keep, state.shape)
@@ -558,47 +495,39 @@
     hist[0:8] = jnp.concatenate([jnp.zeros((5, hist.shape[1]), F32)] + before, axis=0)
 
 
-def recur_kernel(
-    resets, u, branch, init_state, init_conv, conv, gate_w, bias, decay,
-    states, mixture, conv_low, recall, ingate, final_state, final_conv,
-    hist, decay_buf, drive_buf, carry,
-):
-    sequence, chunk = pl.program_id(0), pl.program_id(1)
-    rows, channels = u.shape
+def recur_chunk(base, u, branch, conv, gate_w, bias, decay, kept, hist, decay_buf, drive_buf, carry):
+    states, mixture, conv_low, recall, ingate = kept
+    rows, channels = decay_buf.shape
     tile = 32
-    here = pl.ds(sequence, 1)
-
-    @pl.when(chunk == 0)
-    def _():
-        starts(resets[sequence], here, init_state, init_conv, carry, hist)
-
-    @pl.when(chunk > 0)
-    def _():
-        hist[0:8] = hist[rows : rows + 8]
-
-    hist[8:] = u[...]
+
+    def rows_of(i, size):
+        return pl.ds(pl.multiple_of(base + i * size, size), size)
+
+    whole = rows_of(0, rows)
+    hist[8:] = u[whole]
 
     def convolve(i):
         window = hist[pl.ds(pl.multiple_of(i * tile, tile), tile + 8)]
         value = conv[4:5] + conv[0:1] * window[8:] + conv[1:2] * window[7 : tile + 7]
         value = value + conv[2:3] * window[6 : tile + 6] + conv[3:4] * window[5 : tile + 5]
-        conv_low[span(i, tile)] = value.astype(BF16)
+        conv_low[rows_of(i, tile)] = value.astype(BF16)
 
     loop(rows // tile, convolve)
-    low = conv_low[...]
-    recall[...] = dot(low, gate_w[0])
-    ingate[...] = dot(low, gate_w[1])
+    hist[0:8] = hist[rows : rows + 8]
+    low = conv_low[whole]
+    recall[whole] = dot(low, gate_w[0])
+    ingate[whole] = dot(low, gate_w[1])
 
     def gates(i):
-        at = span(i, tile)
+        at, here = rows_of(i, tile), span(i, tile)
         r = sigmoid(recall[at] + bias[0:1])
         k = sigmoid(ingate[at] + bias[1:2])
         recall[at] = r
         ingate[at] = k
         log_decay = -8.0 * r * decay[...][None]
         step = jnp.exp(log_decay)
-        decay_buf[at] = step
-        drive_buf[at] = jnp.sqrt(one_minus_square(log_decay, step)) * k * conv_low[at].astype(F32)
+        decay_buf[here] = step
+        drive_buf[here] = jnp.sqrt(one_minus_square(log_decay, step)) * k * conv_low[at].astype(F32)
 
     loop(rows // tile, gates)
     row = lax.broadcasted_iota(jnp.int32, (8, channels), 0)
@@ -612,74 +541,137 @@
                 b = b + a * jnp.where(inside, pltpu.roll(b, shift, 0), 0.0)
                 a = a * jnp.where(inside, pltpu.roll(a, shift, 0), 1.0)
             h = a * before + b
-            states[at] = h
+            states[pl.ds(pl.multiple_of(base + i * 32 + part * 8, 8), 8)] = h
             before = jnp.broadcast_to(h[7:8], (8, channels))
         return before
 
     carry[...] = lax.fori_loop(0, rows // 32, scan, carry[...])
 
     def mix(i):
-        at = span(i, tile)
+        at = rows_of(i, tile)
         value, _ = gelu_parts(branch[at])
         mixture[at] = (states[at] * value).astype(BF16)
 
     loop(rows // tile, mix)
 
-    @pl.when(chunk == pl.num_programs(1) - 1)
-    def _():
+
+def project_kernel(
+    n, arrive, tokens, gain, w_in, w_br, resets, init_state, init_conv, conv, gate_w, bias, decay,
+    normed, recur, branch, states, mixture, conv_low, recall, ingate, final_state, final_conv,
+    full, sent, came, held_a, held_b, kept_s, kept_m, kept_c, kept_r, kept_i,
+    hist, decay_buf, drive_buf, carry, saved, written,
+):
+    g = Place(n)
+    gather = Gather(g, full, sent, came)
+    rows = full.shape[1]
+    part = 64
+
+    def normalize(i):
+        at = span(i, part)
+        values = tokens[at].astype(F32)
+        full[g.t, at] = (values * inv_rms(values) * gain[...].astype(F32)).astype(BF16)
+
+    loop(rows // part, normalize)
+    g.greet()
+    gather.start()
+    arrive(2, 3)
+
+    def out(t):
+        return pltpu.make_async_copy(full.at[t], normed.at[t], saved.at[t])
+
+    def use(t):
+        out(t).start()
+        at = span(t, rows)
+        held_a[at] = dot_nt(full[t], w_in[...])
+        held_b[at] = dot_nt(full[t], w_br[...])
+
+    kept = (kept_s, kept_m, kept_c, kept_r, kept_i)
+    pairs = ((held_a, recur), (held_b, branch)) + tuple(zip(kept, (states, mixture, conv_low, recall, ingate)))
+    sequences = init_state.shape[0]
+    length = n * rows // sequences
+    size = decay_buf.shape[0]
+    chunks = length // size
+
+    def leave(c, act):
+        at = span(c, size)
+        for q, (held, target) in enumerate(pairs):
+            act(pltpu.make_async_copy(held.at[at], target.at[at], written.at[c, q]))
+
+    def sequence(s):
+        here = pl.ds(s, 1)
+        starts(resets[s], here, init_state, init_conv, carry, hist)
+
+        def chunk(c):
+            index = s * chunks + c
+            base = index * size
+            recur_chunk(base, held_a, held_b, conv, gate_w, bias, decay, kept, hist, decay_buf, drive_buf, carry)
+            leave(index, lambda copy: copy.start())
+
+        loop(chunks, chunk)
         final_state[here] = carry[0:1]
         for q in range(3):
-            final_conv[q, here] = hist[rows + 5 + q : rows + 6 + q]
-
-
-def recur_forward(resets, u, branch, init_state, init_conv, conv, gate_w, bias, decay):
-    total, channels = u.shape
+            final_conv[q, here] = hist[5 + q : 6 + q]
+
+    def step(d):
+        pl.when(d > 0)(lambda: gather.forward(d))
+        gather.each(d, use)
+
+        def whole(s):
+            first = lax.div(s * length, 2 * rows)
+            last = lax.div((s + 1) * length - 1, 2 * rows)
+            pl.when(jnp.maximum(jnp.abs(first - g.j), jnp.abs(last - g.j)) == d)(lambda: sequence(s))
+
+        loop(sequences, whole)
+
+    loop(g.nz, step)
+    loop(n, lambda t: out(t).wait())
+    loop(sequences * chunks, lambda c: leave(c, lambda copy: copy.wait()))
+    gather.finish()
+
+
+def project(n, tokens, gain, w_in, w_br, resets, init_state, init_conv, conv, gate_w, bias, decay):
+    rows, width = tokens.shape
+    channels = w_in.shape[0]
     sequences = init_state.shape[0]
-    length = total // sequences
-    rows = tile_of(length, 256)
-    chunks = length // rows
-    block = pl.BlockSpec((rows, channels), lambda s, c: (s * chunks + c, 0))
-
-    def whole(x):
-        return pl.BlockSpec(x.shape, lambda s, c: (0,) * x.ndim)
-
+    total = n * rows
+    size = tile_of(total // sequences, 256)
+    inputs = (tokens, gain, w_in, w_br, resets, init_state, init_conv, conv, gate_w, bias, decay)
+    specs, kept = fetched_specs(inputs, (2, 3))
+    specs[4] = pl.BlockSpec(memory_space=pltpu.SMEM)
+    wide, narrow = (total, channels), pltpu.VMEM((total, channels), BF16)
     return pl.pallas_call(
-        recur_kernel,
-        grid=(sequences, chunks),
+        fetching(functools.partial(project_kernel, n), (2, 3)),
         out_shape=(
-            shape(total, channels),
-            shape(total, channels, dtype=BF16),
-            shape(total, channels, dtype=BF16),
-            shape(total, channels),
-            shape(total, channels),
+            shape(n, rows, width, dtype=BF16),
+            shape(*wide),
+            shape(*wide),
+            shape(*wide),
+            shape(*wide, dtype=BF16),
+            shape(*wide, dtype=BF16),
+            shape(*wide),
+            shape(*wide),
             shape(sequences, channels),
             shape(3, sequences, channels),
         ),
-        in_specs=[
-            pl.BlockSpec(memory_space=pltpu.SMEM),
-            block,
-            block,
-            whole(init_state),
-            whole(init_conv),
-            whole(conv),
-            whole(gate_w),
-            whole(bias),
-            whole(decay),
-        ],
-        out_specs=(block,) * 5
-        + (
-            whole(init_state),
-            whole(init_conv),
-        ),
-        scratch_shapes=[
-            pltpu.VMEM((rows + 8, channels), F32),
-            pltpu.VMEM((rows, channels), F32),
-            pltpu.VMEM((rows, channels), F32),
+        in_specs=specs,
+        out_specs=(ANY,) * 8 + (VM,) * 2,
+        scratch_shapes=Gather.scratch(n, rows, width)
+        + [pltpu.VMEM(wide, F32)] * 3
+        + [narrow] * 2
+        + [pltpu.VMEM(wide, F32)] * 2
+        + [
+            pltpu.VMEM((size + 8, channels), F32),
+            pltpu.VMEM((size, channels), F32),
+            pltpu.VMEM((size, channels), F32),
             pltpu.VMEM((8, channels), F32),
-        ],
-        compiler_params=pltpu.CompilerParams(vmem_limit_bytes=VMEM_LIMIT),
-        name="recur_forward",
-    )(resets, u, branch, init_state, init_conv, conv, gate_w, bias, decay)
+            pltpu.SemaphoreType.DMA((n,)),
+            pltpu.SemaphoreType.DMA((total // size, 7)),
+        ]
+        + kept,
+        compiler_params=comm_params(1),
+        cost_estimate=cost(4 * n * rows * width * channels),
+        name="project",
+    )(*inputs)
 
 
 def mixer_out_kernel(
@@ -1595,10 +1587,8 @@
     def blocked(x):
         return x.reshape(n, rows, x.shape[-1])
 
-    normed, recur, branch = project(n, tokens, gain_first, w_in, w_br)
-    recur, branch = flat(recur), flat(branch)
-    states, mixture, conv_low, recall, ingate, final_state, final_conv = recur_forward(
-        resets, recur, branch, init_state, before_conv, conv_params, gate_w, gate_bias, decay_rate
+    normed, recur, branch, states, mixture, conv_low, recall, ingate, final_state, final_conv = project(
+        n, tokens, gain_first, w_in, w_br, resets, init_state, before_conv, conv_params, gate_w, gate_bias, decay_rate
     )
     mixture = blocked(mixture)
     cot_full, residual, normed_mlp = mixer_out(n, mixture, w_output, cotangent, tokens, gain_second)

time: 647 us -> 639 us (0.988)
  Pallas kernels: 611 us -> 602 us
    pallas_call x1 -> x0, Pallas kernels: 19.4 us -> none  [recur_forward(): pl.pallas_call(recur_kernel, grid=(sequences, chunks), out_shape=(shape(t...]
    pallas_call x1, Pallas kernels: 106 us -> 114 us  [mixer_out(): pl.pallas_call(fetching(functools.partial(mixer_out_kernel, n), which), o...]
where the time goes in v7:
time: 639 us; the launch traced here: 638 us
  Pallas kernels  602 us (94%)
  local copies, waits for them, and re-layouts  14.3 us (2%)
  between operations  14.2 us (2%)
    pallas_call x1, Pallas kernels, mlp(): pl.pallas_call(fetching(functools.partial(mlp_kernel, n, copies), which),...  164 us
    pallas_call x1, Pallas kernels, mixer_out(): pl.pallas_call(fetching(functools.partial(mixer_out_kernel, n), which), o...  114 us
    pallas_call x1, Pallas kernels, down(): pl.pallas_call(fetching(functools.partial(down_kernel, n, copies), which)...  106 us
    pallas_call x1, Pallas kernels, input_back(): pl.pallas_call(fetching(functools.partial(input_back_kernel, n, copies),...  103 us
    pallas_call x1, Pallas kernels, project(): pl.pallas_call(fetching(functools.partial(project_kernel, n), (2, 3)), ou...  72.9 us
    pallas_call x1, Pallas kernels, recur_back(): pl.pallas_call(recur_back_kernel, grid=(sequences, chunks), out_shape=(sh...  30.4 us
  transfers between devices with their start and end apart: 2, of which 1 were waited for; matrix products, arithmetic and copies ran while one was open for 1% of the time, Pallas kernels for 37%

profile of v7, /device:TPU:8, one launch (start us, length us, event | category | flops | bytes accessed | tf_op | source)
XLA Modules:
  0.0 638.0 jit_solution(10204611828313108778)
XLA Ops:
  7.2 1.3 broadcast_in_dim.8.refs_1_.refs_7_
  8.5 1.3 broadcast_in_dim.9.refs_4_.refs_6_
  10.3 1.0 copy.33
  11.3 0.4 mul.20
  11.7 0.4 mul.21
  12.1 0.9 broadcast_multiply_fusion.refs_8_.gate_w
  13.0 72.9 %project.1 = (bf16[8,256,2048]{2,1,0:T(8,128)(2,1)}, f32[2048,344]{1,0:T(8,128)}, f32[2048,344]{1,0:T(8,128)}, f32[2048,344]{1,0:T(8,128)}, bf16[2048,344]{1,0:T...) custom-call(bf16[256,2048]{1,0:T(8,128)(2,1)} %refs_5_.3, ...), custom_call_target="tpu_custom_call" | custom-call | flops 5771362304 | bytes 200000000 | tf_op jit(solution)/shard_map/project/pallas_call | solution.py:642
  85.8 114.1 %mixer_out.1 = (bf16[8,256,2048]{2,1,0:T(8,128)(2,1)}, f32[256,2048]{1,0:T(8,128)}, bf16[256,2048]{1,0:T(8,128)(2,1)}) custom-call(bf16[8,256,344]{2,1,0:T(8,128)(2,1)} %bitcast.24, bf16[344,2048]{1,0:T(8,128)(2,1)} %refs_4_.5, bf16[256,2048]{1,0:T(8,128)(2,1)} %refs_2_.2, bf16[256,2048]{1,0:T(8,128)(2,1)} %refs_5_.3, ...), custom_call_target="tpu_custom_call" | custom-call | flops 2885681152 | bytes 200000000 | tf_op jit(solution)/shard_map/mixer_out/pallas_call | solution.py:725
  200.0 163.8 %mlp.1 = (bf16[8,256,768]{2,1,0:T(8,128)(2,1)}, bf16[2048,768]{1,0:T(8,128)(2,1)}, bf16[2048,768]{1,0:T(8,128)(2,1)}, bf16[768,2048]{1,0:T(8,128)(2,1)}, f32[256...) custom-call(bf16[256,2048]{1,0:T(8,128)(2,1)} %get-tuple-element.62.refs_0_, ...), custom_call_target="tpu_custom_call" | custom-call | flops 51539607552 | bytes 200000000 | tf_op jit(solution)/shard_map/mlp/pallas_call | solution.py:1024
  363.8 106.0 %down.1 = (bf16[256,2048]{1,0:T(8,128)(2,1)}, f32[8,256,344]{2,1,0:T(8,128)}, bf16[4,344,512]{2,1,0:T(8,128)(2,1)}) custom-call(bf16[8,256,768]{2,1,0:T(8,128)(2,1)} %get-tuple-element.65.refs_0_, bf16[768,2048]{1,0:T(8,128)(2,1)} %refs_1_.3, f32[256,2048]{1,0:T(8,128)} %get-tuple-element.64.refs_5_.refs_2_, bf16[256,2048]{1,0:T(8,128)(2,1)} %get-tuple-element.66.refs_3_, ...), custom_call_target="tpu_custom_call" | custom-call | flops 12213813248 | bytes 200000000 | tf_op jit(solution)/shard_map/down/pallas_call | solution.py:1116
  469.8 30.4 %recur_back.1 = (bf16[2048,344]{1,0:T(8,128)(2,1)}, bf16[2048,344]{1,0:T(8,128)(2,1)}, f32[8,344]{1,0:T(8,128)}, f32[2,344,344]{2,1,0:T(8,128)}, f32[768,2048]{1,0:T(8,128)}) custom-call(s32[2]{0:T(128)} %resets.1, f32[2048,344]{1,0:T(8,128)} %bitcast.11, f32[2048,344]{1,0:T(8,128)} %get-tuple-element.69.branch, ...), custom_call_target="tpu_custom_call" | custom-call | tf_op jit(solution)/shard_map/recur_back/pallas_call | solution.py:1282
  500.2 5.7 all-reduce.6.cloned.1.call-done
  505.9 102.5 %input_back.1 = (f32[256,2048]{1,0:T(8,128)}, bf16[344,2048]{1,0:T(8,128)(2,1)}, bf16[344,2048]{1,0:T(8,128)(2,1)}, f32[2,2,172,172]{3,2,1,0:T(8,128)}, f32[5,34...) custom-call(bf16[2048,344]{1,0:T(8,128)(2,1)} %get-tuple-element.76.refs_0_, ...), custom_call_target="tpu_custom_call" | custom-call | flops 11542724608 | bytes 200000000 | tf_op jit(solution)/shard_map/input_back/pallas_call | solution.py:1486
  608.5 2.5 copy.34
  611.0 1.3 reduce
  612.3 1.3 fusion
  613.6 11.9 %widen.1 = (f32[2048,768]{1,0:T(8,128)}, f32[2048,768]{1,0:T(8,128)}, f32[344,2048]{1,0:T(8,128)}, f32[344,2048]{1,0:T(8,128)}, f32[344,2048]{1,0:T(8,128)}) custom-call(bf16[2048,768]{1,0:T(8,128)(2,1)} %get-tuple-element.91.refs_0_, bf16[2048,768]{1,0:T(8,128)(2,1)} %get-tuple-element.92.refs_1_, bf16[344,2048]{1,0:T(8,128)(2,1)} %get-tuple-element.93.refs_2_, ...), custom_call_target="tpu_custom_call" | custom-call | tf_op jit(solution)/shard_map/widen/pallas_call | solution.py:1541
  625.6 1.0 copy.44
  626.6 0.9 copy-done
  627.5 1.3 copy.45
  628.8 0.6 copy.46
  629.4 0.6 copy.47
  630.0 0.6 copy.48
  630.6 0.6 copy.49
  (19 shorter events, 0.6 us)
Async XLA Ops:
  7.2 498.7 %all-reduce.6.cloned.1.call-start = ((), (), s32[]{:S(2)}) async-start(), calls=%async_computation.1 | async-start | bytes 12582912 | tf_op jit(solution)/shard_map/psum | solution.py:1598
  363.8 249.8 %all-reduce.4.cloned.1.call-start = ((), (), s32[]{:S(2)}) async-start(), calls=%async_computation | async-start | bytes 2818048 | tf_op jit(solution)/shard_map/psum | solution.py:1605
  613.6 11.9 %copy-start.1 = (bf16[256,2048]{1,0:T(8,128)(2,1)S(1)}, bf16[256,2048]{1,0:T(8,128)(2,1)}, u32[]{:S(2)}) copy-start(bf16[256,2048]{1,0:T(8,128)(2,1)} %get-tuple-element.142) | copy-start | bytes 3145732
  625.5 2.0 copy-start
  625.6 3.3 copy-start.4
  625.6 3.9 copy-start.3
  625.6 4.4 copy-start.2
  625.6 5.0 copy-start.5
Sparse Core Ops, SparseCore 0:
  363.9 141.9 all-reduce.5
  509.0 76.3 all-reduce.3

commit v8 on v7

--- a/solution.py
+++ b/solution.py
@@ -569,7 +569,7 @@
     def normalize(i):
         at = span(i, part)
         values = tokens[at].astype(F32)
-        full[g.t, at] = (values * inv_rms(values) * gain[...].astype(F32)).astype(BF16)
+        full[g.t, at] = (values * inv_rms(values) * gain[...].astype(F32)[None]).astype(BF16)
 
     loop(rows // part, normalize)
     g.greet()
@@ -709,7 +709,7 @@
         at = span(i, part)
         values = scatter.acc[at] + tokens[at].astype(F32)
         residual[at] = values
-        normed[at] = (values * inv_rms(values) * gain[...].astype(F32)).astype(BF16)
+        normed[at] = (values * inv_rms(values) * gain[...].astype(F32)[None]).astype(BF16)
 
     loop(residual.shape[0] // part, rows_of)
     gather.each(g.nz - 1, use)
@@ -918,10 +918,14 @@
                 pl.when(lower)(lambda: fall(i - 1))
                 pl.when(jnp.logical_not(lower))(lambda: rise(i - 1))
 
+        middle = jnp.logical_and(g.has_up, g.has_down)
+        for event in events:
+            pl.when(jnp.logical_not(middle))(event)
+
         def between(i):
             strips(i)
             for q, event in enumerate(events):
-                pl.when(i == (q + 1) * PARTS // len(events))(event)
+                pl.when(jnp.logical_and(middle, i == min(2 * q + 2, PARTS)))(event)
 
         loop(PARTS + 1, between)
 
@@ -985,7 +989,7 @@
 
     def rows_of(i):
         at = span(i, lines)
-        back, terms = norm_grad(residual[at], gain[...].astype(F32), acc[at])
+        back, terms = norm_grad(residual[at], gain[...].astype(F32)[None], acc[at])
         value = cot[0, at].astype(F32) + back
         acc[at] = value
         cot[1, at] = value.astype(BF16)
@@ -1316,14 +1320,14 @@
 
 def input_back_kernel(
     n, copies, arrive, g_recur, g_branch, w_in, w_br, normed, tokens, g_residual, gain, second_gain, g_gates, small,
-    input_grad, in_out, br_out, gates_out, conv_out, bias_out, decay_out, gains_out,
+    input_grad, in_out, br_out, gates_out, conv_out, bias_out, decay_out, first_out, second_out,
     gain_row, gain_parts, gain_in, gain_sum, gain_dp, gain_sent, gain_came, gain_dp_sent, gain_dp_came, *bufs
 ):
     g = Place(n)
     me = lax.axis_index("dp")
     rows, width = tokens.shape
     channels = w_in.shape[0]
-    blocks, block_width = gates_out.shape[1], gates_out.shape[2]
+    block_width, blocks = gates_out.shape[1], gates_out.shape[2]
     segment = width // (2 * copies)
     gain_width = width // n
     weights = Halving.over(me, copies, *bufs[:4])
@@ -1393,9 +1397,10 @@
                         (padded - channels, segment), BF16
                     )
         terms = jnp.sum(w_in[:, cols].astype(F32) * first + w_br[:, cols].astype(F32) * second, axis=0, keepdims=True)
-        gain_row[0:1, cols] = terms / gain[0:1, cols].astype(F32)
+        gain_row[0:1, cols] = terms
 
     loop(copies, weigh)
+    gain_row[0:1] = gain_row[0:1] / gain[...].astype(F32)[None]
     weights.start()
     gain_row[1:2] = second_gain[...]
     gain_row[2:8] = jnp.zeros((6, width), F32)
@@ -1438,7 +1443,7 @@
 
     def rows_of(i):
         at = span(i, part)
-        back, _ = norm_grad(tokens[at].astype(F32), gain[...].astype(F32), scatter.acc[at])
+        back, _ = norm_grad(tokens[at].astype(F32), gain[...].astype(F32)[None], scatter.acc[at])
         input_grad[at] = g_residual[at] + back
 
     loop(rows // part, rows_of)
@@ -1446,16 +1451,17 @@
     total = gain_dp[0]
     for i in range(1, copies):
         total = total + gain_dp[i]
-    gains_out[...] = total
+    first_out[...] = total[0]
+    second_out[...] = total[1]
     rest.finish()
     flat = jnp.concatenate([bufs[6][i // copies, i % copies, 0].astype(F32) for i in range(2 * copies)], axis=0)
     for q in (0, 1):
         for i in range(blocks):
             start = q * channels + i * block_width
-            gates_out[q, i] = flat[start : start + block_width, i * block_width : (i + 1) * block_width]
+            gates_out[q, :, i] = flat[start : start + block_width, i * block_width : (i + 1) * block_width]
     conv_out[...] = flat[2 * channels : 2 * channels + 5]
     bias_out[...] = flat[2 * channels + 5 : 2 * channels + 7]
-    decay_out[...] = flat[2 * channels + 7 : 2 * channels + 8]
+    decay_out[...] = flat[2 * channels + 7]
     weights.finish()
     for i in range(2 * copies):
         for q, out in enumerate((in_out, br_out)):
@@ -1488,14 +1494,15 @@
         out_shape=(shape(rows, width),)
         + (shape(channels, width, dtype=BF16),) * 2
         + (
-            shape(2, blocks, block, block),
+            shape(2, block, blocks, block),
             shape(5, channels),
             shape(2, channels),
-            shape(1, channels),
-            shape(*gain_shape),
+            shape(channels),
+            shape(width // n),
+            shape(width // n),
         ),
         in_specs=specs,
-        out_specs=(VM,) * 8,
+        out_specs=(VM,) * 9,
         scratch_shapes=[
             pltpu.VMEM((8, width), F32),
             pltpu.VMEM((n, *gain_shape), F32),
@@ -1517,18 +1524,35 @@
     )(*inputs)
 
 
-def widen_kernel(*refs):
+def widen_kernel(small, *refs):
     half = len(refs) // 2
-    for narrow, wide in zip(refs[:half], refs[half:]):
-        wide[...] = narrow[...].reshape(wide.shape).astype(F32)
-
-
-def widen(by_rows, by_columns, in_parts):
+    for q, (narrow, wide) in enumerate(zip(refs[:half], refs[half:])):
+
+        def pass_on(narrow=narrow, wide=wide):
+            wide[...] = narrow[...].reshape(wide.shape).astype(wide.dtype)
+
+        if q < small:
+            pl.when(pl.program_id(0) == 0)(pass_on)
+        else:
+            pass_on()
+
+
+def widen(small, as_is, by_rows, by_columns, in_parts):
     steps = 8
     width = by_columns[0].shape[1]
     tile = width // steps
     per_part = in_parts.shape[2] // tile
     specs, outs = [], []
+
+    def whole(x):
+        return pl.BlockSpec(x.shape, lambda i: (0,) * x.ndim)
+
+    for x in small:
+        specs.append(whole(x))
+        outs.append(shape(*x.shape))
+    for x in as_is:
+        specs.append(pl.BlockSpec((x.shape[0] // steps, x.shape[1]), lambda i: (i, 0)))
+        outs.append(shape(*x.shape, dtype=x.dtype))
     for x in by_rows:
         specs.append(pl.BlockSpec((x.shape[0] // steps, x.shape[1]), lambda i: (i, 0)))
         outs.append(shape(*x.shape))
@@ -1539,14 +1563,14 @@
     outs.append(shape(in_parts.shape[1], width))
     wide = pl.BlockSpec((in_parts.shape[1], tile), lambda i: (0, i))
     return pl.pallas_call(
-        widen_kernel,
+        functools.partial(widen_kernel, len(small)),
         grid=(steps,),
         out_shape=tuple(outs),
         in_specs=specs + [last],
         out_specs=tuple(specs) + (wide,),
         compiler_params=pltpu.CompilerParams(vmem_limit_bytes=VMEM_LIMIT),
         name="widen",
-    )(*by_rows, *by_columns, in_parts)
+    )(*small, *as_is, *by_rows, *by_columns, in_parts)
 
 
 def body(
@@ -1575,7 +1599,7 @@
     channels = w_input.shape[1]
     blocks, block = gate_weights.shape[1], gate_weights.shape[2]
     before_conv = init_conv.transpose(1, 0, 2)
-    gain_first, gain_second = norm_gain[None], mlp_gain[None]
+    gain_first, gain_second = norm_gain, mlp_gain
     gate_w = (gate_weights[:, :, :, None] * jnp.eye(blocks, dtype=BF16)[None, :, None, :, None]).reshape(
         2, channels, channels
     )
@@ -1603,27 +1627,34 @@
     )
     mlp_sums, grad_output, small = lax.optimization_barrier((mlp_sums, grad_output, small))
     grad_output = lax.psum(grad_output, "dp")
-    input_grad, grad_input, grad_branch, gates, g_conv, g_bias, g_decay, gains = input_back(
+    input_grad, grad_input, grad_branch, gates, g_conv, g_bias, g_decay, g_first_gain, g_second_gain = input_back(
         n, copies, g_recur, g_branch, w_in, w_br, flat(normed), tokens, g_residual, gain_first,
         gain_second_grad, g_gates, small, blocks,
     )
-    grad_gelu, grad_linear, grad_input, grad_branch, grad_output = widen(
-        mlp_sums, (grad_input, grad_branch), grad_output
+    (
+        final_state, final_conv, gates, g_conv, g_bias, g_decay, g_first_gain, g_second_gain, output, input_grad,
+        grad_gelu, grad_linear, grad_input, grad_branch, grad_output,
+    ) = widen(
+        (final_state, final_conv, gates, g_conv, g_bias, g_decay, g_first_gain, g_second_gain),
+        (output, input_grad),
+        mlp_sums,
+        (grad_input, grad_branch),
+        grad_output,
     )
     return (
         output,
         input_grad,
         final_state,
         final_conv.transpose(1, 0, 2),
-        gains[0],
+        g_first_gain,
         grad_input.T,
         grad_branch.T,
         g_conv,
-        gates,
+        gates.transpose(0, 2, 1, 3),
         g_bias,
-        g_decay[0],
+        g_decay,
         grad_output,
-        gains[1],
+        g_second_gain,
         grad_gelu,
         grad_linear,
         grad_down,

time: 639 us -> 625 us (0.978)
  local copies, waits for them, and re-layouts: 14.3 us -> 2.22 us
    unnamed x20 -> x1, local copies, waits for them, and re-layouts: 9.15 us -> 1.02 us
    pallas_call x1, Pallas kernels: 164 us -> 157 us  [mlp(): pl.pallas_call(fetching(functools.partial(mlp_kernel, n, copies), which),...]
  transfers between devices with their start and end apart: 2 -> 2, of which waited for: 1 -> 1; matrix products, arithmetic and copies ran while one was open for 1% -> 0% of each run, Pallas kernels for 37% -> 39%
where the time goes in v8:
time: 625 us
  Pallas kernels  603 us (96%)
  between operations  14.2 us (2%)
    pallas_call x1, Pallas kernels, mlp(): pl.pallas_call(fetching(functools.partial(mlp_kernel, n, copies), which),...  157 us
    pallas_call x1, Pallas kernels, mixer_out(): pl.pallas_call(fetching(functools.partial(mixer_out_kernel, n), which), o...  114 us
    pallas_call x1, Pallas kernels, down(): pl.pallas_call(fetching(functools.partial(down_kernel, n, copies), which)...  110 us
    pallas_call x1, Pallas kernels, input_back(): pl.pallas_call(fetching(functools.partial(input_back_kernel, n, copies),...  103 us
    pallas_call x1, Pallas kernels, project(): pl.pallas_call(fetching(functools.partial(project_kernel, n), (2, 3)), ou...  72.9 us
    pallas_call x1, Pallas kernels, recur_back(): pl.pallas_call(recur_back_kernel, grid=(sequences, chunks), out_shape=(sh...  30 us
    pallas_call x1, Pallas kernels, widen(): pl.pallas_call(functools.partial(widen_kernel, len(small)), grid=(steps,)...  15.1 us
  transfers between devices with their start and end apart: 2, of which 1 were waited for; matrix products, arithmetic and copies ran while one was open for 0% of the time, Pallas kernels for 39%

profile of v8, /device:TPU:8, one launch (start us, length us, event | category | flops | bytes accessed | tf_op | source)
XLA Modules:
  0.0 624.8 jit_solution(14036529621374653860)
XLA Ops:
  7.2 0.0 all-reduce.6.cloned.1.call-start
  7.2 0.3 mul.22
  7.5 0.2 mul.23
  7.7 1.0 copy.33
  8.7 0.4 mul.20
  9.1 0.4 mul.21
  9.5 0.9 broadcast_multiply_fusion.refs_8_.gate_w
  10.4 72.9 %project.1 = (bf16[8,256,2048]{2,1,0:T(8,128)(2,1)}, f32[2048,344]{1,0:T(8,128)}, f32[2048,344]{1,0:T(8,128)}, f32[2048,344]{1,0:T(8,128)}, bf16[2048,344]{1,0:T...) custom-call(bf16[256,2048]{1,0:T(8,128)(2,1)} %refs_5_.3, ...), custom_call_target="tpu_custom_call" | custom-call | flops 5771362304 | bytes 200000000 | tf_op jit(solution)/shard_map/project/pallas_call | solution.py:642
  83.3 114.2 %mixer_out.1 = (bf16[8,256,2048]{2,1,0:T(8,128)(2,1)}, f32[256,2048]{1,0:T(8,128)}, bf16[256,2048]{1,0:T(8,128)(2,1)}) custom-call(bf16[8,256,344]{2,1,0:T(8,128)(2,1)} %bitcast.22, bf16[344,2048]{1,0:T(8,128)(2,1)} %refs_4_.7, bf16[256,2048]{1,0:T(8,128)(2,1)} %refs_2_.2, bf16[256,2048]{1,0:T(8,128)(2,1)} %refs_5_.3, bf16[2048]{0:T(1024)(128)(2,1)} %refs_6_.1), custom_call_target="tpu_custom_call" | custom-call | flops 2885681152 | bytes 200000000 | tf_op jit(solution)/shard_map/mixer_out/pallas_call | solution.py:725
  197.5 157.0 %mlp.1 = (bf16[8,256,768]{2,1,0:T(8,128)(2,1)}, bf16[2048,768]{1,0:T(8,128)(2,1)}, bf16[2048,768]{1,0:T(8,128)(2,1)}, bf16[768,2048]{1,0:T(8,128)(2,1)}, f32[256...) custom-call(bf16[256,2048]{1,0:T(8,128)(2,1)} %get-tuple-element.75.refs_0_, ...), custom_call_target="tpu_custom_call" | custom-call | flops 51539607552 | bytes 200000000 | tf_op jit(solution)/shard_map/mlp/pallas_call | solution.py:1028
  354.5 0.0 all-reduce.6.cloned.1.call-update
  354.5 0.0 all-reduce.4.cloned.1.call-start
  354.6 110.5 %down.1 = (bf16[256,2048]{1,0:T(8,128)(2,1)}, f32[8,256,344]{2,1,0:T(8,128)}, bf16[4,344,512]{2,1,0:T(8,128)(2,1)}) custom-call(bf16[8,256,768]{2,1,0:T(8,128)(2,1)} %get-tuple-element.78.refs_0_, bf16[768,2048]{1,0:T(8,128)(2,1)} %refs_1_.5, f32[256,2048]{1,0:T(8,128)} %get-tuple-element.77.refs_5_.refs_2_, bf16[256,2048]{1,0:T(8,128)(2,1)} %get-tuple-element.79.refs_3_, ...), custom_call_target="tpu_custom_call" | custom-call | flops 12213813248 | bytes 200000000 | tf_op jit(solution)/shard_map/down/pallas_call | solution.py:1120
  465.0 30.0 %recur_back.1 = (bf16[2048,344]{1,0:T(8,128)(2,1)}, bf16[2048,344]{1,0:T(8,128)(2,1)}, f32[8,344]{1,0:T(8,128)}, f32[2,344,344]{2,1,0:T(8,128)}, f32[768,2048]{1,0:T(8,128)}) custom-call(s32[2]{0:T(128)} %resets.1, f32[2048,344]{1,0:T(8,128)} %bitcast.10, f32[2048,344]{1,0:T(8,128)} %get-tuple-element.81.branch, ...), custom_call_target="tpu_custom_call" | custom-call | tf_op jit(solution)/shard_map/recur_back/pallas_call | solution.py:1286
  495.1 4.8 all-reduce.6.cloned.1.call-done
  499.9 0.0 all-reduce.4.cloned.1.call-update
  499.9 102.9 %input_back.1 = (f32[256,2048]{1,0:T(8,128)}, bf16[344,2048]{1,0:T(8,128)(2,1)}, bf16[344,2048]{1,0:T(8,128)(2,1)}, f32[2,172,2,172]{3,2,1,0:T(2,128)}, f32[5,34...) custom-call(bf16[2048,344]{1,0:T(8,128)(2,1)} %get-tuple-element.88.refs_0_, ...), custom_call_target="tpu_custom_call" | custom-call | flops 11542724608 | bytes 200000000 | tf_op jit(solution)/shard_map/input_back/pallas_call | solution.py:1492
  602.8 0.0 all-reduce.4.cloned.1.call-done.refs_14_
  602.8 15.1 %widen.1 = (f32[2,344]{1,0:T(2,128)}, f32[3,2,344]{2,1,0:T(2,128)}, f32[2,172,2,172]{3,2,1,0:T(2,128)}, f32[5,344]{1,0:T(8,128)}, f32[2,344]{1,0:T(2,128)}, /*in...) custom-call(f32[2,344]{1,0:T(2,128)} %get-tuple-element.72.refs_0_, ...), custom_call_target="tpu_custom_call" | custom-call | tf_op jit(solution)/shard_map/widen/pallas_call | solution.py:1565
  (1 shorter events, 0.0 us)
Async XLA Ops:
  7.2 492.7 %all-reduce.6.cloned.1.call-start = ((), (), s32[]{:S(2)}) async-start(), calls=%async_computation.1 | async-start | bytes 12582912 | tf_op jit(solution)/shard_map/psum | solution.py:1622
  354.5 248.3 %all-reduce.4.cloned.1.call-start = ((), (), s32[]{:S(2)}) async-start(), calls=%async_computation | async-start | bytes 2818048 | tf_op jit(solution)/shard_map/psum | solution.py:1629
Sparse Core Ops, SparseCore 0:
  354.7 145.1 all-reduce.5
  503.0 76.3 all-reduce.3

commit v9 on v8

--- a/solution.py
+++ b/solution.py
@@ -752,7 +752,7 @@
     columns = w_gelu.shape[1]
     rows, width = acc.shape
     tile = tile_of(columns, 256)
-    wide = tile_of(width, 512)
+    wide = tile_of(width, 1024)
     strip = rows // PARTS
     me = lax.axis_index("dp")
     start = pltpu.make_async_copy(normed, full.at[g.t], saved.at[0])

time: 625 us -> 622 us (level)
  no operation moved by 1% of the time
where the time goes in v9:
time: 622 us; the launch traced here: 621 us
  Pallas kernels  599 us (96%)
  between operations  14.2 us (2%)
    pallas_call x1, Pallas kernels, mlp(): pl.pallas_call(fetching(functools.partial(mlp_kernel, n, copies), which),...  153 us
    pallas_call x1, Pallas kernels, mixer_out(): pl.pallas_call(fetching(functools.partial(mixer_out_kernel, n), which), o...  114 us
    pallas_call x1, Pallas kernels, down(): pl.pallas_call(fetching(functools.partial(down_kernel, n, copies), which)...  111 us
    pallas_call x1, Pallas kernels, input_back(): pl.pallas_call(fetching(functools.partial(input_back_kernel, n, copies),...  103 us
    pallas_call x1, Pallas kernels, project(): pl.pallas_call(fetching(functools.partial(project_kernel, n), (2, 3)), ou...  72.9 us
    pallas_call x1, Pallas kernels, recur_back(): pl.pallas_call(recur_back_kernel, grid=(sequences, chunks), out_shape=(sh...  30 us
    pallas_call x1, Pallas kernels, widen(): pl.pallas_call(functools.partial(widen_kernel, len(small)), grid=(steps,)...  15.1 us
  transfers between devices with their start and end apart: 2, of which 1 were waited for; matrix products, arithmetic and copies ran while one was open for 0% of the time, Pallas kernels for 39%

profile of v9, /device:TPU:8, one launch (start us, length us, event | category | flops | bytes accessed | tf_op | source)
XLA Modules:
  0.0 621.0 jit_solution(16672159206952923536)
XLA Ops:
  7.2 0.0 all-reduce.6.cloned.1.call-start
  7.2 0.3 mul.22
  7.5 0.2 mul.23
  7.7 1.0 copy.33
  8.7 0.4 mul.20
  9.1 0.4 mul.21
  9.5 0.9 broadcast_multiply_fusion.refs_8_.gate_w
  10.4 72.9 %project.1 = (bf16[8,256,2048]{2,1,0:T(8,128)(2,1)}, f32[2048,344]{1,0:T(8,128)}, f32[2048,344]{1,0:T(8,128)}, f32[2048,344]{1,0:T(8,128)}, bf16[2048,344]{1,0:T...) custom-call(bf16[256,2048]{1,0:T(8,128)(2,1)} %refs_5_.3, ...), custom_call_target="tpu_custom_call" | custom-call | flops 5771362304 | bytes 200000000 | tf_op jit(solution)/shard_map/project/pallas_call | solution.py:642
  83.3 114.2 %mixer_out.1 = (bf16[8,256,2048]{2,1,0:T(8,128)(2,1)}, f32[256,2048]{1,0:T(8,128)}, bf16[256,2048]{1,0:T(8,128)(2,1)}) custom-call(bf16[8,256,344]{2,1,0:T(8,128)(2,1)} %bitcast.22, bf16[344,2048]{1,0:T(8,128)(2,1)} %refs_4_.7, bf16[256,2048]{1,0:T(8,128)(2,1)} %refs_2_.2, bf16[256,2048]{1,0:T(8,128)(2,1)} %refs_5_.3, bf16[2048]{0:T(1024)(128)(2,1)} %refs_6_.1), custom_call_target="tpu_custom_call" | custom-call | flops 2885681152 | bytes 200000000 | tf_op jit(solution)/shard_map/mixer_out/pallas_call | solution.py:725
  197.5 153.2 %mlp.1 = (bf16[8,256,768]{2,1,0:T(8,128)(2,1)}, bf16[2048,768]{1,0:T(8,128)(2,1)}, bf16[2048,768]{1,0:T(8,128)(2,1)}, bf16[768,2048]{1,0:T(8,128)(2,1)}, f32[256...) custom-call(bf16[256,2048]{1,0:T(8,128)(2,1)} %get-tuple-element.75.refs_0_, ...), custom_call_target="tpu_custom_call" | custom-call | flops 51539607552 | bytes 200000000 | tf_op jit(solution)/shard_map/mlp/pallas_call | solution.py:1028
  350.7 0.0 all-reduce.6.cloned.1.call-update
  350.7 0.0 all-reduce.4.cloned.1.call-start
  350.8 110.5 %down.1 = (bf16[256,2048]{1,0:T(8,128)(2,1)}, f32[8,256,344]{2,1,0:T(8,128)}, bf16[4,344,512]{2,1,0:T(8,128)(2,1)}) custom-call(bf16[8,256,768]{2,1,0:T(8,128)(2,1)} %get-tuple-element.78.refs_0_, bf16[768,2048]{1,0:T(8,128)(2,1)} %refs_1_.5, f32[256,2048]{1,0:T(8,128)} %get-tuple-element.77.refs_5_.refs_2_, bf16[256,2048]{1,0:T(8,128)(2,1)} %get-tuple-element.79.refs_3_, ...), custom_call_target="tpu_custom_call" | custom-call | flops 12213813248 | bytes 200000000 | tf_op jit(solution)/shard_map/down/pallas_call | solution.py:1120
  461.3 30.0 %recur_back.1 = (bf16[2048,344]{1,0:T(8,128)(2,1)}, bf16[2048,344]{1,0:T(8,128)(2,1)}, f32[8,344]{1,0:T(8,128)}, f32[2,344,344]{2,1,0:T(8,128)}, f32[768,2048]{1,0:T(8,128)}) custom-call(s32[2]{0:T(128)} %resets.1, f32[2048,344]{1,0:T(8,128)} %bitcast.10, f32[2048,344]{1,0:T(8,128)} %get-tuple-element.81.branch, ...), custom_call_target="tpu_custom_call" | custom-call | tf_op jit(solution)/shard_map/recur_back/pallas_call | solution.py:1286
  491.3 4.7 all-reduce.6.cloned.1.call-done
  496.1 0.0 all-reduce.4.cloned.1.call-update
  496.1 102.9 %input_back.1 = (f32[256,2048]{1,0:T(8,128)}, bf16[344,2048]{1,0:T(8,128)(2,1)}, bf16[344,2048]{1,0:T(8,128)(2,1)}, f32[2,172,2,172]{3,2,1,0:T(2,128)}, f32[5,34...) custom-call(bf16[2048,344]{1,0:T(8,128)(2,1)} %get-tuple-element.88.refs_0_, ...), custom_call_target="tpu_custom_call" | custom-call | flops 11542724608 | bytes 200000000 | tf_op jit(solution)/shard_map/input_back/pallas_call | solution.py:1492
  599.0 0.0 all-reduce.4.cloned.1.call-done.refs_14_
  599.0 15.1 %widen.1 = (f32[2,344]{1,0:T(2,128)}, f32[3,2,344]{2,1,0:T(2,128)}, f32[2,172,2,172]{3,2,1,0:T(2,128)}, f32[5,344]{1,0:T(8,128)}, f32[2,344]{1,0:T(2,128)}, /*in...) custom-call(f32[2,344]{1,0:T(2,128)} %get-tuple-element.72.refs_0_, ...), custom_call_target="tpu_custom_call" | custom-call | tf_op jit(solution)/shard_map/widen/pallas_call | solution.py:1565
  (1 shorter events, 0.0 us)
Async XLA Ops:
  7.2 488.9 %all-reduce.6.cloned.1.call-start = ((), (), s32[]{:S(2)}) async-start(), calls=%async_computation.1 | async-start | bytes 12582912 | tf_op jit(solution)/shard_map/psum | solution.py:1622
  350.7 248.3 %all-reduce.4.cloned.1.call-start = ((), (), s32[]{:S(2)}) async-start(), calls=%async_computation | async-start | bytes 2818048 | tf_op jit(solution)/shard_map/psum | solution.py:1629
Sparse Core Ops, SparseCore 0:
  350.8 145.1 all-reduce.5
  499.2 76.3 all-reduce.3

commit v10 on v9

--- a/solution.py
+++ b/solution.py
@@ -824,10 +824,10 @@
         layer(other, its)
 
         def offer(i):
-            cols = span(i, wide)
+            cols = span(i, width)
             to_sib[:, cols] = partial(its, cols).astype(BF16)
 
-        loop(width // wide, offer)
+        loop(1, offer)
         sib_copy(k).start()
         layer(own, mine)
         sib_copy(k).wait()
@@ -835,18 +835,18 @@
         @pl.when(d == 0)
         def _():
             def part(i):
-                cols = span(i, wide)
+                cols = span(i, width)
                 acc[:, cols] = partial(mine, cols) + sums[k, :, cols].astype(F32)
 
-            loop(width // wide, part)
+            loop(1, part)
 
         @pl.when(d > 0)
         def _():
             def part(i):
-                cols = span(i, wide)
+                cols = span(i, width)
                 sums[k, :, cols] = (partial(mine, cols) + sums[k, :, cols].astype(F32)).astype(BF16)
 
-            loop(width // wide, part)
+            loop(1, part)
             first = jnp.logical_or(
                 jnp.logical_and(way > 0, jnp.logical_not(g.has_down)),
                 jnp.logical_and(way < 0, jnp.logical_not(g.has_up)),

time: 622 us -> 620 us (level)
  no operation moved by 1% of the time
where the time goes in v10:
time: 620 us
  Pallas kernels  598 us (96%)
  between operations  14.2 us (2%)
    pallas_call x1, Pallas kernels, mlp(): pl.pallas_call(fetching(functools.partial(mlp_kernel, n, copies), which),...  152 us
    pallas_call x1, Pallas kernels, mixer_out(): pl.pallas_call(fetching(functools.partial(mixer_out_kernel, n), which), o...  114 us
    pallas_call x1, Pallas kernels, down(): pl.pallas_call(fetching(functools.partial(down_kernel, n, copies), which)...  111 us
    pallas_call x1, Pallas kernels, input_back(): pl.pallas_call(fetching(functools.partial(input_back_kernel, n, copies),...  103 us
    pallas_call x1, Pallas kernels, project(): pl.pallas_call(fetching(functools.partial(project_kernel, n), (2, 3)), ou...  72.9 us
    pallas_call x1, Pallas kernels, recur_back(): pl.pallas_call(recur_back_kernel, grid=(sequences, chunks), out_shape=(sh...  30 us
    pallas_call x1, Pallas kernels, widen(): pl.pallas_call(functools.partial(widen_kernel, len(small)), grid=(steps,)...  15.1 us
  transfers between devices with their start and end apart: 2, of which 1 were waited for; matrix products, arithmetic and copies ran while one was open for 0% of the time, Pallas kernels for 39%

profile of v10, /device:TPU:8, one launch (start us, length us, event | category | flops | bytes accessed | tf_op | source)
XLA Modules:
  0.0 619.9 jit_solution(18054443424478754461)
XLA Ops:
  7.2 0.0 all-reduce.6.cloned.1.call-start
  7.2 0.3 mul.22
  7.5 0.2 mul.23
  7.7 1.0 copy.33
  8.7 0.4 mul.20
  9.1 0.4 mul.21
  9.5 0.9 broadcast_multiply_fusion.refs_8_.gate_w
  10.4 72.9 %project.1 = (bf16[8,256,2048]{2,1,0:T(8,128)(2,1)}, f32[2048,344]{1,0:T(8,128)}, f32[2048,344]{1,0:T(8,128)}, f32[2048,344]{1,0:T(8,128)}, bf16[2048,344]{1,0:T...) custom-call(bf16[256,2048]{1,0:T(8,128)(2,1)} %refs_5_.3, ...), custom_call_target="tpu_custom_call" | custom-call | flops 5771362304 | bytes 200000000 | tf_op jit(solution)/shard_map/project/pallas_call | solution.py:642
  83.3 114.2 %mixer_out.1 = (bf16[8,256,2048]{2,1,0:T(8,128)(2,1)}, f32[256,2048]{1,0:T(8,128)}, bf16[256,2048]{1,0:T(8,128)(2,1)}) custom-call(bf16[8,256,344]{2,1,0:T(8,128)(2,1)} %bitcast.22, bf16[344,2048]{1,0:T(8,128)(2,1)} %refs_4_.7, bf16[256,2048]{1,0:T(8,128)(2,1)} %refs_2_.2, bf16[256,2048]{1,0:T(8,128)(2,1)} %refs_5_.3, bf16[2048]{0:T(1024)(128)(2,1)} %refs_6_.1), custom_call_target="tpu_custom_call" | custom-call | flops 2885681152 | bytes 200000000 | tf_op jit(solution)/shard_map/mixer_out/pallas_call | solution.py:725
  197.5 152.0 %mlp.1 = (bf16[8,256,768]{2,1,0:T(8,128)(2,1)}, bf16[2048,768]{1,0:T(8,128)(2,1)}, bf16[2048,768]{1,0:T(8,128)(2,1)}, bf16[768,2048]{1,0:T(8,128)(2,1)}, f32[256...) custom-call(bf16[256,2048]{1,0:T(8,128)(2,1)} %get-tuple-element.75.refs_0_, ...), custom_call_target="tpu_custom_call" | custom-call | flops 51539607552 | bytes 200000000 | tf_op jit(solution)/shard_map/mlp/pallas_call | solution.py:1028
  349.4 0.0 all-reduce.6.cloned.1.call-update
  349.5 0.0 all-reduce.4.cloned.1.call-start
  349.5 110.9 %down.1 = (bf16[256,2048]{1,0:T(8,128)(2,1)}, f32[8,256,344]{2,1,0:T(8,128)}, bf16[4,344,512]{2,1,0:T(8,128)(2,1)}) custom-call(bf16[8,256,768]{2,1,0:T(8,128)(2,1)} %get-tuple-element.78.refs_0_, bf16[768,2048]{1,0:T(8,128)(2,1)} %refs_1_.5, f32[256,2048]{1,0:T(8,128)} %get-tuple-element.77.refs_5_.refs_2_, bf16[256,2048]{1,0:T(8,128)(2,1)} %get-tuple-element.79.refs_3_, ...), custom_call_target="tpu_custom_call" | custom-call | flops 12213813248 | bytes 200000000 | tf_op jit(solution)/shard_map/down/pallas_call | solution.py:1120
  460.4 30.0 %recur_back.1 = (bf16[2048,344]{1,0:T(8,128)(2,1)}, bf16[2048,344]{1,0:T(8,128)(2,1)}, f32[8,344]{1,0:T(8,128)}, f32[2,344,344]{2,1,0:T(8,128)}, f32[768,2048]{1,0:T(8,128)}) custom-call(s32[2]{0:T(128)} %resets.1, f32[2048,344]{1,0:T(8,128)} %bitcast.10, f32[2048,344]{1,0:T(8,128)} %get-tuple-element.81.branch, ...), custom_call_target="tpu_custom_call" | custom-call | tf_op jit(solution)/shard_map/recur_back/pallas_call | solution.py:1286
  490.4 4.6 all-reduce.6.cloned.1.call-done
  494.9 0.0 all-reduce.4.cloned.1.call-update
  495.0 102.9 %input_back.1 = (f32[256,2048]{1,0:T(8,128)}, bf16[344,2048]{1,0:T(8,128)(2,1)}, bf16[344,2048]{1,0:T(8,128)(2,1)}, f32[2,172,2,172]{3,2,1,0:T(2,128)}, f32[5,34...) custom-call(bf16[2048,344]{1,0:T(8,128)(2,1)} %get-tuple-element.88.refs_0_, ...), custom_call_target="tpu_custom_call" | custom-call | flops 11542724608 | bytes 200000000 | tf_op jit(solution)/shard_map/input_back/pallas_call | solution.py:1492
  597.9 0.0 all-reduce.4.cloned.1.call-done.refs_14_
  597.9 15.1 %widen.1 = (f32[2,344]{1,0:T(2,128)}, f32[3,2,344]{2,1,0:T(2,128)}, f32[2,172,2,172]{3,2,1,0:T(2,128)}, f32[5,344]{1,0:T(8,128)}, f32[2,344]{1,0:T(2,128)}, /*in...) custom-call(f32[2,344]{1,0:T(2,128)} %get-tuple-element.72.refs_0_, ...), custom_call_target="tpu_custom_call" | custom-call | tf_op jit(solution)/shard_map/widen/pallas_call | solution.py:1565
  (1 shorter events, 0.0 us)
Async XLA Ops:
  7.2 487.8 %all-reduce.6.cloned.1.call-start = ((), (), s32[]{:S(2)}) async-start(), calls=%async_computation.1 | async-start | bytes 12582912 | tf_op jit(solution)/shard_map/psum | solution.py:1622
  349.5 248.4 %all-reduce.4.cloned.1.call-start = ((), (), s32[]{:S(2)}) async-start(), calls=%async_computation | async-start | bytes 2818048 | tf_op jit(solution)/shard_map/psum | solution.py:1629
Sparse Core Ops, SparseCore 0:
  349.6 145.3 all-reduce.5
  498.1 76.3 all-reduce.3
